TPU v7x, 256 devices: a whole 4x4x8 slice. The times are simulated.
256 devices in a mesh: group: 4 (over x_hi, core), zslab: 64 (over z, x_lo, y).
Axes of the slice: x: 4 (x_hi: 2, x_lo: 2; x = x_hi * 2 + x_lo), y: 4, z: 8, core: 2. Of those that a mesh axis runs over, the one named last changes fastest.
Arguments:
- background: float32 [128, 32, 128], P('zslab'), may hold values from 2.1 to 12.1
- absorb: float32 [128, 32, 128], P('zslab'), may hold values from 0.3 to 1
- density: float32 [128, 32, 128], P('zslab'), may hold values from 0 to 1
- profiles: float32 [6, 2, 128, 32, 128], P(None, None, 'zslab'), may hold values from -6 to 6
- adjoint_source: float32 [16, 2, 128, 32, 128], P('group', None, 'zslab'), may hold values from -6 to 6
- port_modes: int32 [16], P('group'), may hold values from 0 to 5
- design_start: int32 [1], replicated, may hold values from 0 to 64
Outputs:
- forward_field: float32 [16, 2, 128, 32, 128], P('group', None, 'zslab')
- adjoint_field: float32 [16, 2, 128, 32, 128], P('group', None, 'zslab')
- new_density: float32 [128, 32, 128], P('zslab', 'group')
Inputs may be any that keep to these rules, and one draw needn't show every extreme that they name: The design region is planes design_start to design_start + 63. Port p's forward source is the profile of mode port_modes[p].
All inputs are finite; a program needn't handle non-finite values.
Results may differ from a plain program's by a relative error of at most 0.0003.
Values sent between devices are 32-bit elements; how exact they have to be, the bound alone decides.
No kernel may reach another device: no remote copies, remote signals or barrier semaphores. Data moves between devices by JAX's collectives and lax.ppermute only.
A program may use at most 64 MiB of HBM per device.

v0:
```python
import jax
import jax.numpy as jnp
from jax import lax
from jax.sharding import PartitionSpec as P

ITERS = 4


wave_sq = 0.1
step_size = 2.0
perm_span = 10.0
low_perm = 2.1
sharpness = 8.0
threshold = 0.5


def with_halo(block, sides, width):
    for axis, dim in sides:
        count = lax.axis_size(axis)
        forward = [(i, i + 1) for i in range(count - 1)]
        backward = [(target, source) for source, target in forward]
        low = lax.ppermute(
            lax.slice_in_dim(block, block.shape[dim] - width, None, axis=dim), axis, forward
        )
        high = lax.ppermute(lax.slice_in_dim(block, 0, width, axis=dim), axis, backward)
        block = jnp.concatenate([low, block, high], axis=dim)
    return block


def scaled(coef, field):
    coef_re = coef[0].reshape((-1, 1, 1, 1))
    coef_im = coef[1].reshape((-1, 1, 1, 1))
    real_part = coef_re * field[:, 0] - coef_im * field[:, 1]
    imag_part = coef_re * field[:, 1] + coef_im * field[:, 0]
    return jnp.stack([real_part, imag_part], axis=1)


def product_pair(left, right):
    real_part = jnp.sum(left[:, 0] * right[:, 0] + left[:, 1] * right[:, 1], axis=(1, 2, 3))
    imag_part = jnp.sum(left[:, 0] * right[:, 1] - left[:, 1] * right[:, 0], axis=(1, 2, 3))
    return (real_part, imag_part)


def divide_pair(top, bottom):
    denominator = bottom[0] * bottom[0] + bottom[1] * bottom[1]
    return (
        (top[0] * bottom[0] + top[1] * bottom[1]) / denominator,
        (top[1] * bottom[0] - top[0] * bottom[1]) / denominator,
    )


def multiply_pair(left, right):
    return (left[0] * right[0] - left[1] * right[1], left[0] * right[1] + left[1] * right[0])


def with_planes(field):
    return with_halo(field, (("zslab", 2),), 1)


def operate(field, diag_re, diag_im):
    padded = jnp.pad(with_planes(field), ((0, 0), (0, 0), (0, 0), (1, 1), (1, 1)))
    beside = padded[:, :, 2:, 1:-1, 1:-1] + padded[:, :, :-2, 1:-1, 1:-1]
    beside = beside + padded[:, :, 1:-1, 2:, 1:-1] + padded[:, :, 1:-1, :-2, 1:-1]
    beside = beside + padded[:, :, 1:-1, 1:-1, 2:] + padded[:, :, 1:-1, 1:-1, :-2]
    real_part = diag_re * field[:, 0] - diag_im * field[:, 1]
    imag_part = diag_re * field[:, 1] + diag_im * field[:, 0]
    return jnp.stack([real_part, imag_part], axis=1) - beside


def bicgstab(sources, diag_re, diag_im):
    solution = jnp.zeros_like(sources)
    residual = sources
    direction = sources
    bilinear = lax.psum(product_pair(sources, residual), "zslab")
    for iteration in range(ITERS):
        image = operate(direction, diag_re, diag_im)
        along = lax.psum(product_pair(sources, image), "zslab")
        advance = divide_pair(bilinear, along)
        halfway = residual - scaled(advance, image)
        second = operate(halfway, diag_re, diag_im)
        cross_re, cross_im = product_pair(second, halfway)
        energy = jnp.sum(second[:, 0] * second[:, 0] + second[:, 1] * second[:, 1], axis=(1, 2, 3))
        cross_re, cross_im, energy = lax.psum((cross_re, cross_im, energy), "zslab")
        relax_coef = (cross_re / energy, cross_im / energy)
        solution = solution + scaled(advance, direction) + scaled(relax_coef, halfway)
        residual = halfway - scaled(relax_coef, second)
        if iteration + 1 < ITERS:
            bilinear_new = lax.psum(product_pair(sources, residual), "zslab")
        if iteration + 1 < ITERS:
            blend_coef = multiply_pair(
                divide_pair(bilinear_new, bilinear), divide_pair(advance, relax_coef)
            )
            direction = residual + scaled(blend_coef, direction - scaled(relax_coef, image))
            bilinear = bilinear_new
    return solution


def on_device(background, absorb, density, profiles, adjoint_source, port_modes, design_start):
    planes_dev = density.shape[0]
    rows_all = density.shape[1]
    first_plane = lax.axis_index("zslab") * planes_dev
    design_depth = planes_dev * lax.axis_size("zslab") // 2
    planes = first_plane + jnp.arange(planes_dev)
    in_design = (planes >= design_start[0]) & (planes < design_start[0] + design_depth)
    in_design = in_design[:, None, None]
    permittivity = jnp.where(in_design, low_perm + perm_span * density, background)
    diag_re = 6.0 - wave_sq * permittivity
    selector = (port_modes[:, None] == jnp.arange(profiles.shape[0])[None, :]).astype(jnp.float32)
    forward_source = jnp.einsum(
        "pm,mczyx->pczyx", selector, profiles, precision=lax.Precision.HIGHEST
    )
    port_count = forward_source.shape[0]
    sources = jnp.concatenate([forward_source, adjoint_source], axis=0)
    fields = bicgstab(sources, diag_re, absorb)
    forward_field = fields[:port_count]
    adjoint_field = fields[port_count:]
    terms = forward_field[:, 0] * adjoint_field[:, 0] - forward_field[:, 1] * adjoint_field[:, 1]
    local_term = -wave_sq * jnp.sum(terms, axis=0)
    rows_share = rows_all // lax.axis_size("group")
    row_start = lax.axis_index("group") * rows_share
    total = lax.psum(local_term, "group")
    gradient = lax.dynamic_slice_in_dim(total, row_start, rows_share, 1)
    density_rows = lax.dynamic_slice_in_dim(density, row_start, rows_share, 1)
    updated = jnp.where(
        in_design, jnp.clip(density_rows - step_size * perm_span * gradient, 0.0, 1.0), density_rows
    )
    extended = with_halo(updated, (("zslab", 0),), 1)
    padded = jnp.pad(extended, ((0, 0), (0, 0), (1, 1)))
    filtered = (
        2.0 * updated
        + padded[2:, :, 1:-1]
        + padded[:-2, :, 1:-1]
        + padded[1:-1, :, 2:]
        + padded[1:-1, :, :-2]
    ) / 6.0
    new_density = (
        jnp.tanh(sharpness * threshold) + jnp.tanh(sharpness * (filtered - threshold))
    ) / (jnp.tanh(sharpness * threshold) + jnp.tanh(sharpness * (1.0 - threshold)))
    return (forward_field, adjoint_field, new_density)


def solution(mesh):
    return jax.shard_map(
        on_device,
        mesh=mesh,
        in_specs=(
            P("zslab", None, None),
            P("zslab", None, None),
            P("zslab", None, None),
            P(None, None, "zslab", None, None),
            P("group", None, "zslab", None, None),
            P("group"),
            P(),
        ),
        out_specs=(
            P("group", None, "zslab", None, None),
            P("group", None, "zslab", None, None),
            P("zslab", "group", None),
        ),
        check_vma=False,
    )
```

profile of v0, /device:TPU:126, one launch (start us, length us, event | category | flops | bytes accessed | tf_op | source)
XLA Modules:
  0.0 1917.4 jit_solution(3247269837822364543)
XLA Ops:
  23.8 152.1 %all-reduce.19 = (f32[8]{0:T(128)S(1)}, f32[8]{0:T(128)S(1)}, f32[8]{0:T(128)S(1)}, f32[8]{0:T(128)S(1)}) all-reduce(f32[8]{0:T(128)S(1)} %get-tuple-element.33, f32[8]{0:T(128)S(1)} %get-tuple-element.27, f32[8]{0:T(128)S(1)} %get-tuple-element.32, f32[8]{0:T(128)S(1)} %get-tuple-element.26), channel_id=1, replica_groups=mesh['group'=4,'zslab'=64] {'zslab'}, use_global_device_ids=true, to_apply=%region_1.2 | all-reduce | flops 32 | bytes 256 | tf_op jit(solution)/shard_map/psum | solution.py:74
  176.2 8.4 collective-permute-start.3
  188.5 8.6 collective-permute-done.2
  198.4 152.1 %all-reduce.18 = (f32[8]{0:T(128)S(1)}, f32[8]{0:T(128)S(1)}, f32[8]{0:T(128)S(1)}) all-reduce(f32[8]{0:T(128)S(1)} %get-tuple-element.25, f32[8]{0:T(128)S(1)} %get-tuple-element.31, f32[8]{0:T(128)S(1)} %get-tuple-element.24), channel_id=1, replica_groups=mesh['group'=4,'zslab'=64] {'zslab'}, use_global_device_ids=true, to_apply=%region_13.14 | all-reduce | flops 24 | bytes 192 | tf_op jit(solution)/shard_map/psum | solution.py:83
  352.0 154.6 %all-reduce.17 = (f32[8]{0:T(128)S(1)}, f32[8]{0:T(128)S(1)}) all-reduce(f32[8]{0:T(128)S(1)} %get-tuple-element.23, f32[8]{0:T(128)S(1)} %get-tuple-element.22), channel_id=1, replica_groups=mesh['group'=4,'zslab'=64] {'zslab'}, use_global_device_ids=true, to_apply=%region_15.16 | all-reduce | flops 16 | bytes 128 | tf_op jit(solution)/shard_map/psum | solution.py:88
  516.9 8.7 collective-permute-done.4
  527.0 152.1 %all-reduce.16 = (f32[8]{0:T(128)S(1)}, f32[8]{0:T(128)S(1)}) all-reduce(f32[8]{0:T(128)S(1)} %get-tuple-element.21, f32[8]{0:T(128)S(1)} %get-tuple-element.20), channel_id=1, replica_groups=mesh['group'=4,'zslab'=64] {'zslab'}, use_global_device_ids=true, to_apply=%region_21.22 | all-reduce | flops 16 | bytes 128 | tf_op jit(solution)/shard_map/psum | solution.py:77
  680.2 8.4 collective-permute-start.7
  692.5 8.6 collective-permute-done.6
  703.1 152.7 %all-reduce.15 = (f32[8]{0:T(128)}, f32[8]{0:T(128)}, f32[8]{0:T(128)}) all-reduce(f32[8]{0:T(128)} %get-tuple-element.19, f32[8]{0:T(128)} %get-tuple-element.30, f32[8]{0:T(128)S(1)} %get-tuple-element.18), channel_id=1, replica_groups=mesh['group'=4,'zslab'=64] {'zslab'}, use_global_device_ids=true, to_apply=%region_27.28 | all-reduce | flops 24 | bytes 192 | tf_op jit(solution)/shard_map/psum | solution.py:83
  859.7 154.8 %all-reduce.14 = (f32[8]{0:T(128)S(1)}, f32[8]{0:T(128)S(1)}) all-reduce(f32[8]{0:T(128)S(1)} %get-tuple-element.17, f32[8]{0:T(128)S(1)} %get-tuple-element.16), channel_id=1, replica_groups=mesh['group'=4,'zslab'=64] {'zslab'}, use_global_device_ids=true, to_apply=%region_29.30 | all-reduce | flops 16 | bytes 128 | tf_op jit(solution)/shard_map/psum | solution.py:88
  1025.4 8.6 collective-permute-done.8
  1035.9 153.0 %all-reduce.13 = (f32[8]{0:T(128)}, f32[8]{0:T(128)}) all-reduce(f32[8]{0:T(128)} %get-tuple-element.15, f32[8]{0:T(128)} %get-tuple-element.14), channel_id=1, replica_groups=mesh['group'=4,'zslab'=64] {'zslab'}, use_global_device_ids=true, to_apply=%region_35.36 | all-reduce | flops 16 | bytes 128 | tf_op jit(solution)/shard_map/psum | solution.py:77
  1190.7 8.4 collective-permute-start.11
  1203.0 8.7 collective-permute-done.10
  1214.4 152.8 %all-reduce.12 = (f32[8]{0:T(128)}, f32[8]{0:T(128)}, f32[8]{0:T(128)}) all-reduce(f32[8]{0:T(128)} %get-tuple-element.13, f32[8]{0:T(128)} %get-tuple-element.29, f32[8]{0:T(128)S(1)} %get-tuple-element.12), channel_id=1, replica_groups=mesh['group'=4,'zslab'=64] {'zslab'}, use_global_device_ids=true, to_apply=%region_41.42 | all-reduce | flops 24 | bytes 192 | tf_op jit(solution)/shard_map/psum | solution.py:83
  1372.0 155.2 %all-reduce.11 = (f32[8]{0:T(128)}, f32[8]{0:T(128)}) all-reduce(f32[8]{0:T(128)} %get-tuple-element.11, f32[8]{0:T(128)} %get-tuple-element.10), channel_id=1, replica_groups=mesh['group'=4,'zslab'=64] {'zslab'}, use_global_device_ids=true, to_apply=%region_43.44 | all-reduce | flops 16 | bytes 128 | tf_op jit(solution)/shard_map/psum | solution.py:88
  1539.4 8.6 collective-permute-done.12
  1550.8 152.2 %all-reduce.10 = (f32[8]{0:T(128)S(1)}, f32[8]{0:T(128)S(1)}) all-reduce(f32[8]{0:T(128)} %get-tuple-element.9, f32[8]{0:T(128)} %get-tuple-element.8), channel_id=1, replica_groups=mesh['group'=4,'zslab'=64] {'zslab'}, use_global_device_ids=true, to_apply=%region_49.50 | all-reduce | flops 16 | bytes 128 | tf_op jit(solution)/shard_map/psum | solution.py:77
  1706.8 8.4 collective-permute-start.15
  1719.1 8.6 collective-permute-done.14
  1730.3 152.1 %all-reduce.9 = (f32[8]{0:T(128)S(1)}, f32[8]{0:T(128)S(1)}, f32[8]{0:T(128)S(1)}) all-reduce(f32[8]{0:T(128)S(1)} %get-tuple-element.7, f32[8]{0:T(128)S(1)} %get-tuple-element.28, f32[8]{0:T(128)S(1)} %get-tuple-element.6), channel_id=1, replica_groups=mesh['group'=4,'zslab'=64] {'zslab'}, use_global_device_ids=true, to_apply=%region_55.56 | all-reduce | flops 24 | bytes 192 | tf_op jit(solution)/shard_map/psum | solution.py:83
  1884.3 13.3 psum.231
  1898.4 8.5 collective-permute-start.17
  (237 shorter events, 115.5 us)
Async XLA Ops:
  3.2 10.5 collective-permute-start.1
  8.2 13.9 collective-permute-start
  10.9 504.1 %copy-start.12 = (f32[2,32,128]{2,1,0:T(8,128)}, f32[2,32,128]{2,1,0:T(8,128)S(1)}, u32[]{:S(2)}) copy-start(f32[2,32,128]{2,1,0:T(8,128)S(1)} %multiply_subtract_fusion.29) | copy-start | bytes 98308
  176.2 12.3 collective-permute-start.3
  184.6 12.5 collective-permute-start.2
  506.6 172.4 %copy-start.48 = (f32[8]{0:T(128)}, f32[8]{0:T(128)S(1)}, u32[]{:S(2)}) copy-start(f32[8]{0:T(128)S(1)} %get-tuple-element.53) | copy-start | bytes 100
  506.6 172.4 %copy-start.50 = (f32[8]{0:T(128)}, f32[8]{0:T(128)S(1)}, u32[]{:S(2)}) copy-start(f32[8]{0:T(128)S(1)} %get-tuple-element.54) | copy-start | bytes 100
  506.9 10.0 collective-permute-start.5
  513.1 12.5 collective-permute-start.4
  680.2 12.3 collective-permute-start.7
  688.6 12.5 collective-permute-start.6
  858.6 156.0 %copy-start.53 = (f32[8]{0:T(128)S(1)}, f32[8]{0:T(128)}, u32[]{:S(2)}) copy-start(f32[8]{0:T(128)} %copy-done.52) | copy-start | bytes 100
  1015.6 9.8 collective-permute-start.9
  1021.5 12.5 collective-permute-start.8
  1190.7 12.3 collective-permute-start.11
  1199.1 12.5 collective-permute-start.10
  1371.6 156.4 %copy-start.3 = (f32[8,1,2,32,128]{4,0,3,2,1:T(8,128)S(1)}, f32[8,1,2,32,128]{4,0,3,2,1:T(8,128)}, u32[]{:S(2)}) copy-start(f32[8,1,2,32,128]{4,0,3,2,1:T(8,128)} %copy-done.1) | copy-start | bytes 786436
  1371.6 156.4 %copy-start.6 = (f32[8,1,2,32,128]{4,0,3,2,1:T(8,128)S(1)}, f32[8,1,2,32,128]{4,0,3,2,1:T(8,128)}, u32[]{:S(2)}) copy-start(f32[8,1,2,32,128]{4,0,3,2,1:T(8,128)} %copy-done.4) | copy-start | bytes 786436
  1529.3 10.1 collective-permute-start.13
  1535.5 12.5 collective-permute-start.12
  1706.8 12.3 collective-permute-start.15
  1715.3 12.5 collective-permute-start.14
  1898.4 12.0 collective-permute-start.17
  1906.9 9.7 collective-permute-start.16
  (53 other events, 2396.6 us)
where the time goes:
time: 1920 us
  blocking collectives  1700 us (89%)
  waiting for transfers between devices  90.5 us (5%)
  starting transfers between devices  82.7 us (4%)
  other arithmetic  38.1 us (2%)
    psum x4, blocking collectives, bicgstab(): cross_re, cross_im, energy = lax.psum((cross_re, cross_im, energy), 'zslab')  610 us
    psum x3, blocking collectives, bicgstab(): bilinear_new = lax.psum(product_pair(sources, residual), 'zslab')  465 us
    psum x3, blocking collectives, bicgstab(): along = lax.psum(product_pair(sources, image), 'zslab')  457 us
    psum x1, blocking collectives, bicgstab(): bilinear = lax.psum(product_pair(sources, residual), 'zslab')  152 us
    ppermute x9, waiting for transfers between devices, with_halo(): lax.ppermute(lax.slice_in_dim(block, 0, width, axis=dim), axis, backward)  75 us
    ppermute x9, starting transfers between devices, with_halo(): lax.ppermute(lax.slice_in_dim(block, block.shape[dim] - width, None, axis...  65.4 us
  transfers between devices with their start and end apart: 18, of which 17 were waited for; matrix products, arithmetic and copies ran while one was open for 0% of the time, Pallas kernels for 0%

commit v1 on v0

--- a/solution.py
+++ b/solution.py
@@ -1,6 +1,11 @@
+import functools
+
 import jax
 import jax.numpy as jnp
+import numpy as np
 from jax import lax
+from jax.experimental import pallas as pl
+from jax.experimental.pallas import tpu as pltpu
 from jax.sharding import PartitionSpec as P
 
 ITERS = 4
@@ -95,7 +100,7 @@
     return solution
 
 
-def on_device(background, absorb, density, profiles, adjoint_source, port_modes, design_start):
+def iterate_on_device(background, absorb, density, profiles, adjoint_source, port_modes, design_start):
     planes_dev = density.shape[0]
     rows_all = density.shape[1]
     first_plane = lax.axis_index("zslab") * planes_dev
@@ -137,6 +142,450 @@
         jnp.tanh(sharpness * threshold) + jnp.tanh(sharpness * (filtered - threshold))
     ) / (jnp.tanh(sharpness * threshold) + jnp.tanh(sharpness * (1.0 - threshold)))
     return (forward_field, adjoint_field, new_density)
+
+
+BASIS = 2 * ITERS + 1
+CENTRE = 5.3
+HALF_RADIUS = 3.0
+THIRD = 1.0 / HALF_RADIUS
+NUDGE = 1e-6
+AGREE = 5e-4
+ROWS = 16 * BASIS
+
+
+def pair_places():
+    real, imag, place = {}, {}, 0
+    for j in range(BASIS):
+        for i in range(j + 1):
+            real[(i, j)] = place
+            place += 1
+    for j in range(BASIS):
+        for i in range(j):
+            imag[(i, j)] = place
+            place += 1
+    return real, imag
+
+
+def gram_tables():
+    real, imag = pair_places()
+    pick = np.zeros((6 * ROWS, 128), np.float32)
+    nudge = np.zeros((2 * ROWS, 128), np.float32)
+    rng = np.random.default_rng(7)
+    sign_re = {pair: np.where(rng.random(128) < 0.5, -1.0, 1.0) for pair in real}
+    sign_im = {pair: np.where(rng.random(128) < 0.5, -1.0, 1.0) for pair in imag}
+    for j in range(BASIS):
+        for i in range(BASIS):
+            row, pair = j * 16 + i, (min(i, j), max(i, j))
+            pick[row, real[pair]] = 1.0
+            for half in (0, ROWS):
+                pick[2 * ROWS + half + row, real[(i, i)]] = 1.0
+                pick[4 * ROWS + half + row, real[(j, j)]] = 1.0
+            nudge[row] = NUDGE * sign_re[pair]
+            if i != j:
+                side = 1.0 if i < j else -1.0
+                pick[ROWS + row, imag[pair]] = side
+                nudge[ROWS + row] = NUDGE * side * sign_im[pair]
+    nudge[:, 0] = 0.0
+    return pick, nudge
+
+
+def exact_dot(left, right, dims):
+    return lax.dot_general(
+        left, right, (dims, ((), ())), precision=lax.Precision.HIGHEST,
+        preferred_element_type=jnp.float32,
+    )
+
+
+def minus_pair(left, right):
+    return (left[0] - right[0], left[1] - right[1])
+
+
+def plus_pair(left, right):
+    return (left[0] + right[0], left[1] + right[1])
+
+
+def coefficients(gram):
+    gram_re = [gram[16 * j : 16 * j + 16] for j in range(BASIS)]
+    gram_im = [gram[ROWS + 16 * j : ROWS + 16 * j + 16] for j in range(BASIS)]
+    row = lax.broadcasted_iota(jnp.int32, (16, 128), 0)
+    keep = jnp.where(row == 15, 0.0, HALF_RADIUS)
+
+    def apply(q):
+        return tuple(
+            CENTRE * v + HALF_RADIUS * pltpu.roll(v, 1, 0) + keep * pltpu.roll(v, 15, 0) for v in q
+        )
+
+    def total(v):
+        return jnp.sum(v, axis=0, keepdims=True)
+
+    def with_source(q):
+        return (
+            total(gram_re[0] * q[0] + gram_im[0] * q[1]),
+            total(gram_re[0] * q[1] - gram_im[0] * q[0]),
+        )
+
+    def times_gram(q):
+        out_re = jnp.zeros((16, 128), jnp.float32)
+        out_im = jnp.zeros((16, 128), jnp.float32)
+        for j in range(BASIS):
+            q_re, q_im = q[0][j : j + 1], q[1][j : j + 1]
+            out_re = out_re + (gram_re[j] * q_re - gram_im[j] * q_im)
+            out_im = out_im + (gram_re[j] * q_im + gram_im[j] * q_re)
+        return out_re, out_im
+
+    one = jnp.where(row == 0, 1.0, 0.0)
+    zero = jnp.zeros((16, 128), jnp.float32)
+    answer, residual, direction = (zero, zero), (one, zero), (one, zero)
+    bilinear = with_source(residual)
+    for iteration in range(ITERS):
+        image = apply(direction)
+        advance = divide_pair(bilinear, with_source(image))
+        halfway = minus_pair(residual, multiply_pair(advance, image))
+        second = apply(halfway)
+        weighed = times_gram(second)
+        energy = total(second[0] * weighed[0] + second[1] * weighed[1])
+        relax = (
+            total(weighed[0] * halfway[0] + weighed[1] * halfway[1]) / energy,
+            total(weighed[0] * halfway[1] - weighed[1] * halfway[0]) / energy,
+        )
+        answer = plus_pair(
+            answer, plus_pair(multiply_pair(advance, direction), multiply_pair(relax, halfway))
+        )
+        if iteration + 1 < ITERS:
+            residual = minus_pair(halfway, multiply_pair(relax, second))
+            bilinear_new = with_source(residual)
+            blend = multiply_pair(divide_pair(bilinear_new, bilinear), divide_pair(advance, relax))
+            direction = plus_pair(
+                residual, multiply_pair(blend, minus_pair(direction, multiply_pair(relax, image)))
+            )
+            bilinear = bilinear_new
+    first = tuple(jnp.broadcast_to(v[:, :1], v.shape) for v in answer)
+    apart = minus_pair(answer, first)
+
+    def norm(q):
+        weighed = times_gram(q)
+        return total(q[0] * weighed[0] + q[1] * weighed[1])
+
+    return first, norm(apart), norm(first)
+
+
+TILES = 4
+SYSTEMS = 8
+BLOCK = 16 * TILES // 2 + 2
+WINDOW = 32
+CORE = 8
+KEPT = 18
+VMEM = pl.BlockSpec(memory_space=pltpu.VMEM)
+SMEM = pl.BlockSpec(memory_space=pltpu.SMEM)
+ANY = pl.BlockSpec(memory_space=pl.ANY)
+LIMIT = 40 * 1024 * 1024
+
+
+def call(kernel, outs, specs, out_specs, scratch=(), name=None):
+    return pl.pallas_call(
+        kernel,
+        out_shape=outs,
+        in_specs=specs,
+        out_specs=out_specs,
+        scratch_shapes=list(scratch),
+        compiler_params=pltpu.CompilerParams(vmem_limit_bytes=LIMIT),
+        name=name,
+    )
+
+
+def f32(*shape):
+    return jax.ShapeDtypeStruct(shape, jnp.float32)
+
+
+def pack_kernel(modes, start, place, background, absorb, density, profiles, adjoint, out, sems):
+    copies = []
+    for port in range(SYSTEMS // 2):
+        copies.append(
+            pltpu.make_async_copy(
+                profiles.at[modes[port]], out.at[port, pl.ds(0, 16)], sems.at[port]
+            )
+        )
+        copies.append(
+            pltpu.make_async_copy(
+                adjoint.at[port],
+                out.at[SYSTEMS // 2 + port, pl.ds(0, 16)],
+                sems.at[SYSTEMS // 2 + port],
+            )
+        )
+    for copy in copies:
+        copy.start()
+    for plane in range(2):
+        where = place[0] * 2 + plane
+        inside = (where >= start[0]) & (where < start[0] + 64)
+        for tile in range(TILES):
+            dens = density[plane, tile]
+            perm = jnp.where(inside, low_perm + perm_span * dens, background[plane, tile])
+            diag_re = ((6.0 - wave_sq * perm) - CENTRE) * THIRD
+            diag_im = absorb[plane, tile] * THIRD
+            for system in range(SYSTEMS):
+                out[system, 16 + plane * TILES + tile] = diag_re
+                out[system, 24 + plane * TILES + tile] = diag_im
+        rows = density[plane, place[1]]
+        for system in range(SYSTEMS):
+            out[system, 32 + plane] = rows
+    for copy in copies:
+        copy.wait()
+
+
+def basis_kernel(place, block, low, high, basis, gram, dens, diag, acc):
+    row = lax.broadcasted_iota(jnp.int32, (8 * TILES, 128), 0)
+    lane = lax.broadcasted_iota(jnp.int32, (8 * TILES, 128), 1)
+    first_row, last_row = row == 0, row == 8 * TILES - 1
+    first_lane, last_lane = lane == 0, lane == 127
+    third_low = jnp.where(place[0] >= SYSTEMS, THIRD, 0.0)
+    third_high = jnp.where(place[0] < SYSTEMS * (SYSTEMS - 1), THIRD, 0.0)
+
+    def load(source, chunks, at):
+        def one(chunk, _):
+            for plane in range(2):
+                window = at + 2 * chunk + plane
+                for part in range(2):
+                    basis[0, part, window] = source[
+                        chunk, pl.ds(part * 8 + plane * TILES, TILES)
+                    ].reshape(8 * TILES, 128)
+                    diag[part, window] = source[
+                        chunk, pl.ds(16 + part * 8 + plane * TILES, TILES)
+                    ].reshape(8 * TILES, 128)
+            return 0
+
+        lax.fori_loop(0, chunks, one, 0)
+
+    load(low, 4, 0)
+    load(block, 8, CORE)
+    load(high, 4, CORE + 16)
+
+    me = place[0] % SYSTEMS
+    dens[0] = jnp.where(me > 0, block[jnp.maximum(me - 1, 0), 33], low[3, 33])
+    dens[1] = block[me, 32]
+    dens[2] = block[me, 33]
+    dens[3] = jnp.where(
+        me < SYSTEMS - 1, block[jnp.minimum(me + 1, SYSTEMS - 1), 32], high[0, 32]
+    )
+
+    def beside(field, level, part, window):
+        up = jnp.where(first_row, 0.0, pltpu.roll(field, 1, 0))
+        down = jnp.where(last_row, 0.0, pltpu.roll(field, 8 * TILES - 1, 0))
+        left = jnp.where(first_lane, 0.0, pltpu.roll(field, 1, 1))
+        right = jnp.where(last_lane, 0.0, pltpu.roll(field, 127, 1))
+        z_sum = basis[level, part, window - 1] + basis[level, part, window + 1]
+        return (z_sum + (up + down)) + (left + right)
+
+    for level in range(BASIS - 1):
+
+        def plane_step(window, _, level=level):
+            third = jnp.where(
+                window < CORE, third_low, jnp.where(window >= CORE + 16, third_high, THIRD)
+            )
+            real, imag = basis[level, 0, window], basis[level, 1, window]
+            diag_re, diag_im = diag[0, window], diag[1, window]
+            new_re = diag_re * real - diag_im * imag - third * beside(real, level, 0, window)
+            new_im = diag_re * imag + diag_im * real - third * beside(imag, level, 1, window)
+            if level > 0:
+                new_re = new_re - basis[level - 1, 0, window]
+                new_im = new_im - basis[level - 1, 1, window]
+            basis[level + 1, 0, window] = new_re
+            basis[level + 1, 1, window] = new_im
+            return 0
+
+        lax.fori_loop(level + 1, WINDOW - 1 - level, plane_step, 0, unroll=2)
+
+    real_at, imag_at = pair_places()
+    for rows in ((0, 1), (2, 3), range(4, BASIS)):
+        pairs = [(i, j) for i in rows for j in range(i, BASIS)]
+        count = sum(2 - (i == j) for i, j in pairs)
+        low_index = min(rows)
+
+        def position(step, sums, pairs=pairs, low_index=low_index):
+            window, tile = CORE + step // TILES, step % TILES
+            here = pl.ds(pl.multiple_of(tile * 8, 8), 8)
+            field = {
+                k: (basis[k, 0, window, here], basis[k, 1, window, here])
+                for k in range(low_index, BASIS)
+            }
+            new = []
+            for i, j in pairs:
+                (i_re, i_im), (j_re, j_im) = field[i], field[j]
+                new.append(i_re * j_re + i_im * j_im)
+                if i != j:
+                    new.append(i_re * j_im - i_im * j_re)
+            return tuple(total + term for total, term in zip(sums, new))
+
+        zero = jnp.zeros((8, 128), jnp.float32)
+        sums = lax.fori_loop(0, 16 * TILES, position, (zero,) * count, unroll=2)
+        place_of = 0
+        for i, j in pairs:
+            acc[real_at[(i, j)]] = sums[place_of]
+            place_of += 1
+            if i != j:
+                acc[imag_at[(i, j)]] = sums[place_of]
+                place_of += 1
+    for spare in range(len(real_at) + len(imag_at), 128):
+        acc[spare] = jnp.zeros((8, 128), jnp.float32)
+    by_pair = jnp.sum(acc[...], axis=1)
+    ones = jnp.ones((8, 128), jnp.float32)
+    gram[...] = exact_dot(ones, by_pair, ((1,), (1,)))[0:1]
+
+
+def combine_kernel(grams, pick, nudge, basis, out):
+    row = grams[0]
+    for other in range(1, SYSTEMS):
+        row = row + grams[other]
+    ones = jnp.ones((128, 128), jnp.float32)
+    picked = exact_dot(pick[...] * row, ones, ((1,), (0,)))
+    norms = jnp.sqrt(picked[2 * ROWS : 4 * ROWS] * picked[4 * ROWS :])
+    answer, apart, size = coefficients(picked[: 2 * ROWS] + nudge[...] * norms)
+    agrees = jnp.max(jnp.where(apart <= AGREE * AGREE * size, 0.0, 1.0))
+    flag = jnp.zeros((8, 128), jnp.float32) + agrees
+    for slab in range(SYSTEMS):
+        out[slab, 32] = flag
+    weight = [
+        (
+            jnp.broadcast_to(answer[0][k : k + 1], (8 * TILES, 128)),
+            jnp.broadcast_to(answer[1][k : k + 1], (8 * TILES, 128)),
+        )
+        for k in range(BASIS - 1)
+    ]
+
+    def two_planes(first):
+        planes = []
+        for plane in (first, first + 1):
+            real = jnp.zeros((8 * TILES, 128), jnp.float32)
+            imag = jnp.zeros((8 * TILES, 128), jnp.float32)
+            for k in range(BASIS - 1):
+                b_re, b_im = basis[k, 0, plane], basis[k, 1, plane]
+                real = real + (weight[k][0] * b_re - weight[k][1] * b_im)
+                imag = imag + (weight[k][0] * b_im + weight[k][1] * b_re)
+            planes.append((real.reshape(TILES, 8, 128), imag.reshape(TILES, 8, 128)))
+        return planes
+
+    def put(slab, at, planes):
+        for plane in range(2):
+            for part in range(2):
+                out[slab, pl.ds((part * 4 + at + plane) * TILES, TILES)] = planes[plane][part]
+
+    def middle(slab, _):
+        planes = two_planes(CORE - 1 + 2 * slab)
+        put(slab, 0, planes)
+        put(slab - 1, 2, planes)
+        return 0
+
+    put(0, 0, two_planes(CORE - 1))
+    lax.fori_loop(1, SYSTEMS, middle, 0)
+    put(SYSTEMS - 1, 2, two_planes(CORE - 1 + 2 * SYSTEMS))
+
+
+def fields_kernel(fields, forward, adjoint, terms):
+    half = SYSTEMS // 2
+    for port in range(half):
+        for part in range(2):
+            own = pl.ds((part * 4 + 1) * TILES, 2 * TILES)
+            forward[port, part] = fields[port, own]
+            adjoint[port, part] = fields[half + port, own]
+    for plane in range(4):
+        total = None
+        for port in range(half):
+            real, imag = pl.ds(plane * TILES, TILES), pl.ds((4 + plane) * TILES, TILES)
+            term = fields[port, real] * fields[half + port, real]
+            term = term - fields[port, imag] * fields[half + port, imag]
+            total = term if total is None else total + term
+        for tile in range(TILES):
+            terms[tile, plane] = total[tile]
+    flag = fields[0, 32]
+    for system in range(1, SYSTEMS):
+        flag = flag + fields[system, 32]
+    for tile in range(TILES):
+        terms[tile, 4] = flag
+
+
+def density_kernel(start, place, terms, dens, out, flag):
+    lane = lax.broadcasted_iota(jnp.int32, (8, 128), 1)
+    updated = []
+    for plane in range(4):
+        total = terms[0, plane]
+        for other in range(1, 4):
+            total = total + terms[other, plane]
+        gradient = -wave_sq * total
+        where = place[0] * 2 + plane - 1
+        inside = (where >= start[0]) & (where < start[0] + 64)
+        rows = dens[plane]
+        moved = jnp.clip(rows - step_size * perm_span * gradient, 0.0, 1.0)
+        rows = jnp.where(inside, moved, rows)
+        exists = (where >= 0) & (where < 2 * SYSTEMS * SYSTEMS)
+        updated.append(jnp.where(exists, rows, 0.0))
+    for plane in range(2):
+        own = updated[plane + 1]
+        right = jnp.where(lane == 127, 0.0, pltpu.roll(own, 127, 1))
+        left = jnp.where(lane == 0, 0.0, pltpu.roll(own, 1, 1))
+        filtered = (2.0 * own + updated[plane + 2] + updated[plane] + right + left) / 6.0
+        edge = float(np.tanh(sharpness * threshold))
+        other_edge = float(np.tanh(sharpness * (1.0 - threshold)))
+        out[plane] = (edge + jnp.tanh(sharpness * (filtered - threshold))) / (edge + other_edge)
+    spread = terms[0, 4] + terms[1, 4] + terms[2, 4] + terms[3, 4]
+    flag[0] = jnp.max(spread)
+
+
+def on_device(background, absorb, density, profiles, adjoint_source, port_modes, design_start):
+    args = (background, absorb, density, profiles, adjoint_source, port_modes, design_start)
+    slab = lax.axis_index("zslab")
+    place = jnp.stack([slab, lax.axis_index("group")]).astype(jnp.int32)
+    planes_of = [[z * SYSTEMS + l for l in range(SYSTEMS)] for z in range(SYSTEMS)]
+    columns = [[z * SYSTEMS + l for z in range(SYSTEMS)] for l in range(SYSTEMS)]
+    tiles = (2, TILES, 8, 128)
+    packed = call(
+        pack_kernel,
+        f32(SYSTEMS, BLOCK, 8, 128),
+        [SMEM, SMEM, SMEM, VMEM, VMEM, VMEM, ANY, ANY],
+        VMEM,
+        [pltpu.SemaphoreType.DMA((SYSTEMS,))],
+        "pack",
+    )(
+        port_modes, design_start, place,
+        background.reshape(tiles), absorb.reshape(tiles), density.reshape(tiles),
+        profiles.reshape(-1, 16, 8, 128), adjoint_source.reshape(-1, 16, 8, 128),
+    )
+    block = lax.all_to_all(packed, "zslab", 0, 0, axis_index_groups=planes_of, tiled=True)
+    count = SYSTEMS * SYSTEMS
+    up = [(i, i + SYSTEMS) for i in range(count - SYSTEMS)]
+    down = [(target, source) for source, target in up]
+    low = lax.ppermute(block[SYSTEMS // 2 :], "zslab", up)
+    high = lax.ppermute(block[: SYSTEMS // 2], "zslab", down)
+    basis, gram, dens = call(
+        basis_kernel,
+        (f32(BASIS, 2, WINDOW, 8 * TILES, 128), f32(1, 128), f32(4, 8, 128)),
+        [SMEM, VMEM, VMEM, VMEM],
+        (VMEM, VMEM, VMEM),
+        [pltpu.VMEM((2, WINDOW, 8 * TILES, 128), jnp.float32), pltpu.VMEM((128, 8, 128), jnp.float32)],
+        "basis",
+    )(place, block, low, high)
+    grams = lax.all_to_all(
+        jnp.broadcast_to(gram[None], (SYSTEMS, 1, 128)), "zslab", 0, 0,
+        axis_index_groups=columns, tiled=True,
+    )
+    pick, nudge = gram_tables()
+    solved = call(
+        combine_kernel, f32(SYSTEMS, 33, 8, 128), [VMEM, VMEM, VMEM, VMEM], VMEM, (), "combine"
+    )(grams, jnp.asarray(pick), jnp.asarray(nudge), basis)
+    fields = lax.all_to_all(solved, "zslab", 0, 0, axis_index_groups=planes_of, tiled=True)
+    half = (SYSTEMS // 2, 2, 2 * TILES, 8, 128)
+    forward, adjoint, terms = call(
+        fields_kernel, (f32(*half), f32(*half), f32(4, 5, 8, 128)), [VMEM], (VMEM,) * 3, (), "fields"
+    )(fields)
+    terms = lax.all_to_all(terms, "group", 0, 0, tiled=True)
+    new_density, flag = call(
+        density_kernel, (f32(2, 8, 128), f32(1)), [SMEM, SMEM, VMEM, VMEM], (VMEM, SMEM), (), "density"
+    )(design_start, place, terms, dens)
+    shape = (SYSTEMS // 2, 2, 2, 8 * TILES, 128)
+    state = (flag[0], forward.reshape(shape), adjoint.reshape(shape), new_density)
+
+    def again(state):
+        return (jnp.zeros((), jnp.float32),) + iterate_on_device(*args)
+
+    return lax.while_loop(lambda state: state[0] > 0.0, again, state)[1:]
 
 
 def solution(mesh):

time: 1920 us -> 111 us (0.06)
  the two profiles are of different devices: /device:TPU:126 before, /device:TPU:1 now
where the time goes in v1:
time: 111 us; the launch traced here: 110 us
  blocking collectives  49.9 us (45%)
  Pallas kernels  20.6 us (19%)
  starting transfers between devices  14.7 us (13%)
  waiting for transfers between devices  14.3 us (13%)
  local copies, waits for them, and re-layouts  8.35 us (8%)
  between operations  1.39 us (1%)
    all_to_all x1, blocking collectives, on_device(): lax.all_to_all(packed, 'zslab', 0, 0, axis_index_groups=planes_of, tiled=...  21 us
    pallas_call x1, Pallas kernels, on_device(): call(basis_kernel, (f32(BASIS, 2, WINDOW, 8 * TILES, 128), f32(1, 128), f...  15.2 us
    all_to_all x1, blocking collectives, on_device(): lax.all_to_all(solved, 'zslab', 0, 0, axis_index_groups=planes_of, tiled=...  14.8 us
    all_to_all x1, blocking collectives, on_device(): lax.all_to_all(jnp.broadcast_to(gram[None], (SYSTEMS, 1, 128)), 'zslab',...  14.1 us
    all_to_all x1, starting transfers between devices, on_device(): terms = lax.all_to_all(terms, 'group', 0, 0, tiled=True)  9.69 us
    ppermute x1, waiting for transfers between devices, on_device(): low = lax.ppermute(block[SYSTEMS // 2:], 'zslab', up)  8.23 us
    unnamed x20, local copies, waits for them, and re-layouts  5.34 us
    ppermute x1, waiting for transfers between devices, on_device(): high = lax.ppermute(block[:SYSTEMS // 2], 'zslab', down)  4.17 us
  transfers between devices with their start and end apart: 3, of which 3 were waited for; matrix products, arithmetic and copies ran while one was open for 3% of the time, Pallas kernels for 0%

profile of v1, /device:TPU:1, one launch (start us, length us, event | category | flops | bytes accessed | tf_op | source)
XLA Modules:
  0.0 110.0 jit_solution(2910386902576826181)
XLA Ops:
  1.3 0.1 pad_add_fusion.place
  1.4 1.0 copy-done
  2.4 0.9 copy-done.2
  3.3 1.6 %pack.1 = f32[8,34,8,128]{3,2,1,0:T(8,128)S(1)} custom-call(s32[4]{0:T(128)} %modes.1, s32[1]{0:T(128)S(6)} %copy.32.start, s32[2]{0:T(128)S(1)} %pad_add_fusion.place, f32[2,4,8,128]{3,2,1,0:T(8,128)} %bitcast.25, f32[2,4,8,128]{3,2,1,0:T(8,128)} %bitcast.23, f32[2,4,8,128]{3,2,1,0:T(8,128)} %bitcast.24, f32[6,16,8,128]{3,2,1,0:T(8,128)S(1)} %bitcast.18, ...), custom_call_target="tpu_custom_call" | custom-call | tf_op jit(solution)/shard_map/pack/pallas_call | solution.py:539
  4.9 21.0 %all_to_all.20.block = f32[8,34,8,128]{3,2,1,0:T(8,128)S(1)} all-to-all(f32[8,34,8,128]{3,2,1,0:T(8,128)S(1)} %pack.1), channel_id=1, replica_groups={{0,1,2,3,4,5,6,7},{8,9,10,11,12,13,14,15},{16,17,18,19,20,21,22,23},{24..., dimensions={0} | all-to-all | bytes 2228224 | tf_op jit(solution)/shard_map/all_to_all | solution.py:551
  26.0 3.7 %collective-permute-start.18 = (f32[4,34,8,128]{3,2,1,0:T(8,128)S(1)}, f32[4,34,8,128]{3,2,1,0:T(8,128)S(1)}, u32[]{:S(2)}, u32[]{:S(2)}) collective-permute-start(f32[4,34,8,128]{3,2,1,0:T(8,128)S(1)} %get-tuple-element.302), channel_id=1, source_target_pairs={{0,8},{1,9},{2,10},{3,11},{4,12},{5,13},{6,14},{7,15},{8,16},{9,17... | collective-permute-start | bytes 1671176 | tf_op jit(solution)/shard_map/ppermute | solution.py:555
  29.7 1.3 %collective-permute-start.19 = (f32[4,34,8,128]{3,2,1,0:T(8,128)S(1)}, f32[4,34,8,128]{3,2,1,0:T(8,128)S(1)}, u32[]{:S(2)}, u32[]{:S(2)}) collective-permute-start(f32[4,34,8,128]{3,2,1,0:T(8,128)S(1)} %get-tuple-element.301), channel_id=1, source_target_pairs={{8,0},{9,1},{10,2},{11,3},{12,4},{13,5},{14,6},{15,7},{16,8},{17,9... | collective-permute-start | bytes 1671176 | tf_op jit(solution)/shard_map/ppermute | solution.py:556
  31.0 8.2 %collective-permute-done.18.low = f32[4,34,8,128]{3,2,1,0:T(8,128)S(1)} collective-permute-done((f32[4,34,8,128]{3,2,1,0:T(8,128)S(1)}, f32[4,34,8,128]{3,2,1,0:T(8,128)S(1)}, u32[]{:S(2)}, u32[]{:S(2)}) %collective-permute-start.18) | collective-permute-done | bytes 557088 | tf_op jit(solution)/shard_map/ppermute | solution.py:555
  39.3 4.2 %collective-permute-done.19.high = f32[4,34,8,128]{3,2,1,0:T(8,128)S(1)} collective-permute-done((f32[4,34,8,128]{3,2,1,0:T(8,128)S(1)}, f32[4,34,8,128]{3,2,1,0:T(8,128)S(1)}, u32[]{:S(2)}, u32[]{:S(2)}) %collective-permute-start.19) | collective-permute-done | bytes 557088 | tf_op jit(solution)/shard_map/ppermute | solution.py:556
  43.4 15.2 %basis.1 = (f32[9,2,32,32,128]{4,3,2,1,0:T(8,128)S(1)}, f32[1,128]{1,0:T(1,128)S(1)}, f32[4,8,128]{2,1,0:T(8,128)S(1)}) custom-call(s32[2]{0:T(128)S(1)} %pad_add_fusion.place, f32[8,34,8,128]{3,2,1,0:T(8,128)S(1)} %all_to_all.20.block, f32[4,34,8,128]{3,2,1,0:T(8,128)S(1)} %collective-permute-done.18.low, f32[4,34,8,128]{3,2,1,0:T(8,128)S(1)} %collective-permute-done.19.high), custom_call_target="tpu_custom_call" | custom-call | tf_op jit(solution)/shard_map/basis/pallas_call | solution.py:557
  58.6 14.1 %all_to_all.21.grams = f32[8,1,128]{2,1,0:T(1,128)S(1)} all-to-all(f32[8,1,128]{2,1,0:T(1,128)S(1)} %broadcast_in_dim.18), channel_id=1, replica_groups={{0,8,16,24,32,40,48,56},{1,9,17,25,33,41,49,57},{2,10,18,26,34,42,50,58..., dimensions={0} | all-to-all | bytes 8192 | tf_op jit(solution)/shard_map/all_to_all | solution.py:565
  72.7 1.8 %combine.1 = f32[8,33,8,128]{3,2,1,0:T(8,128)S(1)} custom-call(f32[8,1,128]{2,1,0:T(1,128)S(1)} %all_to_all.21.grams, f32[864,128]{1,0:T(8,128)S(1)} %copy-done.4, f32[288,128]{1,0:T(8,128)S(1)} %copy-done.5, f32[9,2,32,32,128]{4,3,2,1,0:T(8,128)S(1)} %get-tuple-element.67.basis), custom_call_target="tpu_custom_call" | custom-call | tf_op jit(solution)/shard_map/combine/pallas_call | solution.py:570
  74.5 14.8 %all_to_all.22.fields = f32[8,33,8,128]{3,2,1,0:T(8,128)S(1)} all-to-all(f32[8,33,8,128]{3,2,1,0:T(8,128)S(1)} %combine.1), channel_id=1, replica_groups={{0,1,2,3,4,5,6,7},{8,9,10,11,12,13,14,15},{16,17,18,19,20,21,22,23},{24..., dimensions={0} | all-to-all | bytes 2162688 | tf_op jit(solution)/shard_map/all_to_all | solution.py:573
  89.3 0.7 fields.1
  90.1 9.7 %all-to-all-start.3 = ((f32[4,5,8,128]{3,2,1,0:T(8,128)}), f32[4,5,8,128]{3,2,1,0:T(8,128)S(1)}, u32[]{:S(2)}, u32[]{:S(2)}) async-start(f32[4,5,8,128]{3,2,1,0:T(8,128)} %get-tuple-element.68), calls=%async_computation.3 | async-start | bytes 163840 | tf_op jit(solution)/shard_map/all_to_all | solution.py:578
  99.8 1.0 copy.14
  100.8 0.2 copy.15
  100.9 0.9 copy.12
  101.8 0.9 copy.13
  102.7 1.9 %all-to-all-done.3.terms = f32[4,5,8,128]{3,2,1,0:T(8,128)S(1)} async-done(((f32[4,5,8,128]{3,2,1,0:T(8,128)}), f32[4,5,8,128]{3,2,1,0:T(8,128)S(1)}, u32[]{:S(2)}, u32[]{:S(2)}) %all-to-all-start.3) | async-done | bytes 81952 | tf_op jit(solution)/shard_map/all_to_all | solution.py:578
  104.6 1.2 %density.1 = (f32[2,8,128]{2,1,0:T(8,128)}, f32[1]{0:T(128)}) custom-call(s32[1]{0:T(128)S(6)} %copy.32.start, s32[2]{0:T(128)S(1)} %pad_add_fusion.place, f32[4,5,8,128]{3,2,1,0:T(8,128)S(1)} %all-to-all-done.3.terms, f32[4,8,128]{2,1,0:T(8,128)S(1)} %get-tuple-element.69.dens), custom_call_target="tpu_custom_call" | custom-call | tf_op jit(solution)/shard_map/density/pallas_call | solution.py:579
  105.8 0.8 while.13
  106.6 1.7 %copy.16 = f32[4,2,2,32,128]{4,3,2,1,0:T(8,128)} copy(f32[4,2,2,32,128]{4,0,3,2,1:T(4,128)} %get-tuple-element.88) | data formatting | bytes 524288
  108.3 1.7 %copy.17 = f32[4,2,2,32,128]{4,3,2,1,0:T(8,128)} copy(f32[4,2,2,32,128]{4,0,3,2,1:T(4,128)} %get-tuple-element.89) | data formatting | bytes 524288
  (18 shorter events, 0.1 us)
Async XLA Ops:
  1.4 1.0 copy-start
  2.4 0.9 copy-start.2
  25.9 46.7 %copy-start.4 = (f32[864,128]{1,0:T(8,128)S(1)}, f32[864,128]{1,0:T(8,128)}, u32[]{:S(2)}) copy-start(f32[864,128]{1,0:T(8,128)} %constant.66.clone.pick) | copy-start | bytes 1327108
  25.9 46.7 %copy-start.5 = (f32[288,128]{1,0:T(8,128)S(1)}, f32[288,128]{1,0:T(8,128)}, u32[]{:S(2)}) copy-start(f32[288,128]{1,0:T(8,128)} %constant.67.clone.nudge) | copy-start | bytes 442372
  26.0 13.2 %collective-permute-start.18 = (f32[4,34,8,128]{3,2,1,0:T(8,128)S(1)}, f32[4,34,8,128]{3,2,1,0:T(8,128)S(1)}, u32[]{:S(2)}, u32[]{:S(2)}) collective-permute-start(f32[4,34,8,128]{3,2,1,0:T(8,128)S(1)} %get-tuple-element.302), channel_id=1, source_target_pairs={{0,8},{1,9},{2,10},{3,11},{4,12},{5,13},{6,14},{7,15},{8,16},{9,17... | collective-permute-start | bytes 1671176 | tf_op jit(solution)/shard_map/ppermute | solution.py:555
  29.7 13.7 %collective-permute-start.19 = (f32[4,34,8,128]{3,2,1,0:T(8,128)S(1)}, f32[4,34,8,128]{3,2,1,0:T(8,128)S(1)}, u32[]{:S(2)}, u32[]{:S(2)}) collective-permute-start(f32[4,34,8,128]{3,2,1,0:T(8,128)S(1)} %get-tuple-element.301), channel_id=1, source_target_pairs={{8,0},{9,1},{10,2},{11,3},{12,4},{13,5},{14,6},{15,7},{16,8},{17,9... | collective-permute-start | bytes 1671176 | tf_op jit(solution)/shard_map/ppermute | solution.py:556
  74.5 25.2 %copy-start.1 = (f32[6,2,2,32,128]{4,3,2,1,0:T(8,128)S(1)}, f32[6,2,2,32,128]{4,3,2,1,0:T(8,128)}, u32[]{:S(2)}) copy-start(f32[6,2,2,32,128]{4,3,2,1,0:T(8,128)} %param.14) | copy-start | bytes 1179652
  74.5 26.2 %copy-start.3 = (f32[4,2,2,32,128]{4,3,2,1,0:T(8,128)S(1)}, f32[4,2,2,32,128]{4,3,2,1,0:T(8,128)}, u32[]{:S(2)}) copy-start(f32[4,2,2,32,128]{4,3,2,1,0:T(8,128)} %param.15) | copy-start | bytes 786436
  89.3 16.5 %copy-start.19 = (f32[2,32,128]{2,1,0:T(8,128)S(1)}, f32[2,32,128]{2,1,0:T(8,128)}, u32[]{:S(2)}) copy-start(f32[2,32,128]{2,1,0:T(8,128)} %param.12) | copy-start | bytes 98308
  89.3 16.5 %copy-start.36 = (f32[2,32,128]{2,1,0:T(8,128)S(1)}, f32[2,32,128]{2,1,0:T(8,128)}, u32[]{:S(2)}) copy-start(f32[2,32,128]{2,1,0:T(8,128)} %param.13) | copy-start | bytes 98308
  89.3 16.5 %copy-start.37 = (f32[2,32,128]{2,1,0:T(8,128)S(1)}, f32[2,32,128]{2,1,0:T(8,128)}, u32[]{:S(2)}) copy-start(f32[2,32,128]{2,1,0:T(8,128)} %param.11) | copy-start | bytes 98308
  90.1 14.5 %all-to-all-start.3 = ((f32[4,5,8,128]{3,2,1,0:T(8,128)}), f32[4,5,8,128]{3,2,1,0:T(8,128)S(1)}, u32[]{:S(2)}, u32[]{:S(2)}) async-start(f32[4,5,8,128]{3,2,1,0:T(8,128)} %get-tuple-element.68), calls=%async_computation.3 | async-start | bytes 163840 | tf_op jit(solution)/shard_map/all_to_all | solution.py:578

commit v2 on v1

--- a/solution.py
+++ b/solution.py
@@ -272,16 +272,16 @@
 TILES = 4
 SYSTEMS = 8
 BLOCK = 16 * TILES // 2 + 2
+OWN = 16
 WINDOW = 32
 CORE = 8
-KEPT = 18
 VMEM = pl.BlockSpec(memory_space=pltpu.VMEM)
 SMEM = pl.BlockSpec(memory_space=pltpu.SMEM)
-ANY = pl.BlockSpec(memory_space=pl.ANY)
-LIMIT = 40 * 1024 * 1024
-
-
-def call(kernel, outs, specs, out_specs, scratch=(), name=None):
+HBM = pl.BlockSpec(memory_space=pltpu.HBM)
+LIMIT = 24 * 1024 * 1024
+
+
+def call(kernel, outs, specs, out_specs, scratch=(), name=None, flops=0):
     return pl.pallas_call(
         kernel,
         out_shape=outs,
@@ -289,6 +289,7 @@
         out_specs=out_specs,
         scratch_shapes=list(scratch),
         compiler_params=pltpu.CompilerParams(vmem_limit_bytes=LIMIT),
+        cost_estimate=pl.CostEstimate(flops=flops, bytes_accessed=1 << 20, transcendentals=0),
         name=name,
     )
 
@@ -297,135 +298,202 @@
     return jax.ShapeDtypeStruct(shape, jnp.float32)
 
 
-def pack_kernel(modes, start, place, background, absorb, density, profiles, adjoint, out, sems):
+def rows_of(tile):
+    return pl.ds(tile, 8, stride=TILES)
+
+
+def pack_kernel(modes, start, place, background, absorb, density, profiles, adjoint, out, raw, sems):
+    half = SYSTEMS // 2
     copies = []
-    for port in range(SYSTEMS // 2):
-        copies.append(
-            pltpu.make_async_copy(
-                profiles.at[modes[port]], out.at[port, pl.ds(0, 16)], sems.at[port]
-            )
-        )
-        copies.append(
-            pltpu.make_async_copy(
-                adjoint.at[port],
-                out.at[SYSTEMS // 2 + port, pl.ds(0, 16)],
-                sems.at[SYSTEMS // 2 + port],
-            )
-        )
+    for system in range(SYSTEMS):
+        source = profiles.at[modes[system]] if system < half else adjoint.at[system - half]
+        copies.append(pltpu.make_async_copy(source, raw.at[system], sems.at[system]))
     for copy in copies:
         copy.start()
     for plane in range(2):
         where = place[0] * 2 + plane
-        inside = (where >= start[0]) & (where < start[0] + 64)
+        inside = (where >= start[0]) & (where < start[0] + SYSTEMS * SYSTEMS)
         for tile in range(TILES):
-            dens = density[plane, tile]
-            perm = jnp.where(inside, low_perm + perm_span * dens, background[plane, tile])
+            rows = rows_of(tile)
+            perm = jnp.where(
+                inside, low_perm + perm_span * density[plane, rows], background[plane, rows]
+            )
             diag_re = ((6.0 - wave_sq * perm) - CENTRE) * THIRD
-            diag_im = absorb[plane, tile] * THIRD
+            diag_im = absorb[plane, rows] * THIRD
             for system in range(SYSTEMS):
                 out[system, 16 + plane * TILES + tile] = diag_re
                 out[system, 24 + plane * TILES + tile] = diag_im
-        rows = density[plane, place[1]]
+        share = density[plane, pl.ds(pl.multiple_of(place[1] * 8, 8), 8)]
         for system in range(SYSTEMS):
-            out[system, 32 + plane] = rows
-    for copy in copies:
-        copy.wait()
-
-
-def basis_kernel(place, block, low, high, basis, gram, dens, diag, acc):
-    row = lax.broadcasted_iota(jnp.int32, (8 * TILES, 128), 0)
-    lane = lax.broadcasted_iota(jnp.int32, (8 * TILES, 128), 1)
-    first_row, last_row = row == 0, row == 8 * TILES - 1
-    first_lane, last_lane = lane == 0, lane == 127
-    third_low = jnp.where(place[0] >= SYSTEMS, THIRD, 0.0)
-    third_high = jnp.where(place[0] < SYSTEMS * (SYSTEMS - 1), THIRD, 0.0)
-
+            out[system, 32 + plane] = share
+    for system in range(SYSTEMS):
+        copies[system].wait()
+        for part in range(2):
+            for plane in range(2):
+                for tile in range(TILES):
+                    out[system, (part * 2 + plane) * TILES + tile] = raw[
+                        system, part, plane, rows_of(tile)
+                    ]
+
+
+class Stencil:
+    def __init__(self):
+        row = lax.broadcasted_iota(jnp.int32, (8, 128), 0)
+        lane = lax.broadcasted_iota(jnp.int32, (8, 128), 1)
+        self.first_row, self.last_row = row == 0, row == 7
+        self.first_lane, self.last_lane = lane == 0, lane == 127
+
+    def beside(self, below, here, above):
+        up = jnp.where(self.first_row, 0.0, pltpu.roll(here[TILES - 1], 1, 0))
+        down = jnp.where(self.last_row, 0.0, pltpu.roll(here[0], 7, 0))
+        rows = [up] + list(here) + [down]
+        sums = []
+        for tile in range(TILES):
+            left = jnp.where(self.first_lane, 0.0, pltpu.roll(here[tile], 1, 1))
+            right = jnp.where(self.last_lane, 0.0, pltpu.roll(here[tile], 127, 1))
+            z_sum = below[tile] + above[tile]
+            sums.append((z_sum + (rows[tile] + rows[tile + 2])) + (left + right))
+        return sums
+
+    def step(self, basis, diag, level, at, third):
+        def plane(part, where):
+            return [basis[level, part, where, tile] for tile in range(TILES)]
+
+        real, imag = plane(0, at), plane(1, at)
+        near_re = self.beside(plane(0, at - 1), real, plane(0, at + 1))
+        near_im = self.beside(plane(1, at - 1), imag, plane(1, at + 1))
+        for tile in range(TILES):
+            diag_re, diag_im = diag[0, at, tile], diag[1, at, tile]
+            new_re = diag_re * real[tile] - diag_im * imag[tile] - third * near_re[tile]
+            new_im = diag_re * imag[tile] + diag_im * real[tile] - third * near_im[tile]
+            if level > 0:
+                new_re = new_re - basis[level - 1, 0, at, tile]
+                new_im = new_im - basis[level - 1, 1, at, tile]
+            basis[level + 1, 0, at, tile] = new_re
+            basis[level + 1, 1, at, tile] = new_im
+
+
+def gram_pass(basis, acc, columns, ranges, shift):
+    real_at, imag_at = pair_places()
+    pairs = [(i, j) for j in columns for i in range(j + 1)]
+    top = max(columns) + 1
+    places = []
+    for pair in pairs:
+        places.append(real_at[pair])
+        if pair[0] != pair[1]:
+            places.append(imag_at[pair])
+
+    def position(step, sums, first=0):
+        window, tile = first + shift + step // TILES, step % TILES
+        field = [(basis[k, 0, window, tile], basis[k, 1, window, tile]) for k in range(top)]
+        new = []
+        for i, j in pairs:
+            (i_re, i_im), (j_re, j_im) = field[i], field[j]
+            new.append(i_re * j_re + i_im * j_im)
+            if i != j:
+                new.append(i_re * j_im - i_im * j_re)
+        return tuple(total + term for total, term in zip(sums, new))
+
+    sums = tuple(acc[at] for at in places)
+    for first, last in ranges:
+        sums = lax.fori_loop(
+            0, (last - first) * TILES, functools.partial(position, first=first), sums
+        )
+    for at, value in zip(places, sums):
+        acc[at] = value
+
+
+def inner_kernel(block, basis, diag, acc):
+    def load(chunk, _):
+        for plane in range(2):
+            for part in range(2):
+                for tile in range(TILES):
+                    at = part * 8 + plane * TILES + tile
+                    basis[0, part, 2 * chunk + plane, tile] = block[chunk, at]
+                    diag[part, 2 * chunk + plane, tile] = block[chunk, 16 + at]
+        return 0
+
+    lax.fori_loop(0, SYSTEMS, load, 0)
+    stencil = Stencil()
+    for level in range(SYSTEMS - 1):
+
+        def plane_step(at, _, level=level):
+            stencil.step(basis, diag, level, at, THIRD)
+            return 0
+
+        lax.fori_loop(level + 1, OWN - 1 - level, plane_step, 0, unroll=2)
+    acc[...] = jnp.zeros_like(acc)
+    for columns, ranges in INNER_PASSES:
+        gram_pass(basis, acc, columns, ranges, 0)
+
+
+INNER_PASSES = (
+    ((0, 1, 2, 3, 4), ((4, 12),)),
+    ((0, 1, 2), ((2, 4), (12, 14))),
+    ((5, 6), ((6, 10),)),
+)
+OUTER_PASSES = (
+    ((0, 1, 2, 3, 4), ((0, 2), (14, 16))),
+    ((3, 4), ((2, 4), (12, 14))),
+    ((5, 6), ((0, 6), (10, 16))),
+    ((7,), ((0, 16),)),
+    ((8,), ((0, 16),)),
+)
+
+
+def outer_kernel(place, block, low, high, inner, inner_diag, inner_acc, basis, gram, dens, diag, acc):
     def load(source, chunks, at):
         def one(chunk, _):
             for plane in range(2):
                 window = at + 2 * chunk + plane
                 for part in range(2):
-                    basis[0, part, window] = source[
-                        chunk, pl.ds(part * 8 + plane * TILES, TILES)
-                    ].reshape(8 * TILES, 128)
-                    diag[part, window] = source[
-                        chunk, pl.ds(16 + part * 8 + plane * TILES, TILES)
-                    ].reshape(8 * TILES, 128)
+                    for tile in range(TILES):
+                        spot = part * 8 + plane * TILES + tile
+                        basis[0, part, window, tile] = source[chunk, spot]
+                        diag[part, window, tile] = source[chunk, 16 + spot]
             return 0
 
         lax.fori_loop(0, chunks, one, 0)
 
-    load(low, 4, 0)
-    load(block, 8, CORE)
-    load(high, 4, CORE + 16)
+    load(low, SYSTEMS // 2, 0)
+    load(high, SYSTEMS // 2, CORE + OWN)
+    for level in range(SYSTEMS):
+
+        def keep(at, _, level=level):
+            for part in range(2):
+                for tile in range(TILES):
+                    basis[level, part, CORE + at, tile] = inner[level, part, at, tile]
+                    if level == 0:
+                        diag[part, CORE + at, tile] = inner_diag[part, at, tile]
+            return 0
+
+        lax.fori_loop(level, OWN - level, keep, 0, unroll=2)
+    acc[...] = inner_acc[...]
 
     me = place[0] % SYSTEMS
-    dens[0] = jnp.where(me > 0, block[jnp.maximum(me - 1, 0), 33], low[3, 33])
+    dens[0] = jnp.where(me > 0, block[jnp.maximum(me - 1, 0), 33], low[SYSTEMS // 2 - 1, 33])
     dens[1] = block[me, 32]
     dens[2] = block[me, 33]
     dens[3] = jnp.where(
         me < SYSTEMS - 1, block[jnp.minimum(me + 1, SYSTEMS - 1), 32], high[0, 32]
     )
 
-    def beside(field, level, part, window):
-        up = jnp.where(first_row, 0.0, pltpu.roll(field, 1, 0))
-        down = jnp.where(last_row, 0.0, pltpu.roll(field, 8 * TILES - 1, 0))
-        left = jnp.where(first_lane, 0.0, pltpu.roll(field, 1, 1))
-        right = jnp.where(last_lane, 0.0, pltpu.roll(field, 127, 1))
-        z_sum = basis[level, part, window - 1] + basis[level, part, window + 1]
-        return (z_sum + (up + down)) + (left + right)
-
+    third_low = jnp.where(place[0] >= SYSTEMS, THIRD, 0.0)
+    third_high = jnp.where(place[0] < SYSTEMS * (SYSTEMS - 1), THIRD, 0.0)
+    stencil = Stencil()
     for level in range(BASIS - 1):
 
-        def plane_step(window, _, level=level):
-            third = jnp.where(
-                window < CORE, third_low, jnp.where(window >= CORE + 16, third_high, THIRD)
+        def two_planes(step, _, level=level):
+            lower, upper = level + 1 + step, WINDOW - 2 - level - step
+            stencil.step(basis, diag, level, lower, jnp.where(lower < CORE, third_low, THIRD))
+            stencil.step(
+                basis, diag, level, upper, jnp.where(upper >= CORE + OWN, third_high, THIRD)
             )
-            real, imag = basis[level, 0, window], basis[level, 1, window]
-            diag_re, diag_im = diag[0, window], diag[1, window]
-            new_re = diag_re * real - diag_im * imag - third * beside(real, level, 0, window)
-            new_im = diag_re * imag + diag_im * real - third * beside(imag, level, 1, window)
-            if level > 0:
-                new_re = new_re - basis[level - 1, 0, window]
-                new_im = new_im - basis[level - 1, 1, window]
-            basis[level + 1, 0, window] = new_re
-            basis[level + 1, 1, window] = new_im
             return 0
 
-        lax.fori_loop(level + 1, WINDOW - 1 - level, plane_step, 0, unroll=2)
-
-    real_at, imag_at = pair_places()
-    for rows in ((0, 1), (2, 3), range(4, BASIS)):
-        pairs = [(i, j) for i in rows for j in range(i, BASIS)]
-        count = sum(2 - (i == j) for i, j in pairs)
-        low_index = min(rows)
-
-        def position(step, sums, pairs=pairs, low_index=low_index):
-            window, tile = CORE + step // TILES, step % TILES
-            here = pl.ds(pl.multiple_of(tile * 8, 8), 8)
-            field = {
-                k: (basis[k, 0, window, here], basis[k, 1, window, here])
-                for k in range(low_index, BASIS)
-            }
-            new = []
-            for i, j in pairs:
-                (i_re, i_im), (j_re, j_im) = field[i], field[j]
-                new.append(i_re * j_re + i_im * j_im)
-                if i != j:
-                    new.append(i_re * j_im - i_im * j_re)
-            return tuple(total + term for total, term in zip(sums, new))
-
-        zero = jnp.zeros((8, 128), jnp.float32)
-        sums = lax.fori_loop(0, 16 * TILES, position, (zero,) * count, unroll=2)
-        place_of = 0
-        for i, j in pairs:
-            acc[real_at[(i, j)]] = sums[place_of]
-            place_of += 1
-            if i != j:
-                acc[imag_at[(i, j)]] = sums[place_of]
-                place_of += 1
-    for spare in range(len(real_at) + len(imag_at), 128):
-        acc[spare] = jnp.zeros((8, 128), jnp.float32)
+        lax.fori_loop(0, CORE, two_planes, 0)
+    for columns, ranges in OUTER_PASSES:
+        gram_pass(basis, acc, columns, ranges, CORE)
     by_pair = jnp.sum(acc[...], axis=1)
     ones = jnp.ones((8, 128), jnp.float32)
     gram[...] = exact_dot(ones, by_pair, ((1,), (1,)))[0:1]
@@ -445,61 +513,61 @@
         out[slab, 32] = flag
     weight = [
         (
-            jnp.broadcast_to(answer[0][k : k + 1], (8 * TILES, 128)),
-            jnp.broadcast_to(answer[1][k : k + 1], (8 * TILES, 128)),
+            jnp.broadcast_to(answer[0][k : k + 1], (8, 128)),
+            jnp.broadcast_to(answer[1][k : k + 1], (8, 128)),
         )
         for k in range(BASIS - 1)
     ]
 
-    def two_planes(first):
-        planes = []
-        for plane in (first, first + 1):
-            real = jnp.zeros((8 * TILES, 128), jnp.float32)
-            imag = jnp.zeros((8 * TILES, 128), jnp.float32)
+    def solve_plane(plane, goals):
+        for tile in range(TILES):
+            real = jnp.zeros((8, 128), jnp.float32)
+            imag = jnp.zeros((8, 128), jnp.float32)
             for k in range(BASIS - 1):
-                b_re, b_im = basis[k, 0, plane], basis[k, 1, plane]
+                b_re, b_im = basis[k, 0, plane, tile], basis[k, 1, plane, tile]
                 real = real + (weight[k][0] * b_re - weight[k][1] * b_im)
                 imag = imag + (weight[k][0] * b_im + weight[k][1] * b_re)
-            planes.append((real.reshape(TILES, 8, 128), imag.reshape(TILES, 8, 128)))
-        return planes
-
-    def put(slab, at, planes):
+            for slab, at in goals:
+                out[slab, at * TILES + tile] = real
+                out[slab, (4 + at) * TILES + tile] = imag
+
+    def middle(slab, _):
         for plane in range(2):
-            for part in range(2):
-                out[slab, pl.ds((part * 4 + at + plane) * TILES, TILES)] = planes[plane][part]
-
-    def middle(slab, _):
-        planes = two_planes(CORE - 1 + 2 * slab)
-        put(slab, 0, planes)
-        put(slab - 1, 2, planes)
+            solve_plane(CORE - 1 + 2 * slab + plane, ((slab, plane), (slab - 1, 2 + plane)))
         return 0
 
-    put(0, 0, two_planes(CORE - 1))
+    for plane in range(2):
+        solve_plane(CORE - 1 + plane, ((0, plane),))
+        solve_plane(CORE + OWN - 1 + plane, ((SYSTEMS - 1, 2 + plane),))
     lax.fori_loop(1, SYSTEMS, middle, 0)
-    put(SYSTEMS - 1, 2, two_planes(CORE - 1 + 2 * SYSTEMS))
-
-
-def fields_kernel(fields, forward, adjoint, terms):
+
+
+def fields_kernel(fields, forward, adjoint, terms, natural):
     half = SYSTEMS // 2
     for port in range(half):
         for part in range(2):
-            own = pl.ds((part * 4 + 1) * TILES, 2 * TILES)
-            forward[port, part] = fields[port, own]
-            adjoint[port, part] = fields[half + port, own]
+            for plane in range(2):
+                for tile in range(TILES):
+                    at = (part * 4 + 1 + plane) * TILES + tile
+                    forward[port, part, plane, rows_of(tile)] = fields[port, at]
+                    adjoint[port, part, plane, rows_of(tile)] = fields[half + port, at]
     for plane in range(4):
-        total = None
-        for port in range(half):
-            real, imag = pl.ds(plane * TILES, TILES), pl.ds((4 + plane) * TILES, TILES)
-            term = fields[port, real] * fields[half + port, real]
-            term = term - fields[port, imag] * fields[half + port, imag]
-            total = term if total is None else total + term
         for tile in range(TILES):
-            terms[tile, plane] = total[tile]
+            real, imag = plane * TILES + tile, (4 + plane) * TILES + tile
+            total = None
+            for port in range(half):
+                term = fields[port, real] * fields[half + port, real]
+                term = term - fields[port, imag] * fields[half + port, imag]
+                total = term if total is None else total + term
+            natural[plane, rows_of(tile)] = total
+    for share in range(4):
+        for plane in range(4):
+            terms[share, plane] = natural[plane, pl.ds(share * 8, 8)]
     flag = fields[0, 32]
     for system in range(1, SYSTEMS):
         flag = flag + fields[system, 32]
-    for tile in range(TILES):
-        terms[tile, 4] = flag
+    for share in range(4):
+        terms[share, 4] = flag
 
 
 def density_kernel(start, place, terms, dens, out, flag):
@@ -511,7 +579,7 @@
             total = total + terms[other, plane]
         gradient = -wave_sq * total
         where = place[0] * 2 + plane - 1
-        inside = (where >= start[0]) & (where < start[0] + 64)
+        inside = (where >= start[0]) & (where < start[0] + SYSTEMS * SYSTEMS)
         rows = dens[plane]
         moved = jnp.clip(rows - step_size * perm_span * gradient, 0.0, 1.0)
         rows = jnp.where(inside, moved, rows)
@@ -529,39 +597,71 @@
     flag[0] = jnp.max(spread)
 
 
+def copy_kernel(count, *refs):
+    sems = refs[-1]
+    arrays = refs[-1 - 2 * count : -1]
+    copies = [
+        pltpu.make_async_copy(arrays[at], arrays[count + at], sems.at[at]) for at in range(count)
+    ]
+    for copy in copies:
+        copy.start()
+    for copy in copies:
+        copy.wait()
+
+
+def row_major(mark, arrays, name):
+    count = len(arrays)
+    return call(
+        functools.partial(copy_kernel, count),
+        tuple(jax.ShapeDtypeStruct(array.shape, array.dtype) for array in arrays),
+        [SMEM] + [HBM] * count,
+        (HBM,) * count,
+        [pltpu.SemaphoreType.DMA((count,))],
+        name,
+    )(mark.reshape(1), *arrays)
+
+
 def on_device(background, absorb, density, profiles, adjoint_source, port_modes, design_start):
-    args = (background, absorb, density, profiles, adjoint_source, port_modes, design_start)
     slab = lax.axis_index("zslab")
     place = jnp.stack([slab, lax.axis_index("group")]).astype(jnp.int32)
     planes_of = [[z * SYSTEMS + l for l in range(SYSTEMS)] for z in range(SYSTEMS)]
     columns = [[z * SYSTEMS + l for z in range(SYSTEMS)] for l in range(SYSTEMS)]
-    tiles = (2, TILES, 8, 128)
     packed = call(
         pack_kernel,
         f32(SYSTEMS, BLOCK, 8, 128),
-        [SMEM, SMEM, SMEM, VMEM, VMEM, VMEM, ANY, ANY],
+        [SMEM, SMEM, SMEM, VMEM, VMEM, VMEM, HBM, HBM],
         VMEM,
-        [pltpu.SemaphoreType.DMA((SYSTEMS,))],
+        [
+            pltpu.VMEM((SYSTEMS,) + profiles.shape[1:], jnp.float32),
+            pltpu.SemaphoreType.DMA((SYSTEMS,)),
+        ],
         "pack",
-    )(
-        port_modes, design_start, place,
-        background.reshape(tiles), absorb.reshape(tiles), density.reshape(tiles),
-        profiles.reshape(-1, 16, 8, 128), adjoint_source.reshape(-1, 16, 8, 128),
-    )
+    )(port_modes, design_start, place, background, absorb, density, profiles, adjoint_source)
     block = lax.all_to_all(packed, "zslab", 0, 0, axis_index_groups=planes_of, tiled=True)
     count = SYSTEMS * SYSTEMS
     up = [(i, i + SYSTEMS) for i in range(count - SYSTEMS)]
     down = [(target, source) for source, target in up]
     low = lax.ppermute(block[SYSTEMS // 2 :], "zslab", up)
     high = lax.ppermute(block[: SYSTEMS // 2], "zslab", down)
+    inner = call(
+        inner_kernel,
+        (f32(SYSTEMS, 2, OWN, TILES, 8, 128), f32(2, OWN, TILES, 8, 128), f32(128, 8, 128)),
+        [VMEM],
+        (VMEM,) * 3,
+        (),
+        "inner",
+        10**8,
+    )(block)
+    plane = (TILES, 8, 128)
     basis, gram, dens = call(
-        basis_kernel,
-        (f32(BASIS, 2, WINDOW, 8 * TILES, 128), f32(1, 128), f32(4, 8, 128)),
-        [SMEM, VMEM, VMEM, VMEM],
+        outer_kernel,
+        (f32(BASIS, 2, WINDOW, *plane), f32(1, 128), f32(4, 8, 128)),
+        [SMEM] + [VMEM] * 6,
         (VMEM, VMEM, VMEM),
-        [pltpu.VMEM((2, WINDOW, 8 * TILES, 128), jnp.float32), pltpu.VMEM((128, 8, 128), jnp.float32)],
-        "basis",
-    )(place, block, low, high)
+        [pltpu.VMEM((2, WINDOW) + plane, jnp.float32), pltpu.VMEM((128, 8, 128), jnp.float32)],
+        "outer",
+        2 * 10**8,
+    )(place, block, low, high, *inner)
     grams = lax.all_to_all(
         jnp.broadcast_to(gram[None], (SYSTEMS, 1, 128)), "zslab", 0, 0,
         axis_index_groups=columns, tiled=True,
@@ -571,20 +671,27 @@
         combine_kernel, f32(SYSTEMS, 33, 8, 128), [VMEM, VMEM, VMEM, VMEM], VMEM, (), "combine"
     )(grams, jnp.asarray(pick), jnp.asarray(nudge), basis)
     fields = lax.all_to_all(solved, "zslab", 0, 0, axis_index_groups=planes_of, tiled=True)
-    half = (SYSTEMS // 2, 2, 2 * TILES, 8, 128)
+    half = f32(SYSTEMS // 2, 2, 2, 8 * TILES, 128)
     forward, adjoint, terms = call(
-        fields_kernel, (f32(*half), f32(*half), f32(4, 5, 8, 128)), [VMEM], (VMEM,) * 3, (), "fields"
+        fields_kernel,
+        (half, half, f32(4, 5, 8, 128)),
+        [VMEM],
+        (VMEM,) * 3,
+        [pltpu.VMEM((4, 8 * TILES, 128), jnp.float32)],
+        "fields",
     )(fields)
     terms = lax.all_to_all(terms, "group", 0, 0, tiled=True)
     new_density, flag = call(
         density_kernel, (f32(2, 8, 128), f32(1)), [SMEM, SMEM, VMEM, VMEM], (VMEM, SMEM), (), "density"
     )(design_start, place, terms, dens)
-    shape = (SYSTEMS // 2, 2, 2, 8 * TILES, 128)
-    state = (flag[0], forward.reshape(shape), adjoint.reshape(shape), new_density)
 
     def again(state):
-        return (jnp.zeros((), jnp.float32),) + iterate_on_device(*args)
-
+        held = (background, absorb, density, profiles, adjoint_source)
+        held = row_major(state[0], held, "arguments")
+        results = iterate_on_device(*held, port_modes, design_start)
+        return (jnp.zeros((), jnp.float32),) + tuple(row_major(state[0], results, "results"))
+
+    state = (flag[0], forward, adjoint, new_density)
     return lax.while_loop(lambda state: state[0] > 0.0, again, state)[1:]
 
 

time: 111 us -> 108 us (0.973)
  blocking collectives: 49.9 us -> 66.3 us
  waiting for transfers between devices: 14.3 us -> 4.78 us
  starting transfers between devices: 14.7 us -> 5.5 us
  local copies, waits for them, and re-layouts: 8.35 us -> 0.09 us
  Pallas kernels: 20.6 us -> 28.2 us
    all_to_all x0 -> x1, blocking collectives: none -> 14.1 us  [on_device(): terms = lax.all_to_all(terms, 'group', 0, 0, tiled=True)]
    all_to_all x1 -> x0, starting transfers between devices: 9.69 us -> none  [on_device(): terms = lax.all_to_all(terms, 'group', 0, 0, tiled=True)]
    pallas_call x2 -> x3, Pallas kernels: 15.9 us -> 23.2 us  [the longest x1 17.7 us: on_device(): call(outer_kernel, (f32(BASIS, 2, WINDOW, *plane), f32(1, 128), f32(4, 8,...]
    ppermute x1, waiting for transfers between devices: 8.23 us -> 0.9 us  [on_device(): low = lax.ppermute(block[SYSTEMS // 2:], 'zslab', up)]
    unnamed x20 -> x6, local copies, waits for them, and re-layouts: 5.34 us -> 0.01 us
    while x4 -> x0, local copies, waits for them, and re-layouts: 2.94 us -> none  [on_device(): return lax.while_loop(lambda state: state[0] > 0.0, again, state)[1:]]
    all_to_all x1, blocking collectives: 14.1 us -> 16.3 us  [on_device(): lax.all_to_all(jnp.broadcast_to(gram[None], (SYSTEMS, 1, 128)), 'zslab',...]
    all_to_all x1 -> x0, waiting for transfers between devices: 1.86 us -> none  [on_device(): terms = lax.all_to_all(terms, 'group', 0, 0, tiled=True)]
  transfers between devices with their start and end apart: 3 -> 2, of which waited for: 3 -> 2; matrix products, arithmetic and copies ran while one was open for 3% -> 0% of each run, Pallas kernels for 0% -> 4%
where the time goes in v2:
time: 108 us; the launch traced here: 107 us
  blocking collectives  66.3 us (61%)
  Pallas kernels  28.2 us (26%)
  starting transfers between devices  5.5 us (5%)
  waiting for transfers between devices  4.78 us (4%)
  between operations  1.54 us (1%)
    all_to_all x1, blocking collectives, on_device(): lax.all_to_all(packed, 'zslab', 0, 0, axis_index_groups=planes_of, tiled=...  21 us
    pallas_call x1, Pallas kernels, on_device(): call(outer_kernel, (f32(BASIS, 2, WINDOW, *plane), f32(1, 128), f32(4, 8,...  17.7 us
    all_to_all x1, blocking collectives, on_device(): lax.all_to_all(jnp.broadcast_to(gram[None], (SYSTEMS, 1, 128)), 'zslab',...  16.3 us
    all_to_all x1, blocking collectives, on_device(): lax.all_to_all(solved, 'zslab', 0, 0, axis_index_groups=planes_of, tiled=...  14.8 us
    all_to_all x1, blocking collectives, on_device(): terms = lax.all_to_all(terms, 'group', 0, 0, tiled=True)  14.1 us
    pallas_call x1, Pallas kernels, on_device(): call(inner_kernel, (f32(SYSTEMS, 2, OWN, TILES, 8, 128), f32(2, OWN, TILE...  4.64 us
    ppermute x1, starting transfers between devices, on_device(): low = lax.ppermute(block[SYSTEMS // 2:], 'zslab', up)  4.2 us
    ppermute x1, waiting for transfers between devices, on_device(): high = lax.ppermute(block[:SYSTEMS // 2], 'zslab', down)  3.88 us
  transfers between devices with their start and end apart: 2, of which 2 were waited for; matrix products, arithmetic and copies ran while one was open for 0% of the time, Pallas kernels for 4%

profile of v2, /device:TPU:1, one launch (start us, length us, event | category | flops | bytes accessed | tf_op | source)
XLA Modules:
  0.0 107.3 jit_solution(9768668436475628504)
XLA Ops:
  1.3 0.1 pad_add_fusion.place
  1.4 1.9 %pack.1 = f32[8,34,8,128]{3,2,1,0:T(8,128)S(1)} custom-call(s32[4]{0:T(128)} %modes.1, s32[1]{0:T(128)S(6)} %copy.32.start, s32[2]{0:T(128)S(1)} %pad_add_fusion.place, f32[2,32,128]{2,1,0:T(8,128)} %background.1, f32[2,32,128]{2,1,0:T(8,128)} %absorb.1, f32[2,32,128]{2,1,0:T(8,128)} %density.2, f32[6,2,2,32,128]{4,3,2,1,0:T(8,128)} %profiles.1, ...), custom_call_target="tpu_custom_call" | custom-call | bytes 1048576 | tf_op jit(solution)/shard_map/pack/pallas_call | solution.py:629
  3.3 21.0 %all_to_all.20.block = f32[8,34,8,128]{3,2,1,0:T(8,128)S(1)} all-to-all(f32[8,34,8,128]{3,2,1,0:T(8,128)S(1)} %pack.1), channel_id=1, replica_groups={{0,1,2,3,4,5,6,7},{8,9,10,11,12,13,14,15},{16,17,18,19,20,21,22,23},{24..., dimensions={0} | all-to-all | bytes 2228224 | tf_op jit(solution)/shard_map/all_to_all | solution.py:640
  24.3 0.1 fusion.55
  24.4 1.3 %collective-permute-start.19 = (f32[4,34,8,128]{3,2,1,0:T(8,128)S(1)}, f32[4,34,8,128]{3,2,1,0:T(8,128)S(1)}, u32[]{:S(2)}, u32[]{:S(2)}) collective-permute-start(f32[4,34,8,128]{3,2,1,0:T(8,128)S(1)} %get-tuple-element.301), channel_id=1, source_target_pairs={{8,0},{9,1},{10,2},{11,3},{12,4},{13,5},{14,6},{15,7},{16,8},{17,9... | collective-permute-start | bytes 1671176 | tf_op jit(solution)/shard_map/ppermute | solution.py:645
  25.7 4.2 %collective-permute-start.18 = (f32[4,34,8,128]{3,2,1,0:T(8,128)S(1)}, f32[4,34,8,128]{3,2,1,0:T(8,128)S(1)}, u32[]{:S(2)}, u32[]{:S(2)}) collective-permute-start(f32[4,34,8,128]{3,2,1,0:T(8,128)S(1)} %get-tuple-element.302), channel_id=1, source_target_pairs={{0,8},{1,9},{2,10},{3,11},{4,12},{5,13},{6,14},{7,15},{8,16},{9,17... | collective-permute-start | bytes 1671176 | tf_op jit(solution)/shard_map/ppermute | solution.py:644
  29.9 4.6 %inner.1 = (f32[8,2,16,4,8,128]{5,4,3,2,1,0:T(8,128)S(1)}, f32[2,16,4,8,128]{4,3,2,1,0:T(8,128)S(1)}, f32[128,8,128]{2,1,0:T(8,128)S(1)}) custom-call(f32[8,34,8,128]{3,2,1,0:T(8,128)S(1)} %all_to_all.20.block), custom_call_target="tpu_custom_call" | custom-call | flops 100000000 | bytes 1048576 | tf_op jit(solution)/shard_map/inner/pallas_call | solution.py:646
  34.6 3.9 %collective-permute-done.19.high = f32[4,34,8,128]{3,2,1,0:T(8,128)S(1)} collective-permute-done((f32[4,34,8,128]{3,2,1,0:T(8,128)S(1)}, f32[4,34,8,128]{3,2,1,0:T(8,128)S(1)}, u32[]{:S(2)}, u32[]{:S(2)}) %collective-permute-start.19) | collective-permute-done | bytes 557088 | tf_op jit(solution)/shard_map/ppermute | solution.py:645
  38.4 0.9 collective-permute-done.18.low
  39.3 0.0 copy-start
  39.3 0.0 copy-start.1
  39.3 17.7 %outer.1 = (f32[9,2,32,4,8,128]{5,4,3,2,1,0:T(8,128)S(1)}, f32[1,128]{1,0:T(1,128)S(1)}, f32[4,8,128]{2,1,0:T(8,128)S(1)}) custom-call(s32[2]{0:T(128)S(1)} %pad_add_fusion.place, f32[8,34,8,128]{3,2,1,0:T(8,128)S(1)} %all_to_all.20.block, f32[4,34,8,128]{3,2,1,0:T(8,128)S(1)} %collective-permute-done.18.low, ...), custom_call_target="tpu_custom_call" | custom-call | flops 200000000 | bytes 1048576 | tf_op jit(solution)/shard_map/outer/pallas_call | solution.py:656
  57.1 16.3 %all_to_all.21.grams = f32[8,1,128]{2,1,0:T(1,128)S(1)} all-to-all(f32[8,1,128]{2,1,0:T(1,128)S(1)} %broadcast_in_dim.18), channel_id=1, replica_groups={{0,8,16,24,32,40,48,56},{1,9,17,25,33,41,49,57},{2,10,18,26,34,42,50,58..., dimensions={0} | all-to-all | bytes 8192 | tf_op jit(solution)/shard_map/all_to_all | solution.py:665
  73.4 0.0 copy-done
  73.4 0.0 copy-done.1
  73.4 1.8 %combine.1 = f32[8,33,8,128]{3,2,1,0:T(8,128)S(1)} custom-call(f32[8,1,128]{2,1,0:T(1,128)S(1)} %all_to_all.21.grams, f32[864,128]{1,0:T(8,128)S(1)} %copy-done, f32[288,128]{1,0:T(8,128)S(1)} %copy-done.1, f32[9,2,32,4,8,128]{5,4,3,2,1,0:T(8,128)S(1)} %get-tuple-element.82.basis), custom_call_target="tpu_custom_call" | custom-call | bytes 1048576 | tf_op jit(solution)/shard_map/combine/pallas_call | solution.py:670
  75.2 0.0 copy-start.22
  75.2 14.8 %all_to_all.22.fields = f32[8,33,8,128]{3,2,1,0:T(8,128)S(1)} all-to-all(f32[8,33,8,128]{3,2,1,0:T(8,128)S(1)} %combine.1), channel_id=1, replica_groups={{0,1,2,3,4,5,6,7},{8,9,10,11,12,13,14,15},{16,17,18,19,20,21,22,23},{24..., dimensions={0} | all-to-all | bytes 2162688 | tf_op jit(solution)/shard_map/all_to_all | solution.py:673
  90.1 0.8 fields.1
  90.9 14.1 %all_to_all.23.terms = f32[4,5,8,128]{3,2,1,0:T(8,128)S(1)} all-to-all(f32[4,5,8,128]{3,2,1,0:T(8,128)S(1)} %get-tuple-element.83), channel_id=1, replica_groups=mesh['group'=4,'zslab'=64] {'group'}, dimensions={0} | all-to-all | bytes 163840 | tf_op jit(solution)/shard_map/all_to_all | solution.py:683
  105.0 1.2 %density.3 = (f32[2,8,128]{2,1,0:T(8,128)}, f32[1]{0:T(128)}) custom-call(s32[1]{0:T(128)S(6)} %copy.32.start, s32[2]{0:T(128)S(1)} %pad_add_fusion.place, f32[4,5,8,128]{3,2,1,0:T(8,128)S(1)} %all_to_all.23.terms, f32[4,8,128]{2,1,0:T(8,128)S(1)} %get-tuple-element.84.dens), custom_call_target="tpu_custom_call" | custom-call | bytes 1048576 | tf_op jit(solution)/shard_map/density/pallas_call | solution.py:684
  106.3 0.0 copy-done.22
  106.3 0.9 while.13
  (1 shorter events, 0.0 us)
Async XLA Ops:
  24.4 14.0 %collective-permute-start.19 = (f32[4,34,8,128]{3,2,1,0:T(8,128)S(1)}, f32[4,34,8,128]{3,2,1,0:T(8,128)S(1)}, u32[]{:S(2)}, u32[]{:S(2)}) collective-permute-start(f32[4,34,8,128]{3,2,1,0:T(8,128)S(1)} %get-tuple-element.301), channel_id=1, source_target_pairs={{8,0},{9,1},{10,2},{11,3},{12,4},{13,5},{14,6},{15,7},{16,8},{17,9... | collective-permute-start | bytes 1671176 | tf_op jit(solution)/shard_map/ppermute | solution.py:645
  25.7 13.6 %collective-permute-start.18 = (f32[4,34,8,128]{3,2,1,0:T(8,128)S(1)}, f32[4,34,8,128]{3,2,1,0:T(8,128)S(1)}, u32[]{:S(2)}, u32[]{:S(2)}) collective-permute-start(f32[4,34,8,128]{3,2,1,0:T(8,128)S(1)} %get-tuple-element.302), channel_id=1, source_target_pairs={{0,8},{1,9},{2,10},{3,11},{4,12},{5,13},{6,14},{7,15},{8,16},{9,17... | collective-permute-start | bytes 1671176 | tf_op jit(solution)/shard_map/ppermute | solution.py:644
  39.3 34.1 %copy-start = (f32[864,128]{1,0:T(8,128)S(1)}, f32[864,128]{1,0:T(8,128)}, u32[]{:S(2)}) copy-start(f32[864,128]{1,0:T(8,128)} %constant.66.clone.pick) | copy-start | bytes 1327108
  39.3 34.1 %copy-start.1 = (f32[288,128]{1,0:T(8,128)S(1)}, f32[288,128]{1,0:T(8,128)}, u32[]{:S(2)}) copy-start(f32[288,128]{1,0:T(8,128)} %constant.67.clone.nudge) | copy-start | bytes 442372
  75.2 31.1 %copy-start.22 = (f32[2,32,128]{2,1,0:T(8,128)S(1)}, f32[2,32,128]{2,1,0:T(8,128)}, u32[]{:S(2)}) copy-start(f32[2,32,128]{2,1,0:T(8,128)} %background.1) | copy-start | bytes 98308

commit v3 on v2

--- a/solution.py
+++ b/solution.py
@@ -397,7 +397,8 @@
     sums = tuple(acc[at] for at in places)
     for first, last in ranges:
         sums = lax.fori_loop(
-            0, (last - first) * TILES, functools.partial(position, first=first), sums
+            0, (last - first) * TILES, functools.partial(position, first=first), sums,
+            unroll=TILES,
         )
     for at, value in zip(places, sums):
         acc[at] = value
@@ -421,7 +422,9 @@
             stencil.step(basis, diag, level, at, THIRD)
             return 0
 
-        lax.fori_loop(level + 1, OWN - 1 - level, plane_step, 0, unroll=2)
+        lax.fori_loop(
+            level + 1, OWN - 1 - level, plane_step, 0, unroll=OWN - 2 - 2 * level
+        )
     acc[...] = jnp.zeros_like(acc)
     for columns, ranges in INNER_PASSES:
         gram_pass(basis, acc, columns, ranges, 0)
@@ -491,7 +494,7 @@
             )
             return 0
 
-        lax.fori_loop(0, CORE, two_planes, 0)
+        lax.fori_loop(0, CORE, two_planes, 0, unroll=CORE)
     for columns, ranges in OUTER_PASSES:
         gram_pass(basis, acc, columns, ranges, CORE)
     by_pair = jnp.sum(acc[...], axis=1)

time: 108 us -> 96.3 us (0.89)
  Pallas kernels: 28.2 us -> 14.3 us
  waiting for transfers between devices: 4.78 us -> 7.26 us
    pallas_call x1, Pallas kernels: 17.7 us -> 6.28 us  [on_device(): call(outer_kernel, (f32(BASIS, 2, WINDOW, *plane), f32(1, 128), f32(4, 8,...]
    ppermute x1, waiting for transfers between devices: 3.88 us -> 6.36 us  [on_device(): high = lax.ppermute(block[:SYSTEMS // 2], 'zslab', down)]
    pallas_call x1, Pallas kernels: 4.64 us -> 2.17 us  [on_device(): call(inner_kernel, (f32(SYSTEMS, 2, OWN, TILES, 8, 128), f32(2, OWN, TILE...]
  transfers between devices with their start and end apart: 2 -> 2, of which waited for: 2 -> 2; matrix products, arithmetic and copies ran while one was open for 0% -> 0% of each run, Pallas kernels for 4% -> 2%
where the time goes in v3:
time: 96.3 us; the launch traced here: 95.9 us
  blocking collectives  66.3 us (69%)
  Pallas kernels  14.3 us (15%)
  waiting for transfers between devices  7.26 us (8%)
  starting transfers between devices  5.5 us (6%)
  between operations  1.53 us (2%)
    all_to_all x1, blocking collectives, on_device(): lax.all_to_all(packed, 'zslab', 0, 0, axis_index_groups=planes_of, tiled=...  21 us
    all_to_all x1, blocking collectives, on_device(): lax.all_to_all(jnp.broadcast_to(gram[None], (SYSTEMS, 1, 128)), 'zslab',...  16.3 us
    all_to_all x1, blocking collectives, on_device(): lax.all_to_all(solved, 'zslab', 0, 0, axis_index_groups=planes_of, tiled=...  14.8 us
    all_to_all x1, blocking collectives, on_device(): terms = lax.all_to_all(terms, 'group', 0, 0, tiled=True)  14.1 us
    ppermute x1, waiting for transfers between devices, on_device(): high = lax.ppermute(block[:SYSTEMS // 2], 'zslab', down)  6.36 us
    pallas_call x1, Pallas kernels, on_device(): call(outer_kernel, (f32(BASIS, 2, WINDOW, *plane), f32(1, 128), f32(4, 8,...  6.28 us
    ppermute x1, starting transfers between devices, on_device(): low = lax.ppermute(block[SYSTEMS // 2:], 'zslab', up)  4.2 us
    pallas_call x1, Pallas kernels, on_device(): call(inner_kernel, (f32(SYSTEMS, 2, OWN, TILES, 8, 128), f32(2, OWN, TILE...  2.17 us
  transfers between devices with their start and end apart: 2, of which 2 were waited for; matrix products, arithmetic and copies ran while one was open for 0% of the time, Pallas kernels for 2%

profile of v3, /device:TPU:1, one launch (start us, length us, event | category | flops | bytes accessed | tf_op | source)
XLA Modules:
  0.0 95.9 jit_solution(2057225597331207631)
XLA Ops:
  1.3 0.1 pad_add_fusion.place
  1.4 1.9 %pack.1 = f32[8,34,8,128]{3,2,1,0:T(8,128)S(1)} custom-call(s32[4]{0:T(128)} %modes.1, s32[1]{0:T(128)S(6)} %copy.32.start, s32[2]{0:T(128)S(1)} %pad_add_fusion.place, f32[2,32,128]{2,1,0:T(8,128)} %background.1, f32[2,32,128]{2,1,0:T(8,128)} %absorb.1, f32[2,32,128]{2,1,0:T(8,128)} %density.2, f32[6,2,2,32,128]{4,3,2,1,0:T(8,128)} %profiles.1, ...), custom_call_target="tpu_custom_call" | custom-call | bytes 1048576 | tf_op jit(solution)/shard_map/pack/pallas_call | solution.py:632
  3.3 21.0 %all_to_all.20.block = f32[8,34,8,128]{3,2,1,0:T(8,128)S(1)} all-to-all(f32[8,34,8,128]{3,2,1,0:T(8,128)S(1)} %pack.1), channel_id=1, replica_groups={{0,1,2,3,4,5,6,7},{8,9,10,11,12,13,14,15},{16,17,18,19,20,21,22,23},{24..., dimensions={0} | all-to-all | bytes 2228224 | tf_op jit(solution)/shard_map/all_to_all | solution.py:643
  24.3 0.1 fusion.55
  24.4 1.3 %collective-permute-start.19 = (f32[4,34,8,128]{3,2,1,0:T(8,128)S(1)}, f32[4,34,8,128]{3,2,1,0:T(8,128)S(1)}, u32[]{:S(2)}, u32[]{:S(2)}) collective-permute-start(f32[4,34,8,128]{3,2,1,0:T(8,128)S(1)} %get-tuple-element.301), channel_id=1, source_target_pairs={{8,0},{9,1},{10,2},{11,3},{12,4},{13,5},{14,6},{15,7},{16,8},{17,9... | collective-permute-start | bytes 1671176 | tf_op jit(solution)/shard_map/ppermute | solution.py:648
  25.7 4.2 %collective-permute-start.18 = (f32[4,34,8,128]{3,2,1,0:T(8,128)S(1)}, f32[4,34,8,128]{3,2,1,0:T(8,128)S(1)}, u32[]{:S(2)}, u32[]{:S(2)}) collective-permute-start(f32[4,34,8,128]{3,2,1,0:T(8,128)S(1)} %get-tuple-element.302), channel_id=1, source_target_pairs={{0,8},{1,9},{2,10},{3,11},{4,12},{5,13},{6,14},{7,15},{8,16},{9,17... | collective-permute-start | bytes 1671176 | tf_op jit(solution)/shard_map/ppermute | solution.py:647
  29.9 2.2 %inner.1 = (f32[8,2,16,4,8,128]{5,4,3,2,1,0:T(8,128)S(1)}, f32[2,16,4,8,128]{4,3,2,1,0:T(8,128)S(1)}, f32[128,8,128]{2,1,0:T(8,128)S(1)}) custom-call(f32[8,34,8,128]{3,2,1,0:T(8,128)S(1)} %all_to_all.20.block), custom_call_target="tpu_custom_call" | custom-call | flops 100000000 | bytes 1048576 | tf_op jit(solution)/shard_map/inner/pallas_call | solution.py:649
  32.1 6.4 %collective-permute-done.19.high = f32[4,34,8,128]{3,2,1,0:T(8,128)S(1)} collective-permute-done((f32[4,34,8,128]{3,2,1,0:T(8,128)S(1)}, f32[4,34,8,128]{3,2,1,0:T(8,128)S(1)}, u32[]{:S(2)}, u32[]{:S(2)}) %collective-permute-start.19) | collective-permute-done | bytes 557088 | tf_op jit(solution)/shard_map/ppermute | solution.py:648
  38.4 0.9 collective-permute-done.18.low
  39.3 0.0 copy-start
  39.3 0.0 copy-start.1
  39.3 6.3 %outer.1 = (f32[9,2,32,4,8,128]{5,4,3,2,1,0:T(8,128)S(1)}, f32[1,128]{1,0:T(1,128)S(1)}, f32[4,8,128]{2,1,0:T(8,128)S(1)}) custom-call(s32[2]{0:T(128)S(1)} %pad_add_fusion.place, f32[8,34,8,128]{3,2,1,0:T(8,128)S(1)} %all_to_all.20.block, f32[4,34,8,128]{3,2,1,0:T(8,128)S(1)} %collective-permute-done.18.low, ...), custom_call_target="tpu_custom_call" | custom-call | flops 200000000 | bytes 1048576 | tf_op jit(solution)/shard_map/outer/pallas_call | solution.py:659
  45.6 16.3 %all_to_all.21.grams = f32[8,1,128]{2,1,0:T(1,128)S(1)} all-to-all(f32[8,1,128]{2,1,0:T(1,128)S(1)} %broadcast_in_dim.18), channel_id=1, replica_groups={{0,8,16,24,32,40,48,56},{1,9,17,25,33,41,49,57},{2,10,18,26,34,42,50,58..., dimensions={0} | all-to-all | bytes 8192 | tf_op jit(solution)/shard_map/all_to_all | solution.py:668
  61.9 0.0 copy-done
  61.9 0.0 copy-done.1
  61.9 1.8 %combine.1 = f32[8,33,8,128]{3,2,1,0:T(8,128)S(1)} custom-call(f32[8,1,128]{2,1,0:T(1,128)S(1)} %all_to_all.21.grams, f32[864,128]{1,0:T(8,128)S(1)} %copy-done, f32[288,128]{1,0:T(8,128)S(1)} %copy-done.1, f32[9,2,32,4,8,128]{5,4,3,2,1,0:T(8,128)S(1)} %get-tuple-element.82.basis), custom_call_target="tpu_custom_call" | custom-call | bytes 1048576 | tf_op jit(solution)/shard_map/combine/pallas_call | solution.py:673
  63.8 0.0 copy-start.22
  63.8 14.8 %all_to_all.22.fields = f32[8,33,8,128]{3,2,1,0:T(8,128)S(1)} all-to-all(f32[8,33,8,128]{3,2,1,0:T(8,128)S(1)} %combine.1), channel_id=1, replica_groups={{0,1,2,3,4,5,6,7},{8,9,10,11,12,13,14,15},{16,17,18,19,20,21,22,23},{24..., dimensions={0} | all-to-all | bytes 2162688 | tf_op jit(solution)/shard_map/all_to_all | solution.py:676
  78.6 0.8 fields.1
  79.5 14.1 %all_to_all.23.terms = f32[4,5,8,128]{3,2,1,0:T(8,128)S(1)} all-to-all(f32[4,5,8,128]{3,2,1,0:T(8,128)S(1)} %get-tuple-element.83), channel_id=1, replica_groups=mesh['group'=4,'zslab'=64] {'group'}, dimensions={0} | all-to-all | bytes 163840 | tf_op jit(solution)/shard_map/all_to_all | solution.py:686
  93.6 1.2 %density.3 = (f32[2,8,128]{2,1,0:T(8,128)}, f32[1]{0:T(128)}) custom-call(s32[1]{0:T(128)S(6)} %copy.32.start, s32[2]{0:T(128)S(1)} %pad_add_fusion.place, f32[4,5,8,128]{3,2,1,0:T(8,128)S(1)} %all_to_all.23.terms, f32[4,8,128]{2,1,0:T(8,128)S(1)} %get-tuple-element.84.dens), custom_call_target="tpu_custom_call" | custom-call | bytes 1048576 | tf_op jit(solution)/shard_map/density/pallas_call | solution.py:687
  94.8 0.0 copy-done.22
  94.8 0.9 while.13
  (1 shorter events, 0.0 us)
Async XLA Ops:
  24.4 14.0 %collective-permute-start.19 = (f32[4,34,8,128]{3,2,1,0:T(8,128)S(1)}, f32[4,34,8,128]{3,2,1,0:T(8,128)S(1)}, u32[]{:S(2)}, u32[]{:S(2)}) collective-permute-start(f32[4,34,8,128]{3,2,1,0:T(8,128)S(1)} %get-tuple-element.301), channel_id=1, source_target_pairs={{8,0},{9,1},{10,2},{11,3},{12,4},{13,5},{14,6},{15,7},{16,8},{17,9... | collective-permute-start | bytes 1671176 | tf_op jit(solution)/shard_map/ppermute | solution.py:648
  25.7 13.6 %collective-permute-start.18 = (f32[4,34,8,128]{3,2,1,0:T(8,128)S(1)}, f32[4,34,8,128]{3,2,1,0:T(8,128)S(1)}, u32[]{:S(2)}, u32[]{:S(2)}) collective-permute-start(f32[4,34,8,128]{3,2,1,0:T(8,128)S(1)} %get-tuple-element.302), channel_id=1, source_target_pairs={{0,8},{1,9},{2,10},{3,11},{4,12},{5,13},{6,14},{7,15},{8,16},{9,17... | collective-permute-start | bytes 1671176 | tf_op jit(solution)/shard_map/ppermute | solution.py:647
  39.3 22.6 %copy-start = (f32[864,128]{1,0:T(8,128)S(1)}, f32[864,128]{1,0:T(8,128)}, u32[]{:S(2)}) copy-start(f32[864,128]{1,0:T(8,128)} %constant.66.clone.pick) | copy-start | bytes 1327108
  39.3 22.6 %copy-start.1 = (f32[288,128]{1,0:T(8,128)S(1)}, f32[288,128]{1,0:T(8,128)}, u32[]{:S(2)}) copy-start(f32[288,128]{1,0:T(8,128)} %constant.67.clone.nudge) | copy-start | bytes 442372
  63.8 31.1 %copy-start.22 = (f32[2,32,128]{2,1,0:T(8,128)S(1)}, f32[2,32,128]{2,1,0:T(8,128)}, u32[]{:S(2)}) copy-start(f32[2,32,128]{2,1,0:T(8,128)} %background.1) | copy-start | bytes 98308

commit v4 on v3

--- a/solution.py
+++ b/solution.py
@@ -545,7 +545,7 @@
     lax.fori_loop(1, SYSTEMS, middle, 0)
 
 
-def fields_kernel(fields, forward, adjoint, terms, natural):
+def fields_kernel(place, fields, forward, adjoint, keep, give, natural):
     half = SYSTEMS // 2
     for port in range(half):
         for part in range(2):
@@ -563,24 +563,30 @@
                 term = term - fields[port, imag] * fields[half + port, imag]
                 total = term if total is None else total + term
             natural[plane, rows_of(tile)] = total
-    for share in range(4):
-        for plane in range(4):
-            terms[share, plane] = natural[plane, pl.ds(share * 8, 8)]
     flag = fields[0, 32]
     for system in range(1, SYSTEMS):
         flag = flag + fields[system, 32]
-    for share in range(4):
-        terms[share, 4] = flag
-
-
-def density_kernel(start, place, terms, dens, out, flag):
+    core = place[1] % 2
+    for out, side in ((keep, core), (give, 1 - core)):
+        for pair in range(2):
+            rows = pl.ds(pl.multiple_of((2 * pair + side) * 8, 8), 8)
+            for plane in range(4):
+                out[pair, plane] = natural[plane, rows]
+            out[pair, 4] = flag
+
+
+def pair_kernel(place, mine, other, keep, give):
+    own = place[1] // 2
+    for at in range(5):
+        keep[at] = mine[own, at] + other[own, at]
+        give[at] = mine[1 - own, at] + other[1 - own, at]
+
+
+def density_kernel(start, place, mine, other, dens, out, flag):
     lane = lax.broadcasted_iota(jnp.int32, (8, 128), 1)
     updated = []
     for plane in range(4):
-        total = terms[0, plane]
-        for other in range(1, 4):
-            total = total + terms[other, plane]
-        gradient = -wave_sq * total
+        gradient = -wave_sq * (mine[plane] + other[plane])
         where = place[0] * 2 + plane - 1
         inside = (where >= start[0]) & (where < start[0] + SYSTEMS * SYSTEMS)
         rows = dens[plane]
@@ -596,8 +602,7 @@
         edge = float(np.tanh(sharpness * threshold))
         other_edge = float(np.tanh(sharpness * (1.0 - threshold)))
         out[plane] = (edge + jnp.tanh(sharpness * (filtered - threshold))) / (edge + other_edge)
-    spread = terms[0, 4] + terms[1, 4] + terms[2, 4] + terms[3, 4]
-    flag[0] = jnp.max(spread)
+    flag[0] = jnp.max(mine[4] + other[4])
 
 
 def copy_kernel(count, *refs):
@@ -675,18 +680,27 @@
     )(grams, jnp.asarray(pick), jnp.asarray(nudge), basis)
     fields = lax.all_to_all(solved, "zslab", 0, 0, axis_index_groups=planes_of, tiled=True)
     half = f32(SYSTEMS // 2, 2, 2, 8 * TILES, 128)
-    forward, adjoint, terms = call(
+    forward, adjoint, keep, give = call(
         fields_kernel,
-        (half, half, f32(4, 5, 8, 128)),
-        [VMEM],
-        (VMEM,) * 3,
+        (half, half, f32(2, 5, 8, 128), f32(2, 5, 8, 128)),
+        [SMEM, VMEM],
+        (VMEM,) * 4,
         [pltpu.VMEM((4, 8 * TILES, 128), jnp.float32)],
         "fields",
-    )(fields)
-    terms = lax.all_to_all(terms, "group", 0, 0, tiled=True)
+    )(place, fields)
+    got = lax.ppermute(give, "group", [(i, i ^ 1) for i in range(4)])
+    keep, give = call(
+        pair_kernel, (f32(5, 8, 128), f32(5, 8, 128)), [SMEM, VMEM, VMEM], (VMEM, VMEM), (), "pair"
+    )(place, keep, got)
+    got = lax.ppermute(give, "group", [(i, i ^ 2) for i in range(4)])
     new_density, flag = call(
-        density_kernel, (f32(2, 8, 128), f32(1)), [SMEM, SMEM, VMEM, VMEM], (VMEM, SMEM), (), "density"
-    )(design_start, place, terms, dens)
+        density_kernel,
+        (f32(2, 8, 128), f32(1)),
+        [SMEM, SMEM, VMEM, VMEM, VMEM],
+        (VMEM, SMEM),
+        (),
+        "density",
+    )(design_start, place, keep, got, dens)
 
     def again(state):
         held = (background, absorb, density, profiles, adjoint_source)

time: 96.3 us -> 93.9 us (0.975)
  blocking collectives: 66.3 us -> 52.2 us
  starting transfers between devices: 5.5 us -> 13.5 us
  waiting for transfers between devices: 7.26 us -> 9.82 us
  Pallas kernels: 14.3 us -> 15.4 us
    all_to_all x1 -> x0, blocking collectives: 14.1 us -> none  [on_device(): terms = lax.all_to_all(terms, 'group', 0, 0, tiled=True)]
    ppermute x0 -> x2, starting transfers between devices: none -> 8.04 us  [the longest x1 5.51 us: on_device(): got = lax.ppermute(give, 'group', [(i, i ^ 1) for i in range(4)])]
    ppermute x0 -> x2, waiting for transfers between devices: none -> 2.56 us  [the longest x1 1.69 us: on_device(): got = lax.ppermute(give, 'group', [(i, i ^ 2) for i in range(4)])]
    pallas_call x2 -> x3, Pallas kernels: 2.09 us -> 3.19 us  [the longest x1 1.39 us: on_device(): call(fields_kernel, (half, half, f32(2, 5, 8, 128), f32(2, 5, 8, 128)), [...]
  transfers between devices with their start and end apart: 2 -> 4, of which waited for: 2 -> 4; matrix products, arithmetic and copies ran while one was open for 0% -> 0% of each run, Pallas kernels for 2% -> 2%
where the time goes in v4:
time: 93.9 us; the launch traced here: 93.5 us
  blocking collectives  52.2 us (56%)
  Pallas kernels  15.4 us (16%)
  starting transfers between devices  13.5 us (14%)
  waiting for transfers between devices  9.82 us (10%)
  between operations  1.54 us (2%)
    all_to_all x1, blocking collectives, on_device(): lax.all_to_all(packed, 'zslab', 0, 0, axis_index_groups=planes_of, tiled=...  21 us
    all_to_all x1, blocking collectives, on_device(): lax.all_to_all(jnp.broadcast_to(gram[None], (SYSTEMS, 1, 128)), 'zslab',...  16.3 us
    all_to_all x1, blocking collectives, on_device(): lax.all_to_all(solved, 'zslab', 0, 0, axis_index_groups=planes_of, tiled=...  14.8 us
    ppermute x1, waiting for transfers between devices, on_device(): high = lax.ppermute(block[:SYSTEMS // 2], 'zslab', down)  6.36 us
    pallas_call x1, Pallas kernels, on_device(): call(outer_kernel, (f32(BASIS, 2, WINDOW, *plane), f32(1, 128), f32(4, 8,...  6.28 us
    ppermute x1, starting transfers between devices, on_device(): got = lax.ppermute(give, 'group', [(i, i ^ 1) for i in range(4)])  5.51 us
    ppermute x1, starting transfers between devices, on_device(): low = lax.ppermute(block[SYSTEMS // 2:], 'zslab', up)  4.2 us
    ppermute x1, starting transfers between devices, on_device(): got = lax.ppermute(give, 'group', [(i, i ^ 2) for i in range(4)])  2.53 us
  transfers between devices with their start and end apart: 4, of which 4 were waited for; matrix products, arithmetic and copies ran while one was open for 0% of the time, Pallas kernels for 2%

profile of v4, /device:TPU:1, one launch (start us, length us, event | category | flops | bytes accessed | tf_op | source)
XLA Modules:
  0.0 93.5 jit_solution(10277827597979886307)
XLA Ops:
  1.3 0.1 pad_add_fusion.place
  1.4 1.9 %pack.1 = f32[8,34,8,128]{3,2,1,0:T(8,128)S(1)} custom-call(s32[4]{0:T(128)} %modes.1, s32[1]{0:T(128)S(6)} %copy.32.start, s32[2]{0:T(128)S(1)} %pad_add_fusion.place, f32[2,32,128]{2,1,0:T(8,128)} %background.1, f32[2,32,128]{2,1,0:T(8,128)} %absorb.1, f32[2,32,128]{2,1,0:T(8,128)} %density.2, f32[6,2,2,32,128]{4,3,2,1,0:T(8,128)} %profiles.1, ...), custom_call_target="tpu_custom_call" | custom-call | bytes 1048576 | tf_op jit(solution)/shard_map/pack/pallas_call | solution.py:637
  3.3 21.0 %all_to_all.15.block = f32[8,34,8,128]{3,2,1,0:T(8,128)S(1)} all-to-all(f32[8,34,8,128]{3,2,1,0:T(8,128)S(1)} %pack.1), channel_id=1, replica_groups={{0,1,2,3,4,5,6,7},{8,9,10,11,12,13,14,15},{16,17,18,19,20,21,22,23},{24..., dimensions={0} | all-to-all | bytes 2228224 | tf_op jit(solution)/shard_map/all_to_all | solution.py:648
  24.3 0.1 fusion.55
  24.4 1.3 %collective-permute-start.19 = (f32[4,34,8,128]{3,2,1,0:T(8,128)S(1)}, f32[4,34,8,128]{3,2,1,0:T(8,128)S(1)}, u32[]{:S(2)}, u32[]{:S(2)}) collective-permute-start(f32[4,34,8,128]{3,2,1,0:T(8,128)S(1)} %get-tuple-element.307), channel_id=1, source_target_pairs={{8,0},{9,1},{10,2},{11,3},{12,4},{13,5},{14,6},{15,7},{16,8},{17,9... | collective-permute-start | bytes 1671176 | tf_op jit(solution)/shard_map/ppermute | solution.py:653
  25.7 4.2 %collective-permute-start.18 = (f32[4,34,8,128]{3,2,1,0:T(8,128)S(1)}, f32[4,34,8,128]{3,2,1,0:T(8,128)S(1)}, u32[]{:S(2)}, u32[]{:S(2)}) collective-permute-start(f32[4,34,8,128]{3,2,1,0:T(8,128)S(1)} %get-tuple-element.308), channel_id=1, source_target_pairs={{0,8},{1,9},{2,10},{3,11},{4,12},{5,13},{6,14},{7,15},{8,16},{9,17... | collective-permute-start | bytes 1671176 | tf_op jit(solution)/shard_map/ppermute | solution.py:652
  29.9 2.2 %inner.1 = (f32[8,2,16,4,8,128]{5,4,3,2,1,0:T(8,128)S(1)}, f32[2,16,4,8,128]{4,3,2,1,0:T(8,128)S(1)}, f32[128,8,128]{2,1,0:T(8,128)S(1)}) custom-call(f32[8,34,8,128]{3,2,1,0:T(8,128)S(1)} %all_to_all.15.block), custom_call_target="tpu_custom_call" | custom-call | flops 100000000 | bytes 1048576 | tf_op jit(solution)/shard_map/inner/pallas_call | solution.py:654
  32.1 6.4 %collective-permute-done.19.high = f32[4,34,8,128]{3,2,1,0:T(8,128)S(1)} collective-permute-done((f32[4,34,8,128]{3,2,1,0:T(8,128)S(1)}, f32[4,34,8,128]{3,2,1,0:T(8,128)S(1)}, u32[]{:S(2)}, u32[]{:S(2)}) %collective-permute-start.19) | collective-permute-done | bytes 557088 | tf_op jit(solution)/shard_map/ppermute | solution.py:653
  38.4 0.9 collective-permute-done.18.low
  39.3 6.3 %outer.1 = (f32[9,2,32,4,8,128]{5,4,3,2,1,0:T(8,128)S(1)}, f32[1,128]{1,0:T(1,128)S(1)}, f32[4,8,128]{2,1,0:T(8,128)S(1)}) custom-call(s32[2]{0:T(128)S(1)} %pad_add_fusion.place, f32[8,34,8,128]{3,2,1,0:T(8,128)S(1)} %all_to_all.15.block, f32[4,34,8,128]{3,2,1,0:T(8,128)S(1)} %collective-permute-done.18.low, ...), custom_call_target="tpu_custom_call" | custom-call | flops 200000000 | bytes 1048576 | tf_op jit(solution)/shard_map/outer/pallas_call | solution.py:664
  45.6 16.3 %all_to_all.16.grams = f32[8,1,128]{2,1,0:T(1,128)S(1)} all-to-all(f32[8,1,128]{2,1,0:T(1,128)S(1)} %broadcast_in_dim.18), channel_id=1, replica_groups={{0,8,16,24,32,40,48,56},{1,9,17,25,33,41,49,57},{2,10,18,26,34,42,50,58..., dimensions={0} | all-to-all | bytes 8192 | tf_op jit(solution)/shard_map/all_to_all | solution.py:673
  61.9 0.0 copy-done
  61.9 0.0 copy-done.1
  61.9 1.8 %combine.1 = f32[8,33,8,128]{3,2,1,0:T(8,128)S(1)} custom-call(f32[8,1,128]{2,1,0:T(1,128)S(1)} %all_to_all.16.grams, f32[864,128]{1,0:T(8,128)S(1)} %copy-done, f32[288,128]{1,0:T(8,128)S(1)} %copy-done.1, f32[9,2,32,4,8,128]{5,4,3,2,1,0:T(8,128)S(1)} %get-tuple-element.85.basis), custom_call_target="tpu_custom_call" | custom-call | bytes 1048576 | tf_op jit(solution)/shard_map/combine/pallas_call | solution.py:678
  63.8 0.0 copy-start.22
  63.8 14.8 %all_to_all.17.fields = f32[8,33,8,128]{3,2,1,0:T(8,128)S(1)} all-to-all(f32[8,33,8,128]{3,2,1,0:T(8,128)S(1)} %combine.1), channel_id=1, replica_groups={{0,1,2,3,4,5,6,7},{8,9,10,11,12,13,14,15},{16,17,18,19,20,21,22,23},{24..., dimensions={0} | all-to-all | bytes 2162688 | tf_op jit(solution)/shard_map/all_to_all | solution.py:681
  78.6 1.4 %fields.1 = (f32[4,2,2,32,128]{4,3,2,1,0:T(8,128)}, f32[4,2,2,32,128]{4,3,2,1,0:T(8,128)}, f32[2,5,8,128]{3,2,1,0:T(8,128)S(1)}, f32[2,5,8,128]{3,2,1,0:T(8,128)S(1)}) custom-call(s32[2]{0:T(128)S(1)} %pad_add_fusion.place, f32[8,33,8,128]{3,2,1,0:T(8,128)S(1)} %all_to_all.17.fields), custom_call_target="tpu_custom_call" | custom-call | bytes 1048576 | tf_op jit(solution)/shard_map/fields/pallas_call | solution.py:683
  80.0 5.5 %collective-permute-start.20 = (f32[2,5,8,128]{3,2,1,0:T(8,128)S(1)}, f32[2,5,8,128]{3,2,1,0:T(8,128)S(1)}, u32[]{:S(2)}, u32[]{:S(2)}) collective-permute-start(f32[2,5,8,128]{3,2,1,0:T(8,128)S(1)} %get-tuple-element.87), channel_id=1, source_target_pairs={{0,64},{64,0},{128,192},{192,128},{1,65},{65,1},{129,193},{193,129... | collective-permute-start | bytes 122888 | tf_op jit(solution)/shard_map/ppermute | solution.py:691
  85.5 0.9 collective-permute-done.20.other
  86.4 0.6 pair.1
  86.9 2.5 %collective-permute-start.21 = (f32[5,8,128]{2,1,0:T(8,128)S(1)}, f32[5,8,128]{2,1,0:T(8,128)S(1)}, u32[]{:S(2)}, u32[]{:S(2)}) collective-permute-start(f32[5,8,128]{2,1,0:T(8,128)S(1)} %get-tuple-element.89), channel_id=1, source_target_pairs={{0,128},{64,192},{128,0},{192,64},{1,129},{65,193},{129,1},{193,65... | collective-permute-start | bytes 61448 | tf_op jit(solution)/shard_map/ppermute | solution.py:695
  89.5 1.7 %collective-permute-done.21.other = f32[5,8,128]{2,1,0:T(8,128)S(1)} collective-permute-done((f32[5,8,128]{2,1,0:T(8,128)S(1)}, f32[5,8,128]{2,1,0:T(8,128)S(1)}, u32[]{:S(2)}, u32[]{:S(2)}) %collective-permute-start.21) | collective-permute-done | bytes 20512 | tf_op jit(solution)/shard_map/ppermute | solution.py:695
  91.2 1.2 %density.3 = (f32[2,8,128]{2,1,0:T(8,128)}, f32[1]{0:T(128)}) custom-call(s32[1]{0:T(128)S(6)} %copy.32.start, s32[2]{0:T(128)S(1)} %pad_add_fusion.place, f32[5,8,128]{2,1,0:T(8,128)S(1)} %get-tuple-element.88.mine, f32[5,8,128]{2,1,0:T(8,128)S(1)} %collective-permute-done.21.other, f32[4,8,128]{2,1,0:T(8,128)S(1)} %get-tuple-element.90.dens), custom_call_target="tpu_custom_call" | custom-call | bytes 1048576 | tf_op jit(solution)/shard_map/density/pallas_call | solution.py:696
  92.4 0.9 while.13
  (4 shorter events, 0.0 us)
Async XLA Ops:
  24.4 14.0 %collective-permute-start.19 = (f32[4,34,8,128]{3,2,1,0:T(8,128)S(1)}, f32[4,34,8,128]{3,2,1,0:T(8,128)S(1)}, u32[]{:S(2)}, u32[]{:S(2)}) collective-permute-start(f32[4,34,8,128]{3,2,1,0:T(8,128)S(1)} %get-tuple-element.307), channel_id=1, source_target_pairs={{8,0},{9,1},{10,2},{11,3},{12,4},{13,5},{14,6},{15,7},{16,8},{17,9... | collective-permute-start | bytes 1671176 | tf_op jit(solution)/shard_map/ppermute | solution.py:653
  25.7 13.6 %collective-permute-start.18 = (f32[4,34,8,128]{3,2,1,0:T(8,128)S(1)}, f32[4,34,8,128]{3,2,1,0:T(8,128)S(1)}, u32[]{:S(2)}, u32[]{:S(2)}) collective-permute-start(f32[4,34,8,128]{3,2,1,0:T(8,128)S(1)} %get-tuple-element.308), channel_id=1, source_target_pairs={{0,8},{1,9},{2,10},{3,11},{4,12},{5,13},{6,14},{7,15},{8,16},{9,17... | collective-permute-start | bytes 1671176 | tf_op jit(solution)/shard_map/ppermute | solution.py:652
  39.3 22.6 %copy-start = (f32[864,128]{1,0:T(8,128)S(1)}, f32[864,128]{1,0:T(8,128)}, u32[]{:S(2)}) copy-start(f32[864,128]{1,0:T(8,128)} %constant.66.clone.pick) | copy-start | bytes 1327108
  39.3 22.6 %copy-start.1 = (f32[288,128]{1,0:T(8,128)S(1)}, f32[288,128]{1,0:T(8,128)}, u32[]{:S(2)}) copy-start(f32[288,128]{1,0:T(8,128)} %constant.67.clone.nudge) | copy-start | bytes 442372
  63.8 28.7 %copy-start.22 = (f32[2,32,128]{2,1,0:T(8,128)S(1)}, f32[2,32,128]{2,1,0:T(8,128)}, u32[]{:S(2)}) copy-start(f32[2,32,128]{2,1,0:T(8,128)} %background.1) | copy-start | bytes 98308
  80.0 6.4 %collective-permute-start.20 = (f32[2,5,8,128]{3,2,1,0:T(8,128)S(1)}, f32[2,5,8,128]{3,2,1,0:T(8,128)S(1)}, u32[]{:S(2)}, u32[]{:S(2)}) collective-permute-start(f32[2,5,8,128]{3,2,1,0:T(8,128)S(1)} %get-tuple-element.87), channel_id=1, source_target_pairs={{0,64},{64,0},{128,192},{192,128},{1,65},{65,1},{129,193},{193,129... | collective-permute-start | bytes 122888 | tf_op jit(solution)/shard_map/ppermute | solution.py:691
  86.9 4.2 %collective-permute-start.21 = (f32[5,8,128]{2,1,0:T(8,128)S(1)}, f32[5,8,128]{2,1,0:T(8,128)S(1)}, u32[]{:S(2)}, u32[]{:S(2)}) collective-permute-start(f32[5,8,128]{2,1,0:T(8,128)S(1)} %get-tuple-element.89), channel_id=1, source_target_pairs={{0,128},{64,192},{128,0},{192,64},{1,129},{65,193},{129,1},{193,65... | collective-permute-start | bytes 61448 | tf_op jit(solution)/shard_map/ppermute | solution.py:695

commit v5 on v4

--- a/solution.py
+++ b/solution.py
@@ -271,7 +271,8 @@
 
 TILES = 4
 SYSTEMS = 8
-BLOCK = 16 * TILES // 2 + 2
+BLOCK = 12 * TILES // 2 + 2
+ROWS_AT = BLOCK - 2
 OWN = 16
 WINDOW = 32
 CORE = 8
@@ -320,12 +321,12 @@
             )
             diag_re = ((6.0 - wave_sq * perm) - CENTRE) * THIRD
             diag_im = absorb[plane, rows] * THIRD
+            part = jnp.where(place[1] % 2 == 0, diag_re, diag_im)
             for system in range(SYSTEMS):
-                out[system, 16 + plane * TILES + tile] = diag_re
-                out[system, 24 + plane * TILES + tile] = diag_im
+                out[system, 16 + plane * TILES + tile] = part
         share = density[plane, pl.ds(pl.multiple_of(place[1] * 8, 8), 8)]
         for system in range(SYSTEMS):
-            out[system, 32 + plane] = share
+            out[system, ROWS_AT + plane] = share
     for system in range(SYSTEMS):
         copies[system].wait()
         for part in range(2):
@@ -404,14 +405,19 @@
         acc[at] = value
 
 
-def inner_kernel(block, basis, diag, acc):
+def inner_kernel(place, block, other, basis, diag, acc):
+    core = place[1] % 2
+
     def load(chunk, _):
         for plane in range(2):
             for part in range(2):
                 for tile in range(TILES):
                     at = part * 8 + plane * TILES + tile
                     basis[0, part, 2 * chunk + plane, tile] = block[chunk, at]
-                    diag[part, 2 * chunk + plane, tile] = block[chunk, 16 + at]
+            for tile in range(TILES):
+                at = plane * TILES + tile
+                diag[core, 2 * chunk + plane, tile] = block[chunk, 16 + at]
+                diag[1 - core, 2 * chunk + plane, tile] = other[chunk, at]
         return 0
 
     lax.fori_loop(0, SYSTEMS, load, 0)
@@ -444,8 +450,12 @@
 )
 
 
-def outer_kernel(place, block, low, high, inner, inner_diag, inner_acc, basis, gram, dens, diag, acc):
-    def load(source, chunks, at):
+def outer_kernel(
+    place, block, low, high, other, inner, inner_diag, inner_acc, basis, gram, dens, diag, acc
+):
+    core = place[1] % 2
+
+    def load(source, first, at):
         def one(chunk, _):
             for plane in range(2):
                 window = at + 2 * chunk + plane
@@ -453,12 +463,15 @@
                     for tile in range(TILES):
                         spot = part * 8 + plane * TILES + tile
                         basis[0, part, window, tile] = source[chunk, spot]
-                        diag[part, window, tile] = source[chunk, 16 + spot]
+                for tile in range(TILES):
+                    spot = plane * TILES + tile
+                    diag[core, window, tile] = source[chunk, 16 + spot]
+                    diag[1 - core, window, tile] = other[first + chunk, spot]
             return 0
 
-        lax.fori_loop(0, chunks, one, 0)
-
-    load(low, SYSTEMS // 2, 0)
+        lax.fori_loop(0, SYSTEMS // 2, one, 0)
+
+    load(low, 0, 0)
     load(high, SYSTEMS // 2, CORE + OWN)
     for level in range(SYSTEMS):
 
@@ -474,11 +487,11 @@
     acc[...] = inner_acc[...]
 
     me = place[0] % SYSTEMS
-    dens[0] = jnp.where(me > 0, block[jnp.maximum(me - 1, 0), 33], low[SYSTEMS // 2 - 1, 33])
-    dens[1] = block[me, 32]
-    dens[2] = block[me, 33]
+    dens[0] = jnp.where(me > 0, block[jnp.maximum(me - 1, 0), ROWS_AT + 1], low[SYSTEMS // 2 - 1, ROWS_AT + 1])
+    dens[1] = block[me, ROWS_AT]
+    dens[2] = block[me, ROWS_AT + 1]
     dens[3] = jnp.where(
-        me < SYSTEMS - 1, block[jnp.minimum(me + 1, SYSTEMS - 1), 32], high[0, 32]
+        me < SYSTEMS - 1, block[jnp.minimum(me + 1, SYSTEMS - 1), ROWS_AT], high[0, ROWS_AT]
     )
 
     third_low = jnp.where(place[0] >= SYSTEMS, THIRD, 0.0)
@@ -545,7 +558,7 @@
     lax.fori_loop(1, SYSTEMS, middle, 0)
 
 
-def fields_kernel(place, fields, forward, adjoint, keep, give, natural):
+def fields_kernel(fields, forward, adjoint):
     half = SYSTEMS // 2
     for port in range(half):
         for part in range(2):
@@ -554,6 +567,10 @@
                     at = (part * 4 + 1 + plane) * TILES + tile
                     forward[port, part, plane, rows_of(tile)] = fields[port, at]
                     adjoint[port, part, plane, rows_of(tile)] = fields[half + port, at]
+
+
+def terms_kernel(place, fields, keep, give, natural):
+    half = SYSTEMS // 2
     for plane in range(4):
         for tile in range(TILES):
             real, imag = plane * TILES + tile, (4 + plane) * TILES + tile
@@ -651,25 +668,30 @@
     down = [(target, source) for source, target in up]
     low = lax.ppermute(block[SYSTEMS // 2 :], "zslab", up)
     high = lax.ppermute(block[: SYSTEMS // 2], "zslab", down)
+    swap = [(i, i ^ 1) for i in range(4)]
+    other = lax.ppermute(block[:, 16:ROWS_AT], "group", swap)
     inner = call(
         inner_kernel,
         (f32(SYSTEMS, 2, OWN, TILES, 8, 128), f32(2, OWN, TILES, 8, 128), f32(128, 8, 128)),
-        [VMEM],
+        [SMEM, VMEM, VMEM],
         (VMEM,) * 3,
         (),
         "inner",
         10**8,
-    )(block)
+    )(place, block, other)
+    low, high, inner = lax.optimization_barrier((low, high, inner))
+    ends = jnp.concatenate([low[:, 16:ROWS_AT], high[:, 16:ROWS_AT]], axis=0)
+    ends = lax.ppermute(ends, "group", swap)
     plane = (TILES, 8, 128)
     basis, gram, dens = call(
         outer_kernel,
         (f32(BASIS, 2, WINDOW, *plane), f32(1, 128), f32(4, 8, 128)),
-        [SMEM] + [VMEM] * 6,
+        [SMEM] + [VMEM] * 7,
         (VMEM, VMEM, VMEM),
         [pltpu.VMEM((2, WINDOW) + plane, jnp.float32), pltpu.VMEM((128, 8, 128), jnp.float32)],
         "outer",
         2 * 10**8,
-    )(place, block, low, high, *inner)
+    )(place, block, low, high, ends, *inner)
     grams = lax.all_to_all(
         jnp.broadcast_to(gram[None], (SYSTEMS, 1, 128)), "zslab", 0, 0,
         axis_index_groups=columns, tiled=True,
@@ -680,13 +702,14 @@
     )(grams, jnp.asarray(pick), jnp.asarray(nudge), basis)
     fields = lax.all_to_all(solved, "zslab", 0, 0, axis_index_groups=planes_of, tiled=True)
     half = f32(SYSTEMS // 2, 2, 2, 8 * TILES, 128)
-    forward, adjoint, keep, give = call(
-        fields_kernel,
-        (half, half, f32(2, 5, 8, 128), f32(2, 5, 8, 128)),
+    forward, adjoint = call(fields_kernel, (half, half), [VMEM], (VMEM,) * 2, (), "fields", 10**7)(fields)
+    keep, give = call(
+        terms_kernel,
+        (f32(2, 5, 8, 128), f32(2, 5, 8, 128)),
         [SMEM, VMEM],
-        (VMEM,) * 4,
+        (VMEM,) * 2,
         [pltpu.VMEM((4, 8 * TILES, 128), jnp.float32)],
-        "fields",
+        "terms",
     )(place, fields)
     got = lax.ppermute(give, "group", [(i, i ^ 1) for i in range(4)])
     keep, give = call(

time: 93.9 us -> 92.2 us (0.982)
  waiting for transfers between devices: 9.82 us -> 4.07 us
  starting transfers between devices: 13.5 us -> 17.6 us
    ppermute x1, waiting for transfers between devices: 6.36 us -> 0.01 us  [on_device(): high = lax.ppermute(block[:SYSTEMS // 2], 'zslab', down)]
    ppermute x0 -> x2, starting transfers between devices: none -> 6.18 us  [the longest x1 3.39 us: on_device(): ends = lax.ppermute(ends, 'group', swap)]
    all_to_all x1, blocking collectives: 21 us -> 18.2 us  [on_device(): lax.all_to_all(packed, 'zslab', 0, 0, axis_index_groups=planes_of, tiled=...]
    ppermute x0 -> x2, waiting for transfers between devices: none -> 2.32 us  [the longest x1 1.16 us: on_device(): other = lax.ppermute(block[:, 16:ROWS_AT], 'group', swap)]
    all_to_all x1, blocking collectives: 14.8 us -> 17 us  [on_device(): lax.all_to_all(solved, 'zslab', 0, 0, axis_index_groups=planes_of, tiled=...]
    ppermute x1, starting transfers between devices: 5.51 us -> 3.43 us  [on_device(): got = lax.ppermute(give, 'group', [(i, i ^ 1) for i in range(4)])]
  transfers between devices with their start and end apart: 4 -> 6, of which waited for: 4 -> 4; matrix products, arithmetic and copies ran while one was open for 0% -> 0% of each run, Pallas kernels for 2% -> 4%
where the time goes in v5:
time: 92.2 us; the launch traced here: 91.7 us
  blocking collectives  51.5 us (56%)
  starting transfers between devices  17.6 us (19%)
  Pallas kernels  15.9 us (17%)
  waiting for transfers between devices  4.07 us (4%)
  between operations  1.61 us (2%)
    all_to_all x1, blocking collectives, on_device(): lax.all_to_all(packed, 'zslab', 0, 0, axis_index_groups=planes_of, tiled=...  18.2 us
    all_to_all x1, blocking collectives, on_device(): lax.all_to_all(solved, 'zslab', 0, 0, axis_index_groups=planes_of, tiled=...  17 us
    all_to_all x1, blocking collectives, on_device(): lax.all_to_all(jnp.broadcast_to(gram[None], (SYSTEMS, 1, 128)), 'zslab',...  16.3 us
    pallas_call x1, Pallas kernels, on_device(): call(outer_kernel, (f32(BASIS, 2, WINDOW, *plane), f32(1, 128), f32(4, 8,...  6.26 us
    ppermute x1, starting transfers between devices, on_device(): low = lax.ppermute(block[SYSTEMS // 2:], 'zslab', up)  4.2 us
    ppermute x1, starting transfers between devices, on_device(): got = lax.ppermute(give, 'group', [(i, i ^ 1) for i in range(4)])  3.43 us
    ppermute x1, starting transfers between devices, on_device(): ends = lax.ppermute(ends, 'group', swap)  3.39 us
    ppermute x1, starting transfers between devices, on_device(): other = lax.ppermute(block[:, 16:ROWS_AT], 'group', swap)  2.8 us
  transfers between devices with their start and end apart: 6, of which 4 were waited for; matrix products, arithmetic and copies ran while one was open for 0% of the time, Pallas kernels for 4%

profile of v5, /device:TPU:1, one launch (start us, length us, event | category | flops | bytes accessed | tf_op | source)
XLA Modules:
  0.0 91.7 jit_solution(2583292049705724619)
XLA Ops:
  1.3 0.1 pad_add_fusion.place
  1.4 1.9 %pack.1 = f32[8,26,8,128]{3,2,1,0:T(8,128)S(1)} custom-call(s32[4]{0:T(128)} %modes.1, s32[1]{0:T(128)S(6)} %copy.32.start, s32[2]{0:T(128)S(1)} %pad_add_fusion.place, f32[2,32,128]{2,1,0:T(8,128)} %background.1, f32[2,32,128]{2,1,0:T(8,128)} %absorb.1, f32[2,32,128]{2,1,0:T(8,128)} %density.2, f32[6,2,2,32,128]{4,3,2,1,0:T(8,128)} %profiles.1, ...), custom_call_target="tpu_custom_call" | custom-call | bytes 1048576 | tf_op jit(solution)/shard_map/pack/pallas_call | solution.py:654
  3.3 18.2 %all_to_all.15.block = f32[8,26,8,128]{3,2,1,0:T(8,128)S(1)} all-to-all(f32[8,26,8,128]{3,2,1,0:T(8,128)S(1)} %pack.1), channel_id=1, replica_groups={{0,1,2,3,4,5,6,7},{8,9,10,11,12,13,14,15},{16,17,18,19,20,21,22,23},{24..., dimensions={0} | all-to-all | bytes 1703936 | tf_op jit(solution)/shard_map/all_to_all | solution.py:665
  21.5 0.1 fusion.55
  21.5 1.3 %collective-permute-start.19 = (f32[4,26,8,128]{3,2,1,0:T(8,128)S(1)}, f32[4,26,8,128]{3,2,1,0:T(8,128)S(1)}, u32[]{:S(2)}, u32[]{:S(2)}) collective-permute-start(f32[4,26,8,128]{3,2,1,0:T(8,128)S(1)} %get-tuple-element.317), channel_id=1, source_target_pairs={{8,0},{9,1},{10,2},{11,3},{12,4},{13,5},{14,6},{15,7},{16,8},{17,9... | collective-permute-start | bytes 1277960 | tf_op jit(solution)/shard_map/ppermute | solution.py:670
  22.8 4.2 %collective-permute-start.18 = (f32[4,26,8,128]{3,2,1,0:T(8,128)S(1)}, f32[4,26,8,128]{3,2,1,0:T(8,128)S(1)}, u32[]{:S(2)}, u32[]{:S(2)}) collective-permute-start(f32[4,26,8,128]{3,2,1,0:T(8,128)S(1)} %get-tuple-element.318), channel_id=1, source_target_pairs={{0,8},{1,9},{2,10},{3,11},{4,12},{5,13},{6,14},{7,15},{8,16},{9,17... | collective-permute-start | bytes 1277960 | tf_op jit(solution)/shard_map/ppermute | solution.py:669
  27.1 2.8 %collective-permute-start.20 = (f32[8,8,8,128]{3,2,1,0:T(8,128)S(1)}, f32[8,8,8,128]{3,2,1,0:T(8,128)S(1)}, u32[]{:S(2)}, u32[]{:S(2)}) collective-permute-start(f32[8,8,8,128]{3,2,1,0:T(8,128)S(1)} %slice.708), channel_id=1, source_target_pairs={{0,64},{64,0},{128,192},{192,128},{1,65},{65,1},{129,193},{193,129... | collective-permute-start | bytes 786440 | tf_op jit(solution)/shard_map/ppermute | solution.py:672
  29.9 1.2 %collective-permute-done.20.other = f32[8,8,8,128]{3,2,1,0:T(8,128)S(1)} collective-permute-done((f32[8,8,8,128]{3,2,1,0:T(8,128)S(1)}, f32[8,8,8,128]{3,2,1,0:T(8,128)S(1)}, u32[]{:S(2)}, u32[]{:S(2)}) %collective-permute-start.20) | collective-permute-done | bytes 262176 | tf_op jit(solution)/shard_map/ppermute | solution.py:672
  31.0 2.7 %inner.1 = (f32[8,2,16,4,8,128]{5,4,3,2,1,0:T(8,128)S(1)}, f32[2,16,4,8,128]{4,3,2,1,0:T(8,128)S(1)}, f32[128,8,128]{2,1,0:T(8,128)S(1)}) custom-call(s32[2]{0:T(128)S(1)} %pad_add_fusion.place, f32[8,26,8,128]{3,2,1,0:T(8,128)S(1)} %all_to_all.15.block, f32[8,8,8,128]{3,2,1,0:T(8,128)S(1)} %collective-permute-done.20.other), custom_call_target="tpu_custom_call" | custom-call | flops 100000000 | bytes 1048576 | tf_op jit(solution)/shard_map/inner/pallas_call | solution.py:673
  33.8 3.4 %collective-permute-start.21 = (f32[8,8,8,128]{3,2,1,0:T(8,128)S(1)}, f32[8,8,8,128]{3,2,1,0:T(8,128)S(1)}, u32[]{:S(2)}, u32[]{:S(2)}) collective-permute-start(f32[8,8,8,128]{3,2,1,0:T(8,128)S(1)} %pad_maximum_fusion.18), channel_id=1, source_target_pairs={{0,64},{64,0},{128,192},{192,128},{1,65},{65,1},{129,193},{193,129... | collective-permute-start | bytes 786440 | tf_op jit(solution)/shard_map/ppermute | solution.py:684
  37.2 1.2 %collective-permute-done.21.other = f32[8,8,8,128]{3,2,1,0:T(8,128)S(1)} collective-permute-done((f32[8,8,8,128]{3,2,1,0:T(8,128)S(1)}, f32[8,8,8,128]{3,2,1,0:T(8,128)S(1)}, u32[]{:S(2)}, u32[]{:S(2)}) %collective-permute-start.21) | collective-permute-done | bytes 262176 | tf_op jit(solution)/shard_map/ppermute | solution.py:684
  38.4 6.3 %outer.1 = (f32[9,2,32,4,8,128]{5,4,3,2,1,0:T(8,128)S(1)}, f32[1,128]{1,0:T(1,128)S(1)}, f32[4,8,128]{2,1,0:T(8,128)S(1)}) custom-call(s32[2]{0:T(128)S(1)} %pad_add_fusion.place, f32[8,26,8,128]{3,2,1,0:T(8,128)S(1)} %all_to_all.15.block, f32[4,26,8,128]{3,2,1,0:T(8,128)S(1)} %collective-permute-done.18.low, ...), custom_call_target="tpu_custom_call" | custom-call | flops 200000000 | bytes 1048576 | tf_op jit(solution)/shard_map/outer/pallas_call | solution.py:686
  44.6 16.3 %all_to_all.16.grams = f32[8,1,128]{2,1,0:T(1,128)S(1)} all-to-all(f32[8,1,128]{2,1,0:T(1,128)S(1)} %broadcast_in_dim.18), channel_id=1, replica_groups={{0,8,16,24,32,40,48,56},{1,9,17,25,33,41,49,57},{2,10,18,26,34,42,50,58..., dimensions={0} | all-to-all | bytes 8192 | tf_op jit(solution)/shard_map/all_to_all | solution.py:695
  60.9 1.8 %combine.1 = f32[8,33,8,128]{3,2,1,0:T(8,128)S(1)} custom-call(f32[8,1,128]{2,1,0:T(1,128)S(1)} %all_to_all.16.grams, f32[864,128]{1,0:T(8,128)S(1)} %copy-done, f32[288,128]{1,0:T(8,128)S(1)} %copy-done.1, f32[9,2,32,4,8,128]{5,4,3,2,1,0:T(8,128)S(1)} %get-tuple-element.95.basis), custom_call_target="tpu_custom_call" | custom-call | bytes 1048576 | tf_op jit(solution)/shard_map/combine/pallas_call | solution.py:700
  62.8 17.0 %all_to_all.17.fields = f32[8,33,8,128]{3,2,1,0:T(8,128)S(1)} all-to-all(f32[8,33,8,128]{3,2,1,0:T(8,128)S(1)} %combine.1), channel_id=1, replica_groups={{0,1,2,3,4,5,6,7},{8,9,10,11,12,13,14,15},{16,17,18,19,20,21,22,23},{24..., dimensions={0} | all-to-all | bytes 2162688 | tf_op jit(solution)/shard_map/all_to_all | solution.py:703
  79.7 0.6 terms.1
  80.3 3.4 %collective-permute-start.22 = (f32[2,5,8,128]{3,2,1,0:T(8,128)S(1)}, f32[2,5,8,128]{3,2,1,0:T(8,128)S(1)}, u32[]{:S(2)}, u32[]{:S(2)}) collective-permute-start(f32[2,5,8,128]{3,2,1,0:T(8,128)S(1)} %get-tuple-element.97), channel_id=1, source_target_pairs={{0,64},{64,0},{128,192},{192,128},{1,65},{65,1},{129,193},{193,129... | collective-permute-start | bytes 122888 | tf_op jit(solution)/shard_map/ppermute | solution.py:714
  83.8 0.9 collective-permute-done.22.other
  84.6 0.6 pair.1
  85.2 2.5 %collective-permute-start.23 = (f32[5,8,128]{2,1,0:T(8,128)S(1)}, f32[5,8,128]{2,1,0:T(8,128)S(1)}, u32[]{:S(2)}, u32[]{:S(2)}) collective-permute-start(f32[5,8,128]{2,1,0:T(8,128)S(1)} %get-tuple-element.99), channel_id=1, source_target_pairs={{0,128},{64,192},{128,0},{192,64},{1,129},{65,193},{129,1},{193,65... | collective-permute-start | bytes 61448 | tf_op jit(solution)/shard_map/ppermute | solution.py:718
  87.7 0.8 fields.1
  88.6 0.9 collective-permute-done.23.other
  89.4 1.2 %density.3 = (f32[2,8,128]{2,1,0:T(8,128)}, f32[1]{0:T(128)}) custom-call(s32[1]{0:T(128)S(6)} %copy.32.start, s32[2]{0:T(128)S(1)} %pad_add_fusion.place, f32[5,8,128]{2,1,0:T(8,128)S(1)} %get-tuple-element.98.mine, f32[5,8,128]{2,1,0:T(8,128)S(1)} %collective-permute-done.23.other, f32[4,8,128]{2,1,0:T(8,128)S(1)} %get-tuple-element.100.dens), custom_call_target="tpu_custom_call" | custom-call | bytes 1048576 | tf_op jit(solution)/shard_map/density/pallas_call | solution.py:719
  90.7 0.9 while.13
  (13 shorter events, 0.1 us)
Async XLA Ops:
  21.5 12.2 %collective-permute-start.19 = (f32[4,26,8,128]{3,2,1,0:T(8,128)S(1)}, f32[4,26,8,128]{3,2,1,0:T(8,128)S(1)}, u32[]{:S(2)}, u32[]{:S(2)}) collective-permute-start(f32[4,26,8,128]{3,2,1,0:T(8,128)S(1)} %get-tuple-element.317), channel_id=1, source_target_pairs={{8,0},{9,1},{10,2},{11,3},{12,4},{13,5},{14,6},{15,7},{16,8},{17,9... | collective-permute-start | bytes 1277960 | tf_op jit(solution)/shard_map/ppermute | solution.py:670
  22.8 10.9 %collective-permute-start.18 = (f32[4,26,8,128]{3,2,1,0:T(8,128)S(1)}, f32[4,26,8,128]{3,2,1,0:T(8,128)S(1)}, u32[]{:S(2)}, u32[]{:S(2)}) collective-permute-start(f32[4,26,8,128]{3,2,1,0:T(8,128)S(1)} %get-tuple-element.318), channel_id=1, source_target_pairs={{0,8},{1,9},{2,10},{3,11},{4,12},{5,13},{6,14},{7,15},{8,16},{9,17... | collective-permute-start | bytes 1277960 | tf_op jit(solution)/shard_map/ppermute | solution.py:669
  27.1 4.0 %collective-permute-start.20 = (f32[8,8,8,128]{3,2,1,0:T(8,128)S(1)}, f32[8,8,8,128]{3,2,1,0:T(8,128)S(1)}, u32[]{:S(2)}, u32[]{:S(2)}) collective-permute-start(f32[8,8,8,128]{3,2,1,0:T(8,128)S(1)} %slice.708), channel_id=1, source_target_pairs={{0,64},{64,0},{128,192},{192,128},{1,65},{65,1},{129,193},{193,129... | collective-permute-start | bytes 786440 | tf_op jit(solution)/shard_map/ppermute | solution.py:672
  33.8 27.2 %copy-start = (f32[864,128]{1,0:T(8,128)S(1)}, f32[864,128]{1,0:T(8,128)}, u32[]{:S(2)}) copy-start(f32[864,128]{1,0:T(8,128)} %constant.66.clone.pick) | copy-start | bytes 1327108
  33.8 27.1 %copy-start.1 = (f32[288,128]{1,0:T(8,128)S(1)}, f32[288,128]{1,0:T(8,128)}, u32[]{:S(2)}) copy-start(f32[288,128]{1,0:T(8,128)} %constant.67.clone.nudge) | copy-start | bytes 442372
  33.8 4.5 %collective-permute-start.21 = (f32[8,8,8,128]{3,2,1,0:T(8,128)S(1)}, f32[8,8,8,128]{3,2,1,0:T(8,128)S(1)}, u32[]{:S(2)}, u32[]{:S(2)}) collective-permute-start(f32[8,8,8,128]{3,2,1,0:T(8,128)S(1)} %pad_maximum_fusion.18), channel_id=1, source_target_pairs={{0,64},{64,0},{128,192},{192,128},{1,65},{65,1},{129,193},{193,129... | collective-permute-start | bytes 786440 | tf_op jit(solution)/shard_map/ppermute | solution.py:684
  62.7 27.9 %copy-start.20 = (f32[2,32,128]{2,1,0:T(8,128)S(1)}, f32[2,32,128]{2,1,0:T(8,128)}, u32[]{:S(2)}) copy-start(f32[2,32,128]{2,1,0:T(8,128)} %background.1) | copy-start | bytes 98308
  80.3 4.3 %collective-permute-start.22 = (f32[2,5,8,128]{3,2,1,0:T(8,128)S(1)}, f32[2,5,8,128]{3,2,1,0:T(8,128)S(1)}, u32[]{:S(2)}, u32[]{:S(2)}) collective-permute-start(f32[2,5,8,128]{3,2,1,0:T(8,128)S(1)} %get-tuple-element.97), channel_id=1, source_target_pairs={{0,64},{64,0},{128,192},{192,128},{1,65},{65,1},{129,193},{193,129... | collective-permute-start | bytes 122888 | tf_op jit(solution)/shard_map/ppermute | solution.py:714
  85.2 4.2 %collective-permute-start.23 = (f32[5,8,128]{2,1,0:T(8,128)S(1)}, f32[5,8,128]{2,1,0:T(8,128)S(1)}, u32[]{:S(2)}, u32[]{:S(2)}) collective-permute-start(f32[5,8,128]{2,1,0:T(8,128)S(1)} %get-tuple-element.99), channel_id=1, source_target_pairs={{0,128},{64,192},{128,0},{192,64},{1,129},{65,193},{129,1},{193,65... | collective-permute-start | bytes 61448 | tf_op jit(solution)/shard_map/ppermute | solution.py:718

commit v6 on v5

--- a/solution.py
+++ b/solution.py
@@ -168,7 +168,7 @@
 
 def gram_tables():
     real, imag = pair_places()
-    pick = np.zeros((6 * ROWS, 128), np.float32)
+    pick = np.zeros((2 * ROWS + 16, 128), np.float32)
     nudge = np.zeros((2 * ROWS, 128), np.float32)
     rng = np.random.default_rng(7)
     sign_re = {pair: np.where(rng.random(128) < 0.5, -1.0, 1.0) for pair in real}
@@ -177,14 +177,12 @@
         for i in range(BASIS):
             row, pair = j * 16 + i, (min(i, j), max(i, j))
             pick[row, real[pair]] = 1.0
-            for half in (0, ROWS):
-                pick[2 * ROWS + half + row, real[(i, i)]] = 1.0
-                pick[4 * ROWS + half + row, real[(j, j)]] = 1.0
             nudge[row] = NUDGE * sign_re[pair]
             if i != j:
                 side = 1.0 if i < j else -1.0
                 pick[ROWS + row, imag[pair]] = side
                 nudge[ROWS + row] = NUDGE * side * sign_im[pair]
+        pick[2 * ROWS + j, real[(j, j)]] = 1.0
     nudge[:, 0] = 0.0
     return pick, nudge
 
@@ -204,9 +202,7 @@
     return (left[0] + right[0], left[1] + right[1])
 
 
-def coefficients(gram):
-    gram_re = [gram[16 * j : 16 * j + 16] for j in range(BASIS)]
-    gram_im = [gram[ROWS + 16 * j : ROWS + 16 * j + 16] for j in range(BASIS)]
+def coefficients(gram_re, gram_im):
     row = lax.broadcasted_iota(jnp.int32, (16, 128), 0)
     keep = jnp.where(row == 15, 0.0, HALF_RADIUS)
 
@@ -271,8 +267,8 @@
 
 TILES = 4
 SYSTEMS = 8
-BLOCK = 12 * TILES // 2 + 2
-ROWS_AT = BLOCK - 2
+BLOCK = 12 * TILES // 2 + 1
+ROWS_AT = BLOCK - 1
 OWN = 16
 WINDOW = 32
 CORE = 8
@@ -324,9 +320,10 @@
             part = jnp.where(place[1] % 2 == 0, diag_re, diag_im)
             for system in range(SYSTEMS):
                 out[system, 16 + plane * TILES + tile] = part
-        share = density[plane, pl.ds(pl.multiple_of(place[1] * 8, 8), 8)]
-        for system in range(SYSTEMS):
-            out[system, ROWS_AT + plane] = share
+    share = pl.ds(pl.multiple_of(place[1] * 8, 8), 8)
+    after = (place[0] + 1) % SYSTEMS
+    for slab in range(SYSTEMS):
+        out[slab, ROWS_AT] = jnp.where(after == slab, density[1, share], density[0, share])
     for system in range(SYSTEMS):
         copies[system].wait()
         for part in range(2):
@@ -420,7 +417,7 @@
                 diag[1 - core, 2 * chunk + plane, tile] = other[chunk, at]
         return 0
 
-    lax.fori_loop(0, SYSTEMS, load, 0)
+    lax.fori_loop(0, SYSTEMS, load, 0, unroll=SYSTEMS)
     stencil = Stencil()
     for level in range(SYSTEMS - 1):
 
@@ -451,7 +448,7 @@
 
 
 def outer_kernel(
-    place, block, low, high, other, inner, inner_diag, inner_acc, basis, gram, dens, diag, acc
+    place, density, block, low, high, other, inner, inner_diag, inner_acc, basis, gram, dens, diag, acc
 ):
     core = place[1] % 2
 
@@ -469,7 +466,7 @@
                     diag[1 - core, window, tile] = other[first + chunk, spot]
             return 0
 
-        lax.fori_loop(0, SYSTEMS // 2, one, 0)
+        lax.fori_loop(0, SYSTEMS // 2, one, 0, unroll=SYSTEMS // 2)
 
     load(low, 0, 0)
     load(high, SYSTEMS // 2, CORE + OWN)
@@ -483,13 +480,16 @@
                         diag[part, CORE + at, tile] = inner_diag[part, at, tile]
             return 0
 
-        lax.fori_loop(level, OWN - level, keep, 0, unroll=2)
+        lax.fori_loop(level, OWN - level, keep, 0, unroll=OWN - 2 * level)
     acc[...] = inner_acc[...]
 
     me = place[0] % SYSTEMS
-    dens[0] = jnp.where(me > 0, block[jnp.maximum(me - 1, 0), ROWS_AT + 1], low[SYSTEMS // 2 - 1, ROWS_AT + 1])
-    dens[1] = block[me, ROWS_AT]
-    dens[2] = block[me, ROWS_AT + 1]
+    share = pl.ds(pl.multiple_of(place[1] * 8, 8), 8)
+    dens[0] = jnp.where(
+        me > 0, block[jnp.maximum(me - 1, 0), ROWS_AT], low[SYSTEMS // 2 - 1, ROWS_AT]
+    )
+    dens[1] = density[0, share]
+    dens[2] = density[1, share]
     dens[3] = jnp.where(
         me < SYSTEMS - 1, block[jnp.minimum(me + 1, SYSTEMS - 1), ROWS_AT], high[0, ROWS_AT]
     )
@@ -521,8 +521,13 @@
         row = row + grams[other]
     ones = jnp.ones((128, 128), jnp.float32)
     picked = exact_dot(pick[...] * row, ones, ((1,), (0,)))
-    norms = jnp.sqrt(picked[2 * ROWS : 4 * ROWS] * picked[4 * ROWS :])
-    answer, apart, size = coefficients(picked[: 2 * ROWS] + nudge[...] * norms)
+    norms = jnp.sqrt(picked[2 * ROWS :])
+    gram = []
+    for column in range(2 * BASIS):
+        rows = slice(16 * column, 16 * column + 16)
+        scale = norms * norms[column % BASIS : column % BASIS + 1]
+        gram.append(picked[rows] + nudge[rows] * scale)
+    answer, apart, size = coefficients(gram[:BASIS], gram[BASIS:])
     agrees = jnp.max(jnp.where(apart <= AGREE * AGREE * size, 0.0, 1.0))
     flag = jnp.zeros((8, 128), jnp.float32) + agrees
     for slab in range(SYSTEMS):
@@ -686,12 +691,12 @@
     basis, gram, dens = call(
         outer_kernel,
         (f32(BASIS, 2, WINDOW, *plane), f32(1, 128), f32(4, 8, 128)),
-        [SMEM] + [VMEM] * 7,
+        [SMEM] + [VMEM] * 8,
         (VMEM, VMEM, VMEM),
         [pltpu.VMEM((2, WINDOW) + plane, jnp.float32), pltpu.VMEM((128, 8, 128), jnp.float32)],
         "outer",
         2 * 10**8,
-    )(place, block, low, high, ends, *inner)
+    )(place, density, block, low, high, ends, *inner)
     grams = lax.all_to_all(
         jnp.broadcast_to(gram[None], (SYSTEMS, 1, 128)), "zslab", 0, 0,
         axis_index_groups=columns, tiled=True,

time: 92.2 us -> 90.7 us (0.984)
  no operation moved by 1% of the time
where the time goes in v6:
time: 90.7 us; the launch traced here: 90.3 us
  blocking collectives  51.1 us (56%)
  starting transfers between devices  16.8 us (19%)
  Pallas kernels  15.6 us (17%)
  waiting for transfers between devices  4.06 us (4%)
  between operations  1.6 us (2%)
    all_to_all x1, blocking collectives, on_device(): lax.all_to_all(packed, 'zslab', 0, 0, axis_index_groups=planes_of, tiled=...  18 us
    all_to_all x1, blocking collectives, on_device(): lax.all_to_all(solved, 'zslab', 0, 0, axis_index_groups=planes_of, tiled=...  16.8 us
    all_to_all x1, blocking collectives, on_device(): lax.all_to_all(jnp.broadcast_to(gram[None], (SYSTEMS, 1, 128)), 'zslab',...  16.3 us
    pallas_call x1, Pallas kernels, on_device(): call(outer_kernel, (f32(BASIS, 2, WINDOW, *plane), f32(1, 128), f32(4, 8,...  6.22 us
    ppermute x1, starting transfers between devices, on_device(): low = lax.ppermute(block[SYSTEMS // 2:], 'zslab', up)  4.2 us
    ppermute x1, starting transfers between devices, on_device(): ends = lax.ppermute(ends, 'group', swap)  3.2 us
    ppermute x1, starting transfers between devices, on_device(): got = lax.ppermute(give, 'group', [(i, i ^ 1) for i in range(4)])  2.93 us
    ppermute x1, starting transfers between devices, on_device(): other = lax.ppermute(block[:, 16:ROWS_AT], 'group', swap)  2.68 us
  transfers between devices with their start and end apart: 6, of which 4 were waited for; matrix products, arithmetic and copies ran while one was open for 0% of the time, Pallas kernels for 4%

profile of v6, /device:TPU:1, one launch (start us, length us, event | category | flops | bytes accessed | tf_op | source)
XLA Modules:
  0.0 90.3 jit_solution(18306845799508733917)
XLA Ops:
  1.3 0.1 pad_add_fusion.place
  1.4 1.9 %pack.1 = f32[8,25,8,128]{3,2,1,0:T(8,128)S(1)} custom-call(s32[4]{0:T(128)} %modes.1, s32[1]{0:T(128)S(6)} %copy.32.start, s32[2]{0:T(128)S(1)} %pad_add_fusion.place, f32[2,32,128]{2,1,0:T(8,128)} %background.1, f32[2,32,128]{2,1,0:T(8,128)} %absorb.1, f32[2,32,128]{2,1,0:T(8,128)} %density.4, f32[6,2,2,32,128]{4,3,2,1,0:T(8,128)} %profiles.1, ...), custom_call_target="tpu_custom_call" | custom-call | bytes 1048576 | tf_op jit(solution)/shard_map/pack/pallas_call | solution.py:659
  3.3 18.0 %all_to_all.15.block = f32[8,25,8,128]{3,2,1,0:T(8,128)S(1)} all-to-all(f32[8,25,8,128]{3,2,1,0:T(8,128)S(1)} %pack.1), channel_id=1, replica_groups={{0,1,2,3,4,5,6,7},{8,9,10,11,12,13,14,15},{16,17,18,19,20,21,22,23},{24..., dimensions={0} | all-to-all | bytes 1638400 | tf_op jit(solution)/shard_map/all_to_all | solution.py:670
  21.3 0.1 fusion.55
  21.4 1.3 %collective-permute-start.19 = (f32[4,25,8,128]{3,2,1,0:T(8,128)S(1)}, f32[4,25,8,128]{3,2,1,0:T(8,128)S(1)}, u32[]{:S(2)}, u32[]{:S(2)}) collective-permute-start(f32[4,25,8,128]{3,2,1,0:T(8,128)S(1)} %get-tuple-element.317), channel_id=1, source_target_pairs={{8,0},{9,1},{10,2},{11,3},{12,4},{13,5},{14,6},{15,7},{16,8},{17,9... | collective-permute-start | bytes 1228808 | tf_op jit(solution)/shard_map/ppermute | solution.py:675
  22.7 4.2 %collective-permute-start.18 = (f32[4,25,8,128]{3,2,1,0:T(8,128)S(1)}, f32[4,25,8,128]{3,2,1,0:T(8,128)S(1)}, u32[]{:S(2)}, u32[]{:S(2)}) collective-permute-start(f32[4,25,8,128]{3,2,1,0:T(8,128)S(1)} %get-tuple-element.318), channel_id=1, source_target_pairs={{0,8},{1,9},{2,10},{3,11},{4,12},{5,13},{6,14},{7,15},{8,16},{9,17... | collective-permute-start | bytes 1228808 | tf_op jit(solution)/shard_map/ppermute | solution.py:674
  26.9 2.7 %collective-permute-start.20 = (f32[8,8,8,128]{3,2,1,0:T(8,128)S(1)}, f32[8,8,8,128]{3,2,1,0:T(8,128)S(1)}, u32[]{:S(2)}, u32[]{:S(2)}) collective-permute-start(f32[8,8,8,128]{3,2,1,0:T(8,128)S(1)} %slice.708), channel_id=1, source_target_pairs={{0,64},{64,0},{128,192},{192,128},{1,65},{65,1},{129,193},{193,129... | collective-permute-start | bytes 786440 | tf_op jit(solution)/shard_map/ppermute | solution.py:677
  29.6 1.2 %collective-permute-done.20.other = f32[8,8,8,128]{3,2,1,0:T(8,128)S(1)} collective-permute-done((f32[8,8,8,128]{3,2,1,0:T(8,128)S(1)}, f32[8,8,8,128]{3,2,1,0:T(8,128)S(1)}, u32[]{:S(2)}, u32[]{:S(2)}) %collective-permute-start.20) | collective-permute-done | bytes 262176 | tf_op jit(solution)/shard_map/ppermute | solution.py:677
  30.8 2.6 %inner.1 = (f32[8,2,16,4,8,128]{5,4,3,2,1,0:T(8,128)S(1)}, f32[2,16,4,8,128]{4,3,2,1,0:T(8,128)S(1)}, f32[128,8,128]{2,1,0:T(8,128)S(1)}) custom-call(s32[2]{0:T(128)S(1)} %pad_add_fusion.place, f32[8,25,8,128]{3,2,1,0:T(8,128)S(1)} %all_to_all.15.block, f32[8,8,8,128]{3,2,1,0:T(8,128)S(1)} %collective-permute-done.20.other), custom_call_target="tpu_custom_call" | custom-call | flops 100000000 | bytes 1048576 | tf_op jit(solution)/shard_map/inner/pallas_call | solution.py:678
  33.5 3.2 %collective-permute-start.21 = (f32[8,8,8,128]{3,2,1,0:T(8,128)S(1)}, f32[8,8,8,128]{3,2,1,0:T(8,128)S(1)}, u32[]{:S(2)}, u32[]{:S(2)}) collective-permute-start(f32[8,8,8,128]{3,2,1,0:T(8,128)S(1)} %pad_maximum_fusion.18), channel_id=1, source_target_pairs={{0,64},{64,0},{128,192},{192,128},{1,65},{65,1},{129,193},{193,129... | collective-permute-start | bytes 786440 | tf_op jit(solution)/shard_map/ppermute | solution.py:689
  36.7 1.2 %collective-permute-done.21.other = f32[8,8,8,128]{3,2,1,0:T(8,128)S(1)} collective-permute-done((f32[8,8,8,128]{3,2,1,0:T(8,128)S(1)}, f32[8,8,8,128]{3,2,1,0:T(8,128)S(1)}, u32[]{:S(2)}, u32[]{:S(2)}) %collective-permute-start.21) | collective-permute-done | bytes 262176 | tf_op jit(solution)/shard_map/ppermute | solution.py:689
  37.9 6.2 %outer.1 = (f32[9,2,32,4,8,128]{5,4,3,2,1,0:T(8,128)S(1)}, f32[1,128]{1,0:T(1,128)S(1)}, f32[4,8,128]{2,1,0:T(8,128)S(1)}) custom-call(s32[2]{0:T(128)S(1)} %pad_add_fusion.place, f32[2,32,128]{2,1,0:T(8,128)S(1)} %copy-done.20, f32[8,25,8,128]{3,2,1,0:T(8,128)S(1)} %all_to_all.15.block, f32[4,25,8,128]{3,2,1,0:T(8,128)S(1)} %collective-permute-done.18.low, ...), custom_call_target="tpu_custom_call" | custom-call | flops 200000000 | bytes 1048576 | tf_op jit(solution)/shard_map/outer/pallas_call | solution.py:691
  44.1 16.3 %all_to_all.16.grams = f32[8,1,128]{2,1,0:T(1,128)S(1)} all-to-all(f32[8,1,128]{2,1,0:T(1,128)S(1)} %broadcast_in_dim.18), channel_id=1, replica_groups={{0,8,16,24,32,40,48,56},{1,9,17,25,33,41,49,57},{2,10,18,26,34,42,50,58..., dimensions={0} | all-to-all | bytes 8192 | tf_op jit(solution)/shard_map/all_to_all | solution.py:700
  60.4 1.6 %combine.1 = f32[8,33,8,128]{3,2,1,0:T(8,128)S(1)} custom-call(f32[8,1,128]{2,1,0:T(1,128)S(1)} %all_to_all.16.grams, f32[304,128]{1,0:T(8,128)S(1)} %copy-done, f32[288,128]{1,0:T(8,128)S(1)} %copy-done.1, f32[9,2,32,4,8,128]{5,4,3,2,1,0:T(8,128)S(1)} %get-tuple-element.95.basis), custom_call_target="tpu_custom_call" | custom-call | bytes 1048576 | tf_op jit(solution)/shard_map/combine/pallas_call | solution.py:705
  62.0 16.8 %all_to_all.17.fields = f32[8,33,8,128]{3,2,1,0:T(8,128)S(1)} all-to-all(f32[8,33,8,128]{3,2,1,0:T(8,128)S(1)} %combine.1), channel_id=1, replica_groups={{0,1,2,3,4,5,6,7},{8,9,10,11,12,13,14,15},{16,17,18,19,20,21,22,23},{24..., dimensions={0} | all-to-all | bytes 2162688 | tf_op jit(solution)/shard_map/all_to_all | solution.py:708
  78.8 0.6 terms.1
  79.4 2.9 %collective-permute-start.22 = (f32[2,5,8,128]{3,2,1,0:T(8,128)S(1)}, f32[2,5,8,128]{3,2,1,0:T(8,128)S(1)}, u32[]{:S(2)}, u32[]{:S(2)}) collective-permute-start(f32[2,5,8,128]{3,2,1,0:T(8,128)S(1)} %get-tuple-element.97), channel_id=1, source_target_pairs={{0,64},{64,0},{128,192},{192,128},{1,65},{65,1},{129,193},{193,129... | collective-permute-start | bytes 122888 | tf_op jit(solution)/shard_map/ppermute | solution.py:719
  82.3 0.9 collective-permute-done.22.other
  83.2 0.6 pair.1
  83.7 2.5 %collective-permute-start.23 = (f32[5,8,128]{2,1,0:T(8,128)S(1)}, f32[5,8,128]{2,1,0:T(8,128)S(1)}, u32[]{:S(2)}, u32[]{:S(2)}) collective-permute-start(f32[5,8,128]{2,1,0:T(8,128)S(1)} %get-tuple-element.99), channel_id=1, source_target_pairs={{0,128},{64,192},{128,0},{192,64},{1,129},{65,193},{129,1},{193,65... | collective-permute-start | bytes 61448 | tf_op jit(solution)/shard_map/ppermute | solution.py:723
  86.3 0.8 fields.1
  87.1 0.9 collective-permute-done.23.other
  88.0 1.2 %density.5 = (f32[2,8,128]{2,1,0:T(8,128)}, f32[1]{0:T(128)}) custom-call(s32[1]{0:T(128)S(6)} %copy.32.start, s32[2]{0:T(128)S(1)} %pad_add_fusion.place, f32[5,8,128]{2,1,0:T(8,128)S(1)} %get-tuple-element.98.mine, f32[5,8,128]{2,1,0:T(8,128)S(1)} %collective-permute-done.23.other, f32[4,8,128]{2,1,0:T(8,128)S(1)} %get-tuple-element.100.dens), custom_call_target="tpu_custom_call" | custom-call | bytes 1048576 | tf_op jit(solution)/shard_map/density/pallas_call | solution.py:724
  89.2 0.9 while.13
  (13 shorter events, 0.1 us)
Async XLA Ops:
  3.3 34.6 %copy-start.20 = (f32[2,32,128]{2,1,0:T(8,128)S(1)}, f32[2,32,128]{2,1,0:T(8,128)}, u32[]{:S(2)}) copy-start(f32[2,32,128]{2,1,0:T(8,128)} %density.4) | copy-start | bytes 98308
  21.4 12.0 %collective-permute-start.19 = (f32[4,25,8,128]{3,2,1,0:T(8,128)S(1)}, f32[4,25,8,128]{3,2,1,0:T(8,128)S(1)}, u32[]{:S(2)}, u32[]{:S(2)}) collective-permute-start(f32[4,25,8,128]{3,2,1,0:T(8,128)S(1)} %get-tuple-element.317), channel_id=1, source_target_pairs={{8,0},{9,1},{10,2},{11,3},{12,4},{13,5},{14,6},{15,7},{16,8},{17,9... | collective-permute-start | bytes 1228808 | tf_op jit(solution)/shard_map/ppermute | solution.py:675
  22.7 10.7 %collective-permute-start.18 = (f32[4,25,8,128]{3,2,1,0:T(8,128)S(1)}, f32[4,25,8,128]{3,2,1,0:T(8,128)S(1)}, u32[]{:S(2)}, u32[]{:S(2)}) collective-permute-start(f32[4,25,8,128]{3,2,1,0:T(8,128)S(1)} %get-tuple-element.318), channel_id=1, source_target_pairs={{0,8},{1,9},{2,10},{3,11},{4,12},{5,13},{6,14},{7,15},{8,16},{9,17... | collective-permute-start | bytes 1228808 | tf_op jit(solution)/shard_map/ppermute | solution.py:674
  26.9 3.8 %collective-permute-start.20 = (f32[8,8,8,128]{3,2,1,0:T(8,128)S(1)}, f32[8,8,8,128]{3,2,1,0:T(8,128)S(1)}, u32[]{:S(2)}, u32[]{:S(2)}) collective-permute-start(f32[8,8,8,128]{3,2,1,0:T(8,128)S(1)} %slice.708), channel_id=1, source_target_pairs={{0,64},{64,0},{128,192},{192,128},{1,65},{65,1},{129,193},{193,129... | collective-permute-start | bytes 786440 | tf_op jit(solution)/shard_map/ppermute | solution.py:677
  33.5 26.9 %copy-start = (f32[304,128]{1,0:T(8,128)S(1)}, f32[304,128]{1,0:T(8,128)}, u32[]{:S(2)}) copy-start(f32[304,128]{1,0:T(8,128)} %constant.66.clone.pick) | copy-start | bytes 466948
  33.5 26.9 %copy-start.1 = (f32[288,128]{1,0:T(8,128)S(1)}, f32[288,128]{1,0:T(8,128)}, u32[]{:S(2)}) copy-start(f32[288,128]{1,0:T(8,128)} %constant.67.clone.nudge) | copy-start | bytes 442372
  33.5 4.4 %collective-permute-start.21 = (f32[8,8,8,128]{3,2,1,0:T(8,128)S(1)}, f32[8,8,8,128]{3,2,1,0:T(8,128)S(1)}, u32[]{:S(2)}, u32[]{:S(2)}) collective-permute-start(f32[8,8,8,128]{3,2,1,0:T(8,128)S(1)} %pad_maximum_fusion.18), channel_id=1, source_target_pairs={{0,64},{64,0},{128,192},{192,128},{1,65},{65,1},{129,193},{193,129... | collective-permute-start | bytes 786440 | tf_op jit(solution)/shard_map/ppermute | solution.py:689
  79.4 3.8 %collective-permute-start.22 = (f32[2,5,8,128]{3,2,1,0:T(8,128)S(1)}, f32[2,5,8,128]{3,2,1,0:T(8,128)S(1)}, u32[]{:S(2)}, u32[]{:S(2)}) collective-permute-start(f32[2,5,8,128]{3,2,1,0:T(8,128)S(1)} %get-tuple-element.97), channel_id=1, source_target_pairs={{0,64},{64,0},{128,192},{192,128},{1,65},{65,1},{129,193},{193,129... | collective-permute-start | bytes 122888 | tf_op jit(solution)/shard_map/ppermute | solution.py:719
  83.7 4.2 %collective-permute-start.23 = (f32[5,8,128]{2,1,0:T(8,128)S(1)}, f32[5,8,128]{2,1,0:T(8,128)S(1)}, u32[]{:S(2)}, u32[]{:S(2)}) collective-permute-start(f32[5,8,128]{2,1,0:T(8,128)S(1)} %get-tuple-element.99), channel_id=1, source_target_pairs={{0,128},{64,192},{128,0},{192,64},{1,129},{65,193},{129,1},{193,65... | collective-permute-start | bytes 61448 | tf_op jit(solution)/shard_map/ppermute | solution.py:723

commit v7 on v6

--- a/solution.py
+++ b/solution.py
@@ -299,14 +299,25 @@
     return pl.ds(tile, 8, stride=TILES)
 
 
-def pack_kernel(modes, start, place, background, absorb, density, profiles, adjoint, out, raw, sems):
+def pack_kernel(
+    modes, start, place, back_arg, absorb_arg, density_arg, profiles, adjoint,
+    out, own, background, absorb, density, raw, sems,
+):
     half = SYSTEMS // 2
     copies = []
     for system in range(SYSTEMS):
         source = profiles.at[modes[system]] if system < half else adjoint.at[system - half]
         copies.append(pltpu.make_async_copy(source, raw.at[system], sems.at[system]))
-    for copy in copies:
+    held = [
+        pltpu.make_async_copy(array, room, sems.at[SYSTEMS + at])
+        for at, (array, room) in enumerate(
+            ((back_arg, background), (absorb_arg, absorb), (density_arg, density))
+        )
+    ]
+    for copy in held + copies:
         copy.start()
+    for copy in held:
+        copy.wait()
     for plane in range(2):
         where = place[0] * 2 + plane
         inside = (where >= start[0]) & (where < start[0] + SYSTEMS * SYSTEMS)
@@ -321,6 +332,8 @@
             for system in range(SYSTEMS):
                 out[system, 16 + plane * TILES + tile] = part
     share = pl.ds(pl.multiple_of(place[1] * 8, 8), 8)
+    own[0] = density[0, share]
+    own[1] = density[1, share]
     after = (place[0] + 1) % SYSTEMS
     for slab in range(SYSTEMS):
         out[slab, ROWS_AT] = jnp.where(after == slab, density[1, share], density[0, share])
@@ -448,7 +461,7 @@
 
 
 def outer_kernel(
-    place, density, block, low, high, other, inner, inner_diag, inner_acc, basis, gram, dens, diag, acc
+    place, block, low, high, other, inner, inner_diag, inner_acc, basis, gram, dens, diag, acc
 ):
     core = place[1] % 2
 
@@ -484,13 +497,10 @@
     acc[...] = inner_acc[...]
 
     me = place[0] % SYSTEMS
-    share = pl.ds(pl.multiple_of(place[1] * 8, 8), 8)
     dens[0] = jnp.where(
         me > 0, block[jnp.maximum(me - 1, 0), ROWS_AT], low[SYSTEMS // 2 - 1, ROWS_AT]
     )
-    dens[1] = density[0, share]
-    dens[2] = density[1, share]
-    dens[3] = jnp.where(
+    dens[1] = jnp.where(
         me < SYSTEMS - 1, block[jnp.minimum(me + 1, SYSTEMS - 1), ROWS_AT], high[0, ROWS_AT]
     )
 
@@ -574,7 +584,7 @@
                     adjoint[port, part, plane, rows_of(tile)] = fields[half + port, at]
 
 
-def terms_kernel(place, fields, keep, give, natural):
+def terms_kernel(place, fields, mine, beside, across, natural):
     half = SYSTEMS // 2
     for plane in range(4):
         for tile in range(TILES):
@@ -588,30 +598,27 @@
     flag = fields[0, 32]
     for system in range(1, SYSTEMS):
         flag = flag + fields[system, 32]
-    core = place[1] % 2
-    for out, side in ((keep, core), (give, 1 - core)):
-        for pair in range(2):
-            rows = pl.ds(pl.multiple_of((2 * pair + side) * 8, 8), 8)
-            for plane in range(4):
-                out[pair, plane] = natural[plane, rows]
-            out[pair, 4] = flag
-
-
-def pair_kernel(place, mine, other, keep, give):
-    own = place[1] // 2
-    for at in range(5):
-        keep[at] = mine[own, at] + other[own, at]
-        give[at] = mine[1 - own, at] + other[1 - own, at]
-
-
-def density_kernel(start, place, mine, other, dens, out, flag):
+    core, chip = place[1] % 2, place[1] // 2
+    for out, pair, side in (
+        (mine, chip, core),
+        (beside, chip, 1 - core),
+        (across.at[0], 1 - chip, core),
+        (across.at[1], 1 - chip, 1 - core),
+    ):
+        rows = pl.ds(pl.multiple_of((2 * pair + side) * 8, 8), 8)
+        for plane in range(4):
+            out[plane] = natural[plane, rows]
+        out[4] = flag
+
+
+def density_kernel(start, place, mine, across, beside, own, dens, out, flag):
     lane = lax.broadcasted_iota(jnp.int32, (8, 128), 1)
     updated = []
     for plane in range(4):
-        gradient = -wave_sq * (mine[plane] + other[plane])
+        gradient = -wave_sq * (mine[plane] + across[0, plane] + beside[plane])
         where = place[0] * 2 + plane - 1
         inside = (where >= start[0]) & (where < start[0] + SYSTEMS * SYSTEMS)
-        rows = dens[plane]
+        rows = (dens[0], own[0], own[1], dens[1])[plane]
         moved = jnp.clip(rows - step_size * perm_span * gradient, 0.0, 1.0)
         rows = jnp.where(inside, moved, rows)
         exists = (where >= 0) & (where < 2 * SYSTEMS * SYSTEMS)
@@ -624,7 +631,7 @@
         edge = float(np.tanh(sharpness * threshold))
         other_edge = float(np.tanh(sharpness * (1.0 - threshold)))
         out[plane] = (edge + jnp.tanh(sharpness * (filtered - threshold))) / (edge + other_edge)
-    flag[0] = jnp.max(mine[4] + other[4])
+    flag[0] = jnp.max(mine[4] + across[0, 4] + beside[4])
 
 
 def copy_kernel(count, *refs):
@@ -656,14 +663,15 @@
     place = jnp.stack([slab, lax.axis_index("group")]).astype(jnp.int32)
     planes_of = [[z * SYSTEMS + l for l in range(SYSTEMS)] for z in range(SYSTEMS)]
     columns = [[z * SYSTEMS + l for z in range(SYSTEMS)] for l in range(SYSTEMS)]
-    packed = call(
+    packed, own_rows = call(
         pack_kernel,
-        f32(SYSTEMS, BLOCK, 8, 128),
-        [SMEM, SMEM, SMEM, VMEM, VMEM, VMEM, HBM, HBM],
-        VMEM,
-        [
+        (f32(SYSTEMS, BLOCK, 8, 128), f32(2, 8, 128)),
+        [SMEM, SMEM, SMEM] + [HBM] * 5,
+        (VMEM, VMEM),
+        [pltpu.VMEM(density.shape, jnp.float32)] * 3
+        + [
             pltpu.VMEM((SYSTEMS,) + profiles.shape[1:], jnp.float32),
-            pltpu.SemaphoreType.DMA((SYSTEMS,)),
+            pltpu.SemaphoreType.DMA((SYSTEMS + 3,)),
         ],
         "pack",
     )(port_modes, design_start, place, background, absorb, density, profiles, adjoint_source)
@@ -690,13 +698,13 @@
     plane = (TILES, 8, 128)
     basis, gram, dens = call(
         outer_kernel,
-        (f32(BASIS, 2, WINDOW, *plane), f32(1, 128), f32(4, 8, 128)),
-        [SMEM] + [VMEM] * 8,
+        (f32(BASIS, 2, WINDOW, *plane), f32(1, 128), f32(2, 8, 128)),
+        [SMEM] + [VMEM] * 7,
         (VMEM, VMEM, VMEM),
         [pltpu.VMEM((2, WINDOW) + plane, jnp.float32), pltpu.VMEM((128, 8, 128), jnp.float32)],
         "outer",
         2 * 10**8,
-    )(place, density, block, low, high, ends, *inner)
+    )(place, block, low, high, ends, *inner)
     grams = lax.all_to_all(
         jnp.broadcast_to(gram[None], (SYSTEMS, 1, 128)), "zslab", 0, 0,
         axis_index_groups=columns, tiled=True,
@@ -708,27 +716,25 @@
     fields = lax.all_to_all(solved, "zslab", 0, 0, axis_index_groups=planes_of, tiled=True)
     half = f32(SYSTEMS // 2, 2, 2, 8 * TILES, 128)
     forward, adjoint = call(fields_kernel, (half, half), [VMEM], (VMEM,) * 2, (), "fields", 10**7)(fields)
-    keep, give = call(
+    mine, beside, across = call(
         terms_kernel,
-        (f32(2, 5, 8, 128), f32(2, 5, 8, 128)),
+        (f32(5, 8, 128), f32(5, 8, 128), f32(2, 5, 8, 128)),
         [SMEM, VMEM],
-        (VMEM,) * 2,
+        (VMEM,) * 3,
         [pltpu.VMEM((4, 8 * TILES, 128), jnp.float32)],
         "terms",
     )(place, fields)
-    got = lax.ppermute(give, "group", [(i, i ^ 1) for i in range(4)])
-    keep, give = call(
-        pair_kernel, (f32(5, 8, 128), f32(5, 8, 128)), [SMEM, VMEM, VMEM], (VMEM, VMEM), (), "pair"
-    )(place, keep, got)
-    got = lax.ppermute(give, "group", [(i, i ^ 2) for i in range(4)])
+    across = lax.ppermute(across, "group", [(i, i ^ 2) for i in range(4)])
+    across, forward, adjoint = lax.optimization_barrier((across, forward, adjoint))
+    beside = lax.ppermute(beside + across[1], "group", swap)
     new_density, flag = call(
         density_kernel,
         (f32(2, 8, 128), f32(1)),
-        [SMEM, SMEM, VMEM, VMEM, VMEM],
+        [SMEM, SMEM] + [VMEM] * 5,
         (VMEM, SMEM),
         (),
         "density",
-    )(design_start, place, keep, got, dens)
+    )(design_start, place, mine, across, beside, own_rows, dens)
 
     def again(state):
         held = (background, absorb, density, profiles, adjoint_source)

time: 90.7 us -> 91.3 us (level)
  starting transfers between devices: 16.8 us -> 17.9 us
    ppermute x2, starting transfers between devices: 5.47 us -> 6.54 us  [the longest x1 4 us: on_device(): beside = lax.ppermute(beside + across[1], 'group', swap)]
    pallas_call x5 -> x4, Pallas kernels: 10.6 us -> 9.97 us  [the longest x1 6.24 us: on_device(): call(outer_kernel, (f32(BASIS, 2, WINDOW, *plane), f32(1, 128), f32(2, 8,...]
where the time goes in v7:
time: 91.3 us; the launch traced here: 91 us
  blocking collectives  51.1 us (56%)
  starting transfers between devices  17.9 us (20%)
  Pallas kernels  15.1 us (17%)
  waiting for transfers between devices  4.25 us (5%)
  between operations  1.6 us (2%)
    all_to_all x1, blocking collectives, on_device(): lax.all_to_all(packed, 'zslab', 0, 0, axis_index_groups=planes_of, tiled=...  18 us
    all_to_all x1, blocking collectives, on_device(): lax.all_to_all(solved, 'zslab', 0, 0, axis_index_groups=planes_of, tiled=...  16.8 us
    all_to_all x1, blocking collectives, on_device(): lax.all_to_all(jnp.broadcast_to(gram[None], (SYSTEMS, 1, 128)), 'zslab',...  16.3 us
    pallas_call x1, Pallas kernels, on_device(): call(outer_kernel, (f32(BASIS, 2, WINDOW, *plane), f32(1, 128), f32(2, 8,...  6.24 us
    ppermute x1, starting transfers between devices, on_device(): low = lax.ppermute(block[SYSTEMS // 2:], 'zslab', up)  4.2 us
    ppermute x1, starting transfers between devices, on_device(): beside = lax.ppermute(beside + across[1], 'group', swap)  4 us
    ppermute x1, starting transfers between devices, on_device(): ends = lax.ppermute(ends, 'group', swap)  3.16 us
    ppermute x1, starting transfers between devices, on_device(): other = lax.ppermute(block[:, 16:ROWS_AT], 'group', swap)  2.68 us
  transfers between devices with their start and end apart: 6, of which 4 were waited for; matrix products, arithmetic and copies ran while one was open for 0% of the time, Pallas kernels for 4%

profile of v7, /device:TPU:1, one launch (start us, length us, event | category | flops | bytes accessed | tf_op | source)
XLA Modules:
  0.0 91.0 jit_solution(9300478608318887896)
XLA Ops:
  1.3 0.1 pad_add_fusion.place
  1.4 1.9 %pack.1 = (f32[8,25,8,128]{3,2,1,0:T(8,128)S(1)}, f32[2,8,128]{2,1,0:T(8,128)S(1)}) custom-call(s32[4]{0:T(128)} %modes.1, s32[1]{0:T(128)S(6)} %copy.32.start, s32[2]{0:T(128)S(1)} %pad_add_fusion.place, f32[2,32,128]{2,1,0:T(8,128)} %back_arg.1, f32[2,32,128]{2,1,0:T(8,128)} %absorb_arg.1, f32[2,32,128]{2,1,0:T(8,128)} %density_arg.1, ...), custom_call_target="tpu_custom_call" | custom-call | bytes 1048576 | tf_op jit(solution)/shard_map/pack/pallas_call | solution.py:666
  3.2 18.0 %all_to_all.15.block = f32[8,25,8,128]{3,2,1,0:T(8,128)S(1)} all-to-all(f32[8,25,8,128]{3,2,1,0:T(8,128)S(1)} %get-tuple-element.90), channel_id=1, replica_groups={{0,1,2,3,4,5,6,7},{8,9,10,11,12,13,14,15},{16,17,18,19,20,21,22,23},{24..., dimensions={0} | all-to-all | bytes 1638400 | tf_op jit(solution)/shard_map/all_to_all | solution.py:678
  21.3 0.1 fusion.55
  21.3 1.3 %collective-permute-start.19 = (f32[4,25,8,128]{3,2,1,0:T(8,128)S(1)}, f32[4,25,8,128]{3,2,1,0:T(8,128)S(1)}, u32[]{:S(2)}, u32[]{:S(2)}) collective-permute-start(f32[4,25,8,128]{3,2,1,0:T(8,128)S(1)} %get-tuple-element.325), channel_id=1, source_target_pairs={{8,0},{9,1},{10,2},{11,3},{12,4},{13,5},{14,6},{15,7},{16,8},{17,9... | collective-permute-start | bytes 1228808 | tf_op jit(solution)/shard_map/ppermute | solution.py:683
  22.6 4.2 %collective-permute-start.18 = (f32[4,25,8,128]{3,2,1,0:T(8,128)S(1)}, f32[4,25,8,128]{3,2,1,0:T(8,128)S(1)}, u32[]{:S(2)}, u32[]{:S(2)}) collective-permute-start(f32[4,25,8,128]{3,2,1,0:T(8,128)S(1)} %get-tuple-element.326), channel_id=1, source_target_pairs={{0,8},{1,9},{2,10},{3,11},{4,12},{5,13},{6,14},{7,15},{8,16},{9,17... | collective-permute-start | bytes 1228808 | tf_op jit(solution)/shard_map/ppermute | solution.py:682
  26.9 2.7 %collective-permute-start.20 = (f32[8,8,8,128]{3,2,1,0:T(8,128)S(1)}, f32[8,8,8,128]{3,2,1,0:T(8,128)S(1)}, u32[]{:S(2)}, u32[]{:S(2)}) collective-permute-start(f32[8,8,8,128]{3,2,1,0:T(8,128)S(1)} %slice.712), channel_id=1, source_target_pairs={{0,64},{64,0},{128,192},{192,128},{1,65},{65,1},{129,193},{193,129... | collective-permute-start | bytes 786440 | tf_op jit(solution)/shard_map/ppermute | solution.py:685
  29.5 1.2 %collective-permute-done.20.other = f32[8,8,8,128]{3,2,1,0:T(8,128)S(1)} collective-permute-done((f32[8,8,8,128]{3,2,1,0:T(8,128)S(1)}, f32[8,8,8,128]{3,2,1,0:T(8,128)S(1)}, u32[]{:S(2)}, u32[]{:S(2)}) %collective-permute-start.20) | collective-permute-done | bytes 262176 | tf_op jit(solution)/shard_map/ppermute | solution.py:685
  30.7 2.7 %inner.1 = (f32[8,2,16,4,8,128]{5,4,3,2,1,0:T(8,128)S(1)}, f32[2,16,4,8,128]{4,3,2,1,0:T(8,128)S(1)}, f32[128,8,128]{2,1,0:T(8,128)S(1)}) custom-call(s32[2]{0:T(128)S(1)} %pad_add_fusion.place, f32[8,25,8,128]{3,2,1,0:T(8,128)S(1)} %all_to_all.15.block, f32[8,8,8,128]{3,2,1,0:T(8,128)S(1)} %collective-permute-done.20.other), custom_call_target="tpu_custom_call" | custom-call | flops 100000000 | bytes 1048576 | tf_op jit(solution)/shard_map/inner/pallas_call | solution.py:686
  33.4 0.0 copy-start
  33.5 3.2 %collective-permute-start.21 = (f32[8,8,8,128]{3,2,1,0:T(8,128)S(1)}, f32[8,8,8,128]{3,2,1,0:T(8,128)S(1)}, u32[]{:S(2)}, u32[]{:S(2)}) collective-permute-start(f32[8,8,8,128]{3,2,1,0:T(8,128)S(1)} %pad_maximum_fusion.18), channel_id=1, source_target_pairs={{0,64},{64,0},{128,192},{192,128},{1,65},{65,1},{129,193},{193,129... | collective-permute-start | bytes 786440 | tf_op jit(solution)/shard_map/ppermute | solution.py:697
  36.6 1.2 %collective-permute-done.21.other = f32[8,8,8,128]{3,2,1,0:T(8,128)S(1)} collective-permute-done((f32[8,8,8,128]{3,2,1,0:T(8,128)S(1)}, f32[8,8,8,128]{3,2,1,0:T(8,128)S(1)}, u32[]{:S(2)}, u32[]{:S(2)}) %collective-permute-start.21) | collective-permute-done | bytes 262176 | tf_op jit(solution)/shard_map/ppermute | solution.py:697
  37.8 6.2 %outer.1 = (f32[9,2,32,4,8,128]{5,4,3,2,1,0:T(8,128)S(1)}, f32[1,128]{1,0:T(1,128)S(1)}, f32[2,8,128]{2,1,0:T(8,128)S(1)}) custom-call(s32[2]{0:T(128)S(1)} %pad_add_fusion.place, f32[8,25,8,128]{3,2,1,0:T(8,128)S(1)} %all_to_all.15.block, f32[4,25,8,128]{3,2,1,0:T(8,128)S(1)} %collective-permute-done.18.low, ...), custom_call_target="tpu_custom_call" | custom-call | flops 200000000 | bytes 1048576 | tf_op jit(solution)/shard_map/outer/pallas_call | solution.py:699
  44.0 16.3 %all_to_all.16.grams = f32[8,1,128]{2,1,0:T(1,128)S(1)} all-to-all(f32[8,1,128]{2,1,0:T(1,128)S(1)} %broadcast_in_dim.18), channel_id=1, replica_groups={{0,8,16,24,32,40,48,56},{1,9,17,25,33,41,49,57},{2,10,18,26,34,42,50,58..., dimensions={0} | all-to-all | bytes 8192 | tf_op jit(solution)/shard_map/all_to_all | solution.py:708
  60.4 1.6 %combine.1 = f32[8,33,8,128]{3,2,1,0:T(8,128)S(1)} custom-call(f32[8,1,128]{2,1,0:T(1,128)S(1)} %all_to_all.16.grams, f32[304,128]{1,0:T(8,128)S(1)} %copy-done, f32[288,128]{1,0:T(8,128)S(1)} %copy-done.1, f32[9,2,32,4,8,128]{5,4,3,2,1,0:T(8,128)S(1)} %get-tuple-element.100.basis), custom_call_target="tpu_custom_call" | custom-call | bytes 1048576 | tf_op jit(solution)/shard_map/combine/pallas_call | solution.py:713
  62.0 16.8 %all_to_all.17.fields = f32[8,33,8,128]{3,2,1,0:T(8,128)S(1)} all-to-all(f32[8,33,8,128]{3,2,1,0:T(8,128)S(1)} %combine.1), channel_id=1, replica_groups={{0,1,2,3,4,5,6,7},{8,9,10,11,12,13,14,15},{16,17,18,19,20,21,22,23},{24..., dimensions={0} | all-to-all | bytes 2162688 | tf_op jit(solution)/shard_map/all_to_all | solution.py:716
  78.8 0.6 terms.1
  79.4 2.5 %collective-permute-start.22 = (f32[2,5,8,128]{3,2,1,0:T(8,128)S(1)}, f32[2,5,8,128]{3,2,1,0:T(8,128)S(1)}, u32[]{:S(2)}, u32[]{:S(2)}) collective-permute-start(f32[2,5,8,128]{3,2,1,0:T(8,128)S(1)} %get-tuple-element.102), channel_id=1, source_target_pairs={{0,128},{64,192},{128,0},{192,64},{1,129},{65,193},{129,1},{193,65... | collective-permute-start | bytes 122888 | tf_op jit(solution)/shard_map/ppermute | solution.py:727
  81.9 0.8 fields.1
  82.7 1.1 %collective-permute-done.22.across = f32[2,5,8,128]{3,2,1,0:T(8,128)S(1)} collective-permute-done((f32[2,5,8,128]{3,2,1,0:T(8,128)S(1)}, f32[2,5,8,128]{3,2,1,0:T(8,128)S(1)}, u32[]{:S(2)}, u32[]{:S(2)}) %collective-permute-start.22) | collective-permute-done | bytes 40992 | tf_op jit(solution)/shard_map/ppermute | solution.py:727
  83.8 4.0 %collective-permute-start.23 = (f32[5,8,128]{2,1,0:T(8,128)S(1)}, f32[5,8,128]{2,1,0:T(8,128)S(1)}, u32[]{:S(2)}, u32[]{:S(2)}) collective-permute-start(f32[5,8,128]{2,1,0:T(8,128)S(1)} %bitcast_add_fusion), channel_id=1, source_target_pairs={{0,64},{64,0},{128,192},{192,128},{1,65},{65,1},{129,193},{193,129... | collective-permute-start | bytes 61448 | tf_op jit(solution)/shard_map/ppermute | solution.py:729
  87.8 0.8 collective-permute-done.23.beside
  88.7 1.2 %density.1 = (f32[2,8,128]{2,1,0:T(8,128)}, f32[1]{0:T(128)}) custom-call(s32[1]{0:T(128)S(6)} %copy.32.start, s32[2]{0:T(128)S(1)} %pad_add_fusion.place, f32[5,8,128]{2,1,0:T(8,128)S(1)} %get-tuple-element.101.mine, f32[2,5,8,128]{3,2,1,0:T(8,128)S(1)} %collective-permute-done.22.across, f32[5,8,128]{2,1,0:T(8,128)S(1)} %collective-permute-done.23.beside, ...), custom_call_target="tpu_custom_call" | custom-call | bytes 1048576 | tf_op jit(solution)/shard_map/density/pallas_call | solution.py:730
  89.9 0.9 while.13
  (13 shorter events, 0.1 us)
Async XLA Ops:
  21.3 12.0 %collective-permute-start.19 = (f32[4,25,8,128]{3,2,1,0:T(8,128)S(1)}, f32[4,25,8,128]{3,2,1,0:T(8,128)S(1)}, u32[]{:S(2)}, u32[]{:S(2)}) collective-permute-start(f32[4,25,8,128]{3,2,1,0:T(8,128)S(1)} %get-tuple-element.325), channel_id=1, source_target_pairs={{8,0},{9,1},{10,2},{11,3},{12,4},{13,5},{14,6},{15,7},{16,8},{17,9... | collective-permute-start | bytes 1228808 | tf_op jit(solution)/shard_map/ppermute | solution.py:683
  22.6 10.8 %collective-permute-start.18 = (f32[4,25,8,128]{3,2,1,0:T(8,128)S(1)}, f32[4,25,8,128]{3,2,1,0:T(8,128)S(1)}, u32[]{:S(2)}, u32[]{:S(2)}) collective-permute-start(f32[4,25,8,128]{3,2,1,0:T(8,128)S(1)} %get-tuple-element.326), channel_id=1, source_target_pairs={{0,8},{1,9},{2,10},{3,11},{4,12},{5,13},{6,14},{7,15},{8,16},{9,17... | collective-permute-start | bytes 1228808 | tf_op jit(solution)/shard_map/ppermute | solution.py:682
  26.9 3.8 %collective-permute-start.20 = (f32[8,8,8,128]{3,2,1,0:T(8,128)S(1)}, f32[8,8,8,128]{3,2,1,0:T(8,128)S(1)}, u32[]{:S(2)}, u32[]{:S(2)}) collective-permute-start(f32[8,8,8,128]{3,2,1,0:T(8,128)S(1)} %slice.712), channel_id=1, source_target_pairs={{0,64},{64,0},{128,192},{192,128},{1,65},{65,1},{129,193},{193,129... | collective-permute-start | bytes 786440 | tf_op jit(solution)/shard_map/ppermute | solution.py:685
  33.4 26.9 %copy-start = (f32[304,128]{1,0:T(8,128)S(1)}, f32[304,128]{1,0:T(8,128)}, u32[]{:S(2)}) copy-start(f32[304,128]{1,0:T(8,128)} %constant.66.clone.pick) | copy-start | bytes 466948
  33.5 26.9 %copy-start.1 = (f32[288,128]{1,0:T(8,128)S(1)}, f32[288,128]{1,0:T(8,128)}, u32[]{:S(2)}) copy-start(f32[288,128]{1,0:T(8,128)} %constant.67.clone.nudge) | copy-start | bytes 442372
  33.5 4.3 %collective-permute-start.21 = (f32[8,8,8,128]{3,2,1,0:T(8,128)S(1)}, f32[8,8,8,128]{3,2,1,0:T(8,128)S(1)}, u32[]{:S(2)}, u32[]{:S(2)}) collective-permute-start(f32[8,8,8,128]{3,2,1,0:T(8,128)S(1)} %pad_maximum_fusion.18), channel_id=1, source_target_pairs={{0,64},{64,0},{128,192},{192,128},{1,65},{65,1},{129,193},{193,129... | collective-permute-start | bytes 786440 | tf_op jit(solution)/shard_map/ppermute | solution.py:697
  62.0 27.9 %copy-start.20 = (f32[2,32,128]{2,1,0:T(8,128)S(1)}, f32[2,32,128]{2,1,0:T(8,128)}, u32[]{:S(2)}) copy-start(f32[2,32,128]{2,1,0:T(8,128)} %back_arg.1) | copy-start | bytes 98308
  79.4 4.4 %collective-permute-start.22 = (f32[2,5,8,128]{3,2,1,0:T(8,128)S(1)}, f32[2,5,8,128]{3,2,1,0:T(8,128)S(1)}, u32[]{:S(2)}, u32[]{:S(2)}) collective-permute-start(f32[2,5,8,128]{3,2,1,0:T(8,128)S(1)} %get-tuple-element.102), channel_id=1, source_target_pairs={{0,128},{64,192},{128,0},{192,64},{1,129},{65,193},{129,1},{193,65... | collective-permute-start | bytes 122888 | tf_op jit(solution)/shard_map/ppermute | solution.py:727
  83.8 4.8 %collective-permute-start.23 = (f32[5,8,128]{2,1,0:T(8,128)S(1)}, f32[5,8,128]{2,1,0:T(8,128)S(1)}, u32[]{:S(2)}, u32[]{:S(2)}) collective-permute-start(f32[5,8,128]{2,1,0:T(8,128)S(1)} %bitcast_add_fusion), channel_id=1, source_target_pairs={{0,64},{64,0},{128,192},{192,128},{1,65},{65,1},{129,193},{193,129... | collective-permute-start | bytes 61448 | tf_op jit(solution)/shard_map/ppermute | solution.py:729

commit v8 on v7

--- a/solution.py
+++ b/solution.py
@@ -300,10 +300,11 @@
 
 
 def pack_kernel(
-    modes, start, place, back_arg, absorb_arg, density_arg, profiles, adjoint,
+    modes, start, back_arg, absorb_arg, density_arg, profiles, adjoint,
     out, own, background, absorb, density, raw, sems,
 ):
     half = SYSTEMS // 2
+    place = slab_and_group()
     copies = []
     for system in range(SYSTEMS):
         source = profiles.at[modes[system]] if system < half else adjoint.at[system - half]
@@ -334,6 +335,7 @@
     share = pl.ds(pl.multiple_of(place[1] * 8, 8), 8)
     own[0] = density[0, share]
     own[1] = density[1, share]
+    own[2] = jnp.full((8, 128), start[0]).astype(jnp.float32)
     after = (place[0] + 1) % SYSTEMS
     for slab in range(SYSTEMS):
         out[slab, ROWS_AT] = jnp.where(after == slab, density[1, share], density[0, share])
@@ -347,6 +349,10 @@
                     ]
 
 
+def slab_and_group():
+    return lax.axis_index("zslab"), lax.axis_index("group")
+
+
 class Stencil:
     def __init__(self):
         row = lax.broadcasted_iota(jnp.int32, (8, 128), 0)
@@ -366,22 +372,26 @@
             sums.append((z_sum + (rows[tile] + rows[tile + 2])) + (left + right))
         return sums
 
-    def step(self, basis, diag, level, at, third):
-        def plane(part, where):
-            return [basis[level, part, where, tile] for tile in range(TILES)]
-
-        real, imag = plane(0, at), plane(1, at)
-        near_re = self.beside(plane(0, at - 1), real, plane(0, at + 1))
-        near_im = self.beside(plane(1, at - 1), imag, plane(1, at + 1))
-        for tile in range(TILES):
-            diag_re, diag_im = diag[0, at, tile], diag[1, at, tile]
-            new_re = diag_re * real[tile] - diag_im * imag[tile] - third * near_re[tile]
-            new_im = diag_re * imag[tile] + diag_im * real[tile] - third * near_im[tile]
-            if level > 0:
-                new_re = new_re - basis[level - 1, 0, at, tile]
-                new_im = new_im - basis[level - 1, 1, at, tile]
-            basis[level + 1, 0, at, tile] = new_re
-            basis[level + 1, 1, at, tile] = new_im
+    def run(self, basis, diag, level, first, last, third_of):
+        def load(at):
+            return [[basis[level, part, at, tile] for tile in range(TILES)] for part in range(2)]
+
+        below, here = load(first - 1), load(first)
+        for at in range(first, last):
+            above = load(at + 1)
+            third = third_of(at)
+            near = [self.beside(below[part], here[part], above[part]) for part in range(2)]
+            for tile in range(TILES):
+                diag_re, diag_im = diag[0, at, tile], diag[1, at, tile]
+                real, imag = here[0][tile], here[1][tile]
+                new_re = diag_re * real - diag_im * imag - third * near[0][tile]
+                new_im = diag_re * imag + diag_im * real - third * near[1][tile]
+                if level > 0:
+                    new_re = new_re - basis[level - 1, 0, at, tile]
+                    new_im = new_im - basis[level - 1, 1, at, tile]
+                basis[level + 1, 0, at, tile] = new_re
+                basis[level + 1, 1, at, tile] = new_im
+            below, here = here, above
 
 
 def gram_pass(basis, acc, columns, ranges, shift):
@@ -409,13 +419,14 @@
     for first, last in ranges:
         sums = lax.fori_loop(
             0, (last - first) * TILES, functools.partial(position, first=first), sums,
-            unroll=TILES,
+            unroll=8,
         )
     for at, value in zip(places, sums):
         acc[at] = value
 
 
-def inner_kernel(place, block, other, basis, diag, acc):
+def inner_kernel(block, other, basis, diag, acc):
+    place = slab_and_group()
     core = place[1] % 2
 
     def load(chunk, _):
@@ -433,14 +444,7 @@
     lax.fori_loop(0, SYSTEMS, load, 0, unroll=SYSTEMS)
     stencil = Stencil()
     for level in range(SYSTEMS - 1):
-
-        def plane_step(at, _, level=level):
-            stencil.step(basis, diag, level, at, THIRD)
-            return 0
-
-        lax.fori_loop(
-            level + 1, OWN - 1 - level, plane_step, 0, unroll=OWN - 2 - 2 * level
-        )
+        stencil.run(basis, diag, level, level + 1, OWN - 1 - level, lambda at: THIRD)
     acc[...] = jnp.zeros_like(acc)
     for columns, ranges in INNER_PASSES:
         gram_pass(basis, acc, columns, ranges, 0)
@@ -461,8 +465,9 @@
 
 
 def outer_kernel(
-    place, block, low, high, other, inner, inner_diag, inner_acc, basis, gram, dens, diag, acc
+    block, low, high, other, inner, inner_diag, inner_acc, basis, gram, dens, diag, acc
 ):
+    place = slab_and_group()
     core = place[1] % 2
 
     def load(source, first, at):
@@ -508,16 +513,15 @@
     third_high = jnp.where(place[0] < SYSTEMS * (SYSTEMS - 1), THIRD, 0.0)
     stencil = Stencil()
     for level in range(BASIS - 1):
-
-        def two_planes(step, _, level=level):
-            lower, upper = level + 1 + step, WINDOW - 2 - level - step
-            stencil.step(basis, diag, level, lower, jnp.where(lower < CORE, third_low, THIRD))
-            stencil.step(
-                basis, diag, level, upper, jnp.where(upper >= CORE + OWN, third_high, THIRD)
-            )
-            return 0
-
-        lax.fori_loop(0, CORE, two_planes, 0, unroll=CORE)
+        lower, upper = level + 1, WINDOW - 1 - level
+        stencil.run(
+            basis, diag, level, lower, lower + CORE,
+            lambda at: third_low if at < CORE else THIRD,
+        )
+        stencil.run(
+            basis, diag, level, upper - CORE, upper,
+            lambda at: third_high if at >= CORE + OWN else THIRD,
+        )
     for columns, ranges in OUTER_PASSES:
         gram_pass(basis, acc, columns, ranges, CORE)
     by_pair = jnp.sum(acc[...], axis=1)
@@ -584,7 +588,7 @@
                     adjoint[port, part, plane, rows_of(tile)] = fields[half + port, at]
 
 
-def terms_kernel(place, fields, mine, beside, across, natural):
+def terms_kernel(fields, mine, beside, across, natural):
     half = SYSTEMS // 2
     for plane in range(4):
         for tile in range(TILES):
@@ -598,7 +602,8 @@
     flag = fields[0, 32]
     for system in range(1, SYSTEMS):
         flag = flag + fields[system, 32]
-    core, chip = place[1] % 2, place[1] // 2
+    group = slab_and_group()[1]
+    core, chip = group % 2, group // 2
     for out, pair, side in (
         (mine, chip, core),
         (beside, chip, 1 - core),
@@ -611,13 +616,14 @@
         out[4] = flag
 
 
-def density_kernel(start, place, mine, across, beside, own, dens, out, flag):
+def density_kernel(mine, across, beside, own, dens, out, flag):
     lane = lax.broadcasted_iota(jnp.int32, (8, 128), 1)
     updated = []
     for plane in range(4):
         gradient = -wave_sq * (mine[plane] + across[0, plane] + beside[plane])
-        where = place[0] * 2 + plane - 1
-        inside = (where >= start[0]) & (where < start[0] + SYSTEMS * SYSTEMS)
+        where = slab_and_group()[0] * 2 + plane - 1
+        depth = where.astype(jnp.float32) - own[2]
+        inside = (depth >= 0.0) & (depth < SYSTEMS * SYSTEMS)
         rows = (dens[0], own[0], own[1], dens[1])[plane]
         moved = jnp.clip(rows - step_size * perm_span * gradient, 0.0, 1.0)
         rows = jnp.where(inside, moved, rows)
@@ -659,14 +665,12 @@
 
 
 def on_device(background, absorb, density, profiles, adjoint_source, port_modes, design_start):
-    slab = lax.axis_index("zslab")
-    place = jnp.stack([slab, lax.axis_index("group")]).astype(jnp.int32)
     planes_of = [[z * SYSTEMS + l for l in range(SYSTEMS)] for z in range(SYSTEMS)]
     columns = [[z * SYSTEMS + l for z in range(SYSTEMS)] for l in range(SYSTEMS)]
     packed, own_rows = call(
         pack_kernel,
-        (f32(SYSTEMS, BLOCK, 8, 128), f32(2, 8, 128)),
-        [SMEM, SMEM, SMEM] + [HBM] * 5,
+        (f32(SYSTEMS, BLOCK, 8, 128), f32(3, 8, 128)),
+        [SMEM, SMEM] + [HBM] * 5,
         (VMEM, VMEM),
         [pltpu.VMEM(density.shape, jnp.float32)] * 3
         + [
@@ -674,7 +678,7 @@
             pltpu.SemaphoreType.DMA((SYSTEMS + 3,)),
         ],
         "pack",
-    )(port_modes, design_start, place, background, absorb, density, profiles, adjoint_source)
+    )(port_modes, design_start, background, absorb, density, profiles, adjoint_source)
     block = lax.all_to_all(packed, "zslab", 0, 0, axis_index_groups=planes_of, tiled=True)
     count = SYSTEMS * SYSTEMS
     up = [(i, i + SYSTEMS) for i in range(count - SYSTEMS)]
@@ -686,12 +690,12 @@
     inner = call(
         inner_kernel,
         (f32(SYSTEMS, 2, OWN, TILES, 8, 128), f32(2, OWN, TILES, 8, 128), f32(128, 8, 128)),
-        [SMEM, VMEM, VMEM],
+        [VMEM, VMEM],
         (VMEM,) * 3,
         (),
         "inner",
         10**8,
-    )(place, block, other)
+    )(block, other)
     low, high, inner = lax.optimization_barrier((low, high, inner))
     ends = jnp.concatenate([low[:, 16:ROWS_AT], high[:, 16:ROWS_AT]], axis=0)
     ends = lax.ppermute(ends, "group", swap)
@@ -699,12 +703,12 @@
     basis, gram, dens = call(
         outer_kernel,
         (f32(BASIS, 2, WINDOW, *plane), f32(1, 128), f32(2, 8, 128)),
-        [SMEM] + [VMEM] * 7,
+        [VMEM] * 7,
         (VMEM, VMEM, VMEM),
         [pltpu.VMEM((2, WINDOW) + plane, jnp.float32), pltpu.VMEM((128, 8, 128), jnp.float32)],
         "outer",
         2 * 10**8,
-    )(place, block, low, high, ends, *inner)
+    )(block, low, high, ends, *inner)
     grams = lax.all_to_all(
         jnp.broadcast_to(gram[None], (SYSTEMS, 1, 128)), "zslab", 0, 0,
         axis_index_groups=columns, tiled=True,
@@ -719,22 +723,22 @@
     mine, beside, across = call(
         terms_kernel,
         (f32(5, 8, 128), f32(5, 8, 128), f32(2, 5, 8, 128)),
-        [SMEM, VMEM],
+        [VMEM],
         (VMEM,) * 3,
         [pltpu.VMEM((4, 8 * TILES, 128), jnp.float32)],
         "terms",
-    )(place, fields)
+    )(fields)
     across = lax.ppermute(across, "group", [(i, i ^ 2) for i in range(4)])
     across, forward, adjoint = lax.optimization_barrier((across, forward, adjoint))
     beside = lax.ppermute(beside + across[1], "group", swap)
     new_density, flag = call(
         density_kernel,
         (f32(2, 8, 128), f32(1)),
-        [SMEM, SMEM] + [VMEM] * 5,
+        [VMEM] * 5,
         (VMEM, SMEM),
         (),
         "density",
-    )(design_start, place, mine, across, beside, own_rows, dens)
+    )(mine, across, beside, own_rows, dens)
 
     def again(state):
         held = (background, absorb, density, profiles, adjoint_source)

time: 91.3 us -> 89.1 us (0.976)
  Pallas kernels: 15.1 us -> 12.2 us
    pallas_call x1, Pallas kernels: 6.24 us -> 5.21 us  [on_device(): call(outer_kernel, (f32(BASIS, 2, WINDOW, *plane), f32(1, 128), f32(2, 8,...]
  transfers between devices with their start and end apart: 6 -> 6, of which waited for: 4 -> 5; matrix products, arithmetic and copies ran while one was open for 0% -> 0% of each run, Pallas kernels for 4% -> 3%
where the time goes in v8:
time: 89.1 us; the launch traced here: 88.8 us
  blocking collectives  51.1 us (57%)
  starting transfers between devices  18 us (20%)
  Pallas kernels  12.2 us (14%)
  waiting for transfers between devices  4.86 us (5%)
  between operations  1.58 us (2%)
    all_to_all x1, blocking collectives, on_device(): lax.all_to_all(packed, 'zslab', 0, 0, axis_index_groups=planes_of, tiled=...  18 us
    all_to_all x1, blocking collectives, on_device(): lax.all_to_all(solved, 'zslab', 0, 0, axis_index_groups=planes_of, tiled=...  16.8 us
    all_to_all x1, blocking collectives, on_device(): lax.all_to_all(jnp.broadcast_to(gram[None], (SYSTEMS, 1, 128)), 'zslab',...  16.3 us
    pallas_call x1, Pallas kernels, on_device(): call(outer_kernel, (f32(BASIS, 2, WINDOW, *plane), f32(1, 128), f32(2, 8,...  5.21 us
    ppermute x1, starting transfers between devices, on_device(): low = lax.ppermute(block[SYSTEMS // 2:], 'zslab', up)  4.2 us
    ppermute x1, starting transfers between devices, on_device(): beside = lax.ppermute(beside + across[1], 'group', swap)  3.99 us
    ppermute x1, starting transfers between devices, on_device(): ends = lax.ppermute(ends, 'group', swap)  3.33 us
    ppermute x1, starting transfers between devices, on_device(): other = lax.ppermute(block[:, 16:ROWS_AT], 'group', swap)  2.68 us
  transfers between devices with their start and end apart: 6, of which 5 were waited for; matrix products, arithmetic and copies ran while one was open for 0% of the time, Pallas kernels for 3%

profile of v8, /device:TPU:1, one launch (start us, length us, event | category | flops | bytes accessed | tf_op | source)
XLA Modules:
  0.0 88.8 jit_solution(1942279752586191225)
XLA Ops:
  1.3 1.9 %pack.1 = (f32[8,25,8,128]{3,2,1,0:T(8,128)S(1)}, f32[3,8,128]{2,1,0:T(8,128)S(1)}) custom-call(s32[4]{0:T(128)} %modes.1, s32[1]{0:T(128)S(6)} %copy.32.start, f32[2,32,128]{2,1,0:T(8,128)} %back_arg.1, f32[2,32,128]{2,1,0:T(8,128)} %absorb_arg.1, f32[2,32,128]{2,1,0:T(8,128)} %density_arg.1, f32[6,2,2,32,128]{4,3,2,1,0:T(8,128)} %profiles.1, ...), custom_call_target="tpu_custom_call" | custom-call | bytes 1048576 | tf_op jit(solution)/shard_map/pack/pallas_call | solution.py:670
  3.2 18.0 %all_to_all.15.block = f32[8,25,8,128]{3,2,1,0:T(8,128)S(1)} all-to-all(f32[8,25,8,128]{3,2,1,0:T(8,128)S(1)} %get-tuple-element.90), channel_id=1, replica_groups={{0,1,2,3,4,5,6,7},{8,9,10,11,12,13,14,15},{16,17,18,19,20,21,22,23},{24..., dimensions={0} | all-to-all | bytes 1638400 | tf_op jit(solution)/shard_map/all_to_all | solution.py:682
  21.2 0.1 fusion.55
  21.2 1.3 %collective-permute-start.19 = (f32[4,25,8,128]{3,2,1,0:T(8,128)S(1)}, f32[4,25,8,128]{3,2,1,0:T(8,128)S(1)}, u32[]{:S(2)}, u32[]{:S(2)}) collective-permute-start(f32[4,25,8,128]{3,2,1,0:T(8,128)S(1)} %get-tuple-element.325), channel_id=1, source_target_pairs={{8,0},{9,1},{10,2},{11,3},{12,4},{13,5},{14,6},{15,7},{16,8},{17,9... | collective-permute-start | bytes 1228808 | tf_op jit(solution)/shard_map/ppermute | solution.py:687
  22.5 4.2 %collective-permute-start.18 = (f32[4,25,8,128]{3,2,1,0:T(8,128)S(1)}, f32[4,25,8,128]{3,2,1,0:T(8,128)S(1)}, u32[]{:S(2)}, u32[]{:S(2)}) collective-permute-start(f32[4,25,8,128]{3,2,1,0:T(8,128)S(1)} %get-tuple-element.326), channel_id=1, source_target_pairs={{0,8},{1,9},{2,10},{3,11},{4,12},{5,13},{6,14},{7,15},{8,16},{9,17... | collective-permute-start | bytes 1228808 | tf_op jit(solution)/shard_map/ppermute | solution.py:686
  26.8 2.7 %collective-permute-start.20 = (f32[8,8,8,128]{3,2,1,0:T(8,128)S(1)}, f32[8,8,8,128]{3,2,1,0:T(8,128)S(1)}, u32[]{:S(2)}, u32[]{:S(2)}) collective-permute-start(f32[8,8,8,128]{3,2,1,0:T(8,128)S(1)} %slice.712), channel_id=1, source_target_pairs={{0,64},{64,0},{128,192},{192,128},{1,65},{65,1},{129,193},{193,129... | collective-permute-start | bytes 786440 | tf_op jit(solution)/shard_map/ppermute | solution.py:689
  29.5 1.2 %collective-permute-done.20.other = f32[8,8,8,128]{3,2,1,0:T(8,128)S(1)} collective-permute-done((f32[8,8,8,128]{3,2,1,0:T(8,128)S(1)}, f32[8,8,8,128]{3,2,1,0:T(8,128)S(1)}, u32[]{:S(2)}, u32[]{:S(2)}) %collective-permute-start.20) | collective-permute-done | bytes 262176 | tf_op jit(solution)/shard_map/ppermute | solution.py:689
  30.6 1.9 %inner.1 = (f32[8,2,16,4,8,128]{5,4,3,2,1,0:T(8,128)S(1)}, f32[2,16,4,8,128]{4,3,2,1,0:T(8,128)S(1)}, f32[128,8,128]{2,1,0:T(8,128)S(1)}) custom-call(f32[8,25,8,128]{3,2,1,0:T(8,128)S(1)} %all_to_all.15.block, f32[8,8,8,128]{3,2,1,0:T(8,128)S(1)} %collective-permute-done.20.other), custom_call_target="tpu_custom_call" | custom-call | flops 100000000 | bytes 1048576 | tf_op jit(solution)/shard_map/inner/pallas_call | solution.py:690
  32.5 0.6 collective-permute-done.18.low
  33.2 0.0 copy-start
  33.2 3.3 %collective-permute-start.21 = (f32[8,8,8,128]{3,2,1,0:T(8,128)S(1)}, f32[8,8,8,128]{3,2,1,0:T(8,128)S(1)}, u32[]{:S(2)}, u32[]{:S(2)}) collective-permute-start(f32[8,8,8,128]{3,2,1,0:T(8,128)S(1)} %pad_maximum_fusion.18), channel_id=1, source_target_pairs={{0,64},{64,0},{128,192},{192,128},{1,65},{65,1},{129,193},{193,129... | collective-permute-start | bytes 786440 | tf_op jit(solution)/shard_map/ppermute | solution.py:701
  36.6 1.2 %collective-permute-done.21.other = f32[8,8,8,128]{3,2,1,0:T(8,128)S(1)} collective-permute-done((f32[8,8,8,128]{3,2,1,0:T(8,128)S(1)}, f32[8,8,8,128]{3,2,1,0:T(8,128)S(1)}, u32[]{:S(2)}, u32[]{:S(2)}) %collective-permute-start.21) | collective-permute-done | bytes 262176 | tf_op jit(solution)/shard_map/ppermute | solution.py:701
  37.7 5.2 %outer.1 = (f32[9,2,32,4,8,128]{5,4,3,2,1,0:T(8,128)S(1)}, f32[1,128]{1,0:T(1,128)S(1)}, f32[2,8,128]{2,1,0:T(8,128)S(1)}) custom-call(f32[8,25,8,128]{3,2,1,0:T(8,128)S(1)} %all_to_all.15.block, f32[4,25,8,128]{3,2,1,0:T(8,128)S(1)} %collective-permute-done.18.low, f32[4,25,8,128]{3,2,1,0:T(8,128)S(1)} %collective-permute-done.19.high, ...), custom_call_target="tpu_custom_call" | custom-call | flops 200000000 | bytes 1048576 | tf_op jit(solution)/shard_map/outer/pallas_call | solution.py:703
  42.9 16.3 %all_to_all.16.grams = f32[8,1,128]{2,1,0:T(1,128)S(1)} all-to-all(f32[8,1,128]{2,1,0:T(1,128)S(1)} %broadcast_in_dim.18), channel_id=1, replica_groups={{0,8,16,24,32,40,48,56},{1,9,17,25,33,41,49,57},{2,10,18,26,34,42,50,58..., dimensions={0} | all-to-all | bytes 8192 | tf_op jit(solution)/shard_map/all_to_all | solution.py:712
  59.3 1.6 %combine.1 = f32[8,33,8,128]{3,2,1,0:T(8,128)S(1)} custom-call(f32[8,1,128]{2,1,0:T(1,128)S(1)} %all_to_all.16.grams, f32[304,128]{1,0:T(8,128)S(1)} %copy-done, f32[288,128]{1,0:T(8,128)S(1)} %copy-done.1, f32[9,2,32,4,8,128]{5,4,3,2,1,0:T(8,128)S(1)} %get-tuple-element.100.basis), custom_call_target="tpu_custom_call" | custom-call | bytes 1048576 | tf_op jit(solution)/shard_map/combine/pallas_call | solution.py:717
  60.9 16.8 %all_to_all.17.fields = f32[8,33,8,128]{3,2,1,0:T(8,128)S(1)} all-to-all(f32[8,33,8,128]{3,2,1,0:T(8,128)S(1)} %combine.1), channel_id=1, replica_groups={{0,1,2,3,4,5,6,7},{8,9,10,11,12,13,14,15},{16,17,18,19,20,21,22,23},{24..., dimensions={0} | all-to-all | bytes 2162688 | tf_op jit(solution)/shard_map/all_to_all | solution.py:720
  77.6 0.1 terms.1
  77.7 2.5 %collective-permute-start.22 = (f32[2,5,8,128]{3,2,1,0:T(8,128)S(1)}, f32[2,5,8,128]{3,2,1,0:T(8,128)S(1)}, u32[]{:S(2)}, u32[]{:S(2)}) collective-permute-start(f32[2,5,8,128]{3,2,1,0:T(8,128)S(1)} %get-tuple-element.102), channel_id=1, source_target_pairs={{0,128},{64,192},{128,0},{192,64},{1,129},{65,193},{129,1},{193,65... | collective-permute-start | bytes 122888 | tf_op jit(solution)/shard_map/ppermute | solution.py:731
  80.2 0.8 fields.1
  81.1 1.1 %collective-permute-done.22.across = f32[2,5,8,128]{3,2,1,0:T(8,128)S(1)} collective-permute-done((f32[2,5,8,128]{3,2,1,0:T(8,128)S(1)}, f32[2,5,8,128]{3,2,1,0:T(8,128)S(1)}, u32[]{:S(2)}, u32[]{:S(2)}) %collective-permute-start.22) | collective-permute-done | bytes 40992 | tf_op jit(solution)/shard_map/ppermute | solution.py:731
  82.2 4.0 %collective-permute-start.23 = (f32[5,8,128]{2,1,0:T(8,128)S(1)}, f32[5,8,128]{2,1,0:T(8,128)S(1)}, u32[]{:S(2)}, u32[]{:S(2)}) collective-permute-start(f32[5,8,128]{2,1,0:T(8,128)S(1)} %bitcast_add_fusion), channel_id=1, source_target_pairs={{0,64},{64,0},{128,192},{192,128},{1,65},{65,1},{129,193},{193,129... | collective-permute-start | bytes 61448 | tf_op jit(solution)/shard_map/ppermute | solution.py:733
  86.1 0.8 collective-permute-done.23.beside
  87.0 0.7 density.1
  87.7 0.9 while.13
  (12 shorter events, 0.1 us)
Async XLA Ops:
  21.2 11.3 %collective-permute-start.19 = (f32[4,25,8,128]{3,2,1,0:T(8,128)S(1)}, f32[4,25,8,128]{3,2,1,0:T(8,128)S(1)}, u32[]{:S(2)}, u32[]{:S(2)}) collective-permute-start(f32[4,25,8,128]{3,2,1,0:T(8,128)S(1)} %get-tuple-element.325), channel_id=1, source_target_pairs={{8,0},{9,1},{10,2},{11,3},{12,4},{13,5},{14,6},{15,7},{16,8},{17,9... | collective-permute-start | bytes 1228808 | tf_op jit(solution)/shard_map/ppermute | solution.py:687
  22.5 10.6 %collective-permute-start.18 = (f32[4,25,8,128]{3,2,1,0:T(8,128)S(1)}, f32[4,25,8,128]{3,2,1,0:T(8,128)S(1)}, u32[]{:S(2)}, u32[]{:S(2)}) collective-permute-start(f32[4,25,8,128]{3,2,1,0:T(8,128)S(1)} %get-tuple-element.326), channel_id=1, source_target_pairs={{0,8},{1,9},{2,10},{3,11},{4,12},{5,13},{6,14},{7,15},{8,16},{9,17... | collective-permute-start | bytes 1228808 | tf_op jit(solution)/shard_map/ppermute | solution.py:686
  26.8 3.8 %collective-permute-start.20 = (f32[8,8,8,128]{3,2,1,0:T(8,128)S(1)}, f32[8,8,8,128]{3,2,1,0:T(8,128)S(1)}, u32[]{:S(2)}, u32[]{:S(2)}) collective-permute-start(f32[8,8,8,128]{3,2,1,0:T(8,128)S(1)} %slice.712), channel_id=1, source_target_pairs={{0,64},{64,0},{128,192},{192,128},{1,65},{65,1},{129,193},{193,129... | collective-permute-start | bytes 786440 | tf_op jit(solution)/shard_map/ppermute | solution.py:689
  33.2 26.0 %copy-start = (f32[304,128]{1,0:T(8,128)S(1)}, f32[304,128]{1,0:T(8,128)}, u32[]{:S(2)}) copy-start(f32[304,128]{1,0:T(8,128)} %constant.57.clone.pick) | copy-start | bytes 466948
  33.2 26.0 %copy-start.1 = (f32[288,128]{1,0:T(8,128)S(1)}, f32[288,128]{1,0:T(8,128)}, u32[]{:S(2)}) copy-start(f32[288,128]{1,0:T(8,128)} %constant.58.clone.nudge) | copy-start | bytes 442372
  33.2 4.5 %collective-permute-start.21 = (f32[8,8,8,128]{3,2,1,0:T(8,128)S(1)}, f32[8,8,8,128]{3,2,1,0:T(8,128)S(1)}, u32[]{:S(2)}, u32[]{:S(2)}) collective-permute-start(f32[8,8,8,128]{3,2,1,0:T(8,128)S(1)} %pad_maximum_fusion.18), channel_id=1, source_target_pairs={{0,64},{64,0},{128,192},{192,128},{1,65},{65,1},{129,193},{193,129... | collective-permute-start | bytes 786440 | tf_op jit(solution)/shard_map/ppermute | solution.py:701
  60.9 26.8 %copy-start.20 = (f32[2,32,128]{2,1,0:T(8,128)S(1)}, f32[2,32,128]{2,1,0:T(8,128)}, u32[]{:S(2)}) copy-start(f32[2,32,128]{2,1,0:T(8,128)} %back_arg.1) | copy-start | bytes 98308
  77.7 4.4 %collective-permute-start.22 = (f32[2,5,8,128]{3,2,1,0:T(8,128)S(1)}, f32[2,5,8,128]{3,2,1,0:T(8,128)S(1)}, u32[]{:S(2)}, u32[]{:S(2)}) collective-permute-start(f32[2,5,8,128]{3,2,1,0:T(8,128)S(1)} %get-tuple-element.102), channel_id=1, source_target_pairs={{0,128},{64,192},{128,0},{192,64},{1,129},{65,193},{129,1},{193,65... | collective-permute-start | bytes 122888 | tf_op jit(solution)/shard_map/ppermute | solution.py:731
  82.2 4.8 %collective-permute-start.23 = (f32[5,8,128]{2,1,0:T(8,128)S(1)}, f32[5,8,128]{2,1,0:T(8,128)S(1)}, u32[]{:S(2)}, u32[]{:S(2)}) collective-permute-start(f32[5,8,128]{2,1,0:T(8,128)S(1)} %bitcast_add_fusion), channel_id=1, source_target_pairs={{0,64},{64,0},{128,192},{192,128},{1,65},{65,1},{129,193},{193,129... | collective-permute-start | bytes 61448 | tf_op jit(solution)/shard_map/ppermute | solution.py:733

commit v9 on v8

--- a/solution.py
+++ b/solution.py
@@ -299,25 +299,18 @@
     return pl.ds(tile, 8, stride=TILES)
 
 
-def pack_kernel(
-    modes, start, back_arg, absorb_arg, density_arg, profiles, adjoint,
-    out, own, background, absorb, density, raw, sems,
-):
+def pack_kernel(*refs):
+    arguments, out, own, held, sems = refs[:7], refs[7], refs[8], refs[9:16], refs[16]
+    modes, start, background, absorb, density, profiles, adjoint = held
     half = SYSTEMS // 2
     place = slab_and_group()
-    copies = []
-    for system in range(SYSTEMS):
-        source = profiles.at[modes[system]] if system < half else adjoint.at[system - half]
-        copies.append(pltpu.make_async_copy(source, raw.at[system], sems.at[system]))
-    held = [
-        pltpu.make_async_copy(array, room, sems.at[SYSTEMS + at])
-        for at, (array, room) in enumerate(
-            ((back_arg, background), (absorb_arg, absorb), (density_arg, density))
-        )
+    copies = [
+        pltpu.make_async_copy(array, room, sems.at[at])
+        for at, (array, room) in enumerate(zip(arguments, held))
     ]
-    for copy in held + copies:
+    for copy in copies:
         copy.start()
-    for copy in held:
+    for copy in copies[:5]:
         copy.wait()
     for plane in range(2):
         where = place[0] * 2 + plane
@@ -339,14 +332,16 @@
     after = (place[0] + 1) % SYSTEMS
     for slab in range(SYSTEMS):
         out[slab, ROWS_AT] = jnp.where(after == slab, density[1, share], density[0, share])
-    for system in range(SYSTEMS):
-        copies[system].wait()
+    for copy in copies[5:]:
+        copy.wait()
+    for system in range(half):
+        mode = modes[system]
         for part in range(2):
             for plane in range(2):
                 for tile in range(TILES):
-                    out[system, (part * 2 + plane) * TILES + tile] = raw[
-                        system, part, plane, rows_of(tile)
-                    ]
+                    at = (part * 2 + plane) * TILES + tile
+                    out[system, at] = profiles[mode, part, plane, rows_of(tile)]
+                    out[half + system, at] = adjoint[system, part, plane, rows_of(tile)]
 
 
 def slab_and_group():
@@ -574,7 +569,7 @@
     for plane in range(2):
         solve_plane(CORE - 1 + plane, ((0, plane),))
         solve_plane(CORE + OWN - 1 + plane, ((SYSTEMS - 1, 2 + plane),))
-    lax.fori_loop(1, SYSTEMS, middle, 0)
+    lax.fori_loop(1, SYSTEMS, middle, 0, unroll=SYSTEMS - 1)
 
 
 def fields_kernel(fields, forward, adjoint):
@@ -670,13 +665,14 @@
     packed, own_rows = call(
         pack_kernel,
         (f32(SYSTEMS, BLOCK, 8, 128), f32(3, 8, 128)),
-        [SMEM, SMEM] + [HBM] * 5,
+        [HBM] * 7,
         (VMEM, VMEM),
-        [pltpu.VMEM(density.shape, jnp.float32)] * 3
+        [pltpu.SMEM(array.shape, array.dtype) for array in (port_modes, design_start)]
         + [
-            pltpu.VMEM((SYSTEMS,) + profiles.shape[1:], jnp.float32),
-            pltpu.SemaphoreType.DMA((SYSTEMS + 3,)),
-        ],
+            pltpu.VMEM(array.shape, array.dtype)
+            for array in (background, absorb, density, profiles, adjoint_source)
+        ]
+        + [pltpu.SemaphoreType.DMA((7,))],
         "pack",
     )(port_modes, design_start, background, absorb, density, profiles, adjoint_source)
     block = lax.all_to_all(packed, "zslab", 0, 0, axis_index_groups=planes_of, tiled=True)

time: 89.1 us -> 88.9 us (level)
  no operation moved by 1% of the time
where the time goes in v9:
time: 88.9 us; the launch traced here: 88.5 us
  blocking collectives  51.1 us (57%)
  starting transfers between devices  18 us (20%)
  Pallas kernels  12 us (13%)
  waiting for transfers between devices  4.86 us (5%)
  between operations  1.58 us (2%)
    all_to_all x1, blocking collectives, on_device(): lax.all_to_all(packed, 'zslab', 0, 0, axis_index_groups=planes_of, tiled=...  18 us
    all_to_all x1, blocking collectives, on_device(): lax.all_to_all(solved, 'zslab', 0, 0, axis_index_groups=planes_of, tiled=...  16.8 us
    all_to_all x1, blocking collectives, on_device(): lax.all_to_all(jnp.broadcast_to(gram[None], (SYSTEMS, 1, 128)), 'zslab',...  16.3 us
    pallas_call x1, Pallas kernels, on_device(): call(outer_kernel, (f32(BASIS, 2, WINDOW, *plane), f32(1, 128), f32(2, 8,...  5.21 us
    ppermute x1, starting transfers between devices, on_device(): low = lax.ppermute(block[SYSTEMS // 2:], 'zslab', up)  4.2 us
    ppermute x1, starting transfers between devices, on_device(): beside = lax.ppermute(beside + across[1], 'group', swap)  3.99 us
    ppermute x1, starting transfers between devices, on_device(): ends = lax.ppermute(ends, 'group', swap)  3.33 us
    ppermute x1, starting transfers between devices, on_device(): other = lax.ppermute(block[:, 16:ROWS_AT], 'group', swap)  2.68 us
  transfers between devices with their start and end apart: 6, of which 5 were waited for; matrix products, arithmetic and copies ran while one was open for 0% of the time, Pallas kernels for 3%

profile of v9, /device:TPU:1, one launch (start us, length us, event | category | flops | bytes accessed | tf_op | source)
XLA Modules:
  0.0 88.5 jit_solution(599945463461533863)
XLA Ops:
  1.3 1.2 %pack.1 = (f32[8,25,8,128]{3,2,1,0:T(8,128)S(1)}, f32[3,8,128]{2,1,0:T(8,128)S(1)}) custom-call(s32[4]{0:T(128)} %refs_0_.1, s32[1]{0:T(128)S(6)} %copy.32.refs_1_, f32[2,32,128]{2,1,0:T(8,128)} %refs_2_.1, f32[2,32,128]{2,1,0:T(8,128)} %refs_3_.1, f32[2,32,128]{2,1,0:T(8,128)} %refs_4_.1, f32[6,2,2,32,128]{4,3,2,1,0:T(8,128)} %refs_5_.1, ...), custom_call_target="tpu_custom_call" | custom-call | bytes 1048576 | tf_op jit(solution)/shard_map/pack/pallas_call | solution.py:665
  2.5 18.0 %all_to_all.15.block = f32[8,25,8,128]{3,2,1,0:T(8,128)S(1)} all-to-all(f32[8,25,8,128]{3,2,1,0:T(8,128)S(1)} %get-tuple-element.90), channel_id=1, replica_groups={{0,1,2,3,4,5,6,7},{8,9,10,11,12,13,14,15},{16,17,18,19,20,21,22,23},{24..., dimensions={0} | all-to-all | bytes 1638400 | tf_op jit(solution)/shard_map/all_to_all | solution.py:678
  20.5 0.1 fusion.55
  20.6 1.3 %collective-permute-start.19 = (f32[4,25,8,128]{3,2,1,0:T(8,128)S(1)}, f32[4,25,8,128]{3,2,1,0:T(8,128)S(1)}, u32[]{:S(2)}, u32[]{:S(2)}) collective-permute-start(f32[4,25,8,128]{3,2,1,0:T(8,128)S(1)} %get-tuple-element.325), channel_id=1, source_target_pairs={{8,0},{9,1},{10,2},{11,3},{12,4},{13,5},{14,6},{15,7},{16,8},{17,9... | collective-permute-start | bytes 1228808 | tf_op jit(solution)/shard_map/ppermute | solution.py:683
  21.9 4.2 %collective-permute-start.18 = (f32[4,25,8,128]{3,2,1,0:T(8,128)S(1)}, f32[4,25,8,128]{3,2,1,0:T(8,128)S(1)}, u32[]{:S(2)}, u32[]{:S(2)}) collective-permute-start(f32[4,25,8,128]{3,2,1,0:T(8,128)S(1)} %get-tuple-element.326), channel_id=1, source_target_pairs={{0,8},{1,9},{2,10},{3,11},{4,12},{5,13},{6,14},{7,15},{8,16},{9,17... | collective-permute-start | bytes 1228808 | tf_op jit(solution)/shard_map/ppermute | solution.py:682
  26.1 2.7 %collective-permute-start.20 = (f32[8,8,8,128]{3,2,1,0:T(8,128)S(1)}, f32[8,8,8,128]{3,2,1,0:T(8,128)S(1)}, u32[]{:S(2)}, u32[]{:S(2)}) collective-permute-start(f32[8,8,8,128]{3,2,1,0:T(8,128)S(1)} %slice.712), channel_id=1, source_target_pairs={{0,64},{64,0},{128,192},{192,128},{1,65},{65,1},{129,193},{193,129... | collective-permute-start | bytes 786440 | tf_op jit(solution)/shard_map/ppermute | solution.py:685
  28.8 1.2 %collective-permute-done.20.other = f32[8,8,8,128]{3,2,1,0:T(8,128)S(1)} collective-permute-done((f32[8,8,8,128]{3,2,1,0:T(8,128)S(1)}, f32[8,8,8,128]{3,2,1,0:T(8,128)S(1)}, u32[]{:S(2)}, u32[]{:S(2)}) %collective-permute-start.20) | collective-permute-done | bytes 262176 | tf_op jit(solution)/shard_map/ppermute | solution.py:685
  30.0 1.9 %inner.1 = (f32[8,2,16,4,8,128]{5,4,3,2,1,0:T(8,128)S(1)}, f32[2,16,4,8,128]{4,3,2,1,0:T(8,128)S(1)}, f32[128,8,128]{2,1,0:T(8,128)S(1)}) custom-call(f32[8,25,8,128]{3,2,1,0:T(8,128)S(1)} %all_to_all.15.block, f32[8,8,8,128]{3,2,1,0:T(8,128)S(1)} %collective-permute-done.20.other), custom_call_target="tpu_custom_call" | custom-call | flops 100000000 | bytes 1048576 | tf_op jit(solution)/shard_map/inner/pallas_call | solution.py:686
  31.9 0.6 collective-permute-done.18.low
  32.6 0.0 copy-start
  32.6 3.3 %collective-permute-start.21 = (f32[8,8,8,128]{3,2,1,0:T(8,128)S(1)}, f32[8,8,8,128]{3,2,1,0:T(8,128)S(1)}, u32[]{:S(2)}, u32[]{:S(2)}) collective-permute-start(f32[8,8,8,128]{3,2,1,0:T(8,128)S(1)} %pad_maximum_fusion.18), channel_id=1, source_target_pairs={{0,64},{64,0},{128,192},{192,128},{1,65},{65,1},{129,193},{193,129... | collective-permute-start | bytes 786440 | tf_op jit(solution)/shard_map/ppermute | solution.py:697
  35.9 1.2 %collective-permute-done.21.other = f32[8,8,8,128]{3,2,1,0:T(8,128)S(1)} collective-permute-done((f32[8,8,8,128]{3,2,1,0:T(8,128)S(1)}, f32[8,8,8,128]{3,2,1,0:T(8,128)S(1)}, u32[]{:S(2)}, u32[]{:S(2)}) %collective-permute-start.21) | collective-permute-done | bytes 262176 | tf_op jit(solution)/shard_map/ppermute | solution.py:697
  37.1 5.2 %outer.1 = (f32[9,2,32,4,8,128]{5,4,3,2,1,0:T(8,128)S(1)}, f32[1,128]{1,0:T(1,128)S(1)}, f32[2,8,128]{2,1,0:T(8,128)S(1)}) custom-call(f32[8,25,8,128]{3,2,1,0:T(8,128)S(1)} %all_to_all.15.block, f32[4,25,8,128]{3,2,1,0:T(8,128)S(1)} %collective-permute-done.18.low, f32[4,25,8,128]{3,2,1,0:T(8,128)S(1)} %collective-permute-done.19.high, ...), custom_call_target="tpu_custom_call" | custom-call | flops 200000000 | bytes 1048576 | tf_op jit(solution)/shard_map/outer/pallas_call | solution.py:699
  42.3 16.3 %all_to_all.16.grams = f32[8,1,128]{2,1,0:T(1,128)S(1)} all-to-all(f32[8,1,128]{2,1,0:T(1,128)S(1)} %broadcast_in_dim.18), channel_id=1, replica_groups={{0,8,16,24,32,40,48,56},{1,9,17,25,33,41,49,57},{2,10,18,26,34,42,50,58..., dimensions={0} | all-to-all | bytes 8192 | tf_op jit(solution)/shard_map/all_to_all | solution.py:708
  58.6 2.0 %combine.1 = f32[8,33,8,128]{3,2,1,0:T(8,128)S(1)} custom-call(f32[8,1,128]{2,1,0:T(1,128)S(1)} %all_to_all.16.grams, f32[304,128]{1,0:T(8,128)S(1)} %copy-done, f32[288,128]{1,0:T(8,128)S(1)} %copy-done.1, f32[9,2,32,4,8,128]{5,4,3,2,1,0:T(8,128)S(1)} %get-tuple-element.100.basis), custom_call_target="tpu_custom_call" | custom-call | bytes 1048576 | tf_op jit(solution)/shard_map/combine/pallas_call | solution.py:713
  60.7 16.8 %all_to_all.17.fields = f32[8,33,8,128]{3,2,1,0:T(8,128)S(1)} all-to-all(f32[8,33,8,128]{3,2,1,0:T(8,128)S(1)} %combine.1), channel_id=1, replica_groups={{0,1,2,3,4,5,6,7},{8,9,10,11,12,13,14,15},{16,17,18,19,20,21,22,23},{24..., dimensions={0} | all-to-all | bytes 2162688 | tf_op jit(solution)/shard_map/all_to_all | solution.py:716
  77.4 0.1 terms.1
  77.5 2.5 %collective-permute-start.22 = (f32[2,5,8,128]{3,2,1,0:T(8,128)S(1)}, f32[2,5,8,128]{3,2,1,0:T(8,128)S(1)}, u32[]{:S(2)}, u32[]{:S(2)}) collective-permute-start(f32[2,5,8,128]{3,2,1,0:T(8,128)S(1)} %get-tuple-element.102), channel_id=1, source_target_pairs={{0,128},{64,192},{128,0},{192,64},{1,129},{65,193},{129,1},{193,65... | collective-permute-start | bytes 122888 | tf_op jit(solution)/shard_map/ppermute | solution.py:727
  80.0 0.8 fields.1
  80.8 1.1 %collective-permute-done.22.across = f32[2,5,8,128]{3,2,1,0:T(8,128)S(1)} collective-permute-done((f32[2,5,8,128]{3,2,1,0:T(8,128)S(1)}, f32[2,5,8,128]{3,2,1,0:T(8,128)S(1)}, u32[]{:S(2)}, u32[]{:S(2)}) %collective-permute-start.22) | collective-permute-done | bytes 40992 | tf_op jit(solution)/shard_map/ppermute | solution.py:727
  81.9 4.0 %collective-permute-start.23 = (f32[5,8,128]{2,1,0:T(8,128)S(1)}, f32[5,8,128]{2,1,0:T(8,128)S(1)}, u32[]{:S(2)}, u32[]{:S(2)}) collective-permute-start(f32[5,8,128]{2,1,0:T(8,128)S(1)} %bitcast_add_fusion), channel_id=1, source_target_pairs={{0,64},{64,0},{128,192},{192,128},{1,65},{65,1},{129,193},{193,129... | collective-permute-start | bytes 61448 | tf_op jit(solution)/shard_map/ppermute | solution.py:729
  85.9 0.8 collective-permute-done.23.beside
  86.8 0.7 density.1
  87.5 0.9 while.13
  (12 shorter events, 0.1 us)
Async XLA Ops:
  20.6 11.3 %collective-permute-start.19 = (f32[4,25,8,128]{3,2,1,0:T(8,128)S(1)}, f32[4,25,8,128]{3,2,1,0:T(8,128)S(1)}, u32[]{:S(2)}, u32[]{:S(2)}) collective-permute-start(f32[4,25,8,128]{3,2,1,0:T(8,128)S(1)} %get-tuple-element.325), channel_id=1, source_target_pairs={{8,0},{9,1},{10,2},{11,3},{12,4},{13,5},{14,6},{15,7},{16,8},{17,9... | collective-permute-start | bytes 1228808 | tf_op jit(solution)/shard_map/ppermute | solution.py:683
  21.9 10.6 %collective-permute-start.18 = (f32[4,25,8,128]{3,2,1,0:T(8,128)S(1)}, f32[4,25,8,128]{3,2,1,0:T(8,128)S(1)}, u32[]{:S(2)}, u32[]{:S(2)}) collective-permute-start(f32[4,25,8,128]{3,2,1,0:T(8,128)S(1)} %get-tuple-element.326), channel_id=1, source_target_pairs={{0,8},{1,9},{2,10},{3,11},{4,12},{5,13},{6,14},{7,15},{8,16},{9,17... | collective-permute-start | bytes 1228808 | tf_op jit(solution)/shard_map/ppermute | solution.py:682
  26.1 3.8 %collective-permute-start.20 = (f32[8,8,8,128]{3,2,1,0:T(8,128)S(1)}, f32[8,8,8,128]{3,2,1,0:T(8,128)S(1)}, u32[]{:S(2)}, u32[]{:S(2)}) collective-permute-start(f32[8,8,8,128]{3,2,1,0:T(8,128)S(1)} %slice.712), channel_id=1, source_target_pairs={{0,64},{64,0},{128,192},{192,128},{1,65},{65,1},{129,193},{193,129... | collective-permute-start | bytes 786440 | tf_op jit(solution)/shard_map/ppermute | solution.py:685
  32.6 26.0 %copy-start = (f32[304,128]{1,0:T(8,128)S(1)}, f32[304,128]{1,0:T(8,128)}, u32[]{:S(2)}) copy-start(f32[304,128]{1,0:T(8,128)} %constant.57.clone.pick) | copy-start | bytes 466948
  32.6 26.0 %copy-start.1 = (f32[288,128]{1,0:T(8,128)S(1)}, f32[288,128]{1,0:T(8,128)}, u32[]{:S(2)}) copy-start(f32[288,128]{1,0:T(8,128)} %constant.58.clone.nudge) | copy-start | bytes 442372
  32.6 4.5 %collective-permute-start.21 = (f32[8,8,8,128]{3,2,1,0:T(8,128)S(1)}, f32[8,8,8,128]{3,2,1,0:T(8,128)S(1)}, u32[]{:S(2)}, u32[]{:S(2)}) collective-permute-start(f32[8,8,8,128]{3,2,1,0:T(8,128)S(1)} %pad_maximum_fusion.18), channel_id=1, source_target_pairs={{0,64},{64,0},{128,192},{192,128},{1,65},{65,1},{129,193},{193,129... | collective-permute-start | bytes 786440 | tf_op jit(solution)/shard_map/ppermute | solution.py:697
  60.6 26.8 %copy-start.20 = (f32[2,32,128]{2,1,0:T(8,128)S(1)}, f32[2,32,128]{2,1,0:T(8,128)}, u32[]{:S(2)}) copy-start(f32[2,32,128]{2,1,0:T(8,128)} %refs_2_.1) | copy-start | bytes 98308
  77.5 4.4 %collective-permute-start.22 = (f32[2,5,8,128]{3,2,1,0:T(8,128)S(1)}, f32[2,5,8,128]{3,2,1,0:T(8,128)S(1)}, u32[]{:S(2)}, u32[]{:S(2)}) collective-permute-start(f32[2,5,8,128]{3,2,1,0:T(8,128)S(1)} %get-tuple-element.102), channel_id=1, source_target_pairs={{0,128},{64,192},{128,0},{192,64},{1,129},{65,193},{129,1},{193,65... | collective-permute-start | bytes 122888 | tf_op jit(solution)/shard_map/ppermute | solution.py:727
  81.9 4.8 %collective-permute-start.23 = (f32[5,8,128]{2,1,0:T(8,128)S(1)}, f32[5,8,128]{2,1,0:T(8,128)S(1)}, u32[]{:S(2)}, u32[]{:S(2)}) collective-permute-start(f32[5,8,128]{2,1,0:T(8,128)S(1)} %bitcast_add_fusion), channel_id=1, source_target_pairs={{0,64},{64,0},{128,192},{192,128},{1,65},{65,1},{129,193},{193,129... | collective-permute-start | bytes 61448 | tf_op jit(solution)/shard_map/ppermute | solution.py:729

commit v10 on v9

--- a/solution.py
+++ b/solution.py
@@ -275,6 +275,7 @@
 VMEM = pl.BlockSpec(memory_space=pltpu.VMEM)
 SMEM = pl.BlockSpec(memory_space=pltpu.SMEM)
 HBM = pl.BlockSpec(memory_space=pltpu.HBM)
+PAIRS = 88
 LIMIT = 24 * 1024 * 1024
 
 
@@ -519,7 +520,9 @@
         )
     for columns, ranges in OUTER_PASSES:
         gram_pass(basis, acc, columns, ranges, CORE)
-    by_pair = jnp.sum(acc[...], axis=1)
+    by_pair = jnp.concatenate(
+        [jnp.sum(acc[...], axis=1), jnp.zeros((128 - PAIRS, 128), jnp.float32)], axis=0
+    )
     ones = jnp.ones((8, 128), jnp.float32)
     gram[...] = exact_dot(ones, by_pair, ((1,), (1,)))[0:1]
 
@@ -569,7 +572,7 @@
     for plane in range(2):
         solve_plane(CORE - 1 + plane, ((0, plane),))
         solve_plane(CORE + OWN - 1 + plane, ((SYSTEMS - 1, 2 + plane),))
-    lax.fori_loop(1, SYSTEMS, middle, 0, unroll=SYSTEMS - 1)
+    lax.fori_loop(1, SYSTEMS, middle, 0)
 
 
 def fields_kernel(fields, forward, adjoint):
@@ -685,7 +688,7 @@
     other = lax.ppermute(block[:, 16:ROWS_AT], "group", swap)
     inner = call(
         inner_kernel,
-        (f32(SYSTEMS, 2, OWN, TILES, 8, 128), f32(2, OWN, TILES, 8, 128), f32(128, 8, 128)),
+        (f32(SYSTEMS, 2, OWN, TILES, 8, 128), f32(2, OWN, TILES, 8, 128), f32(PAIRS, 8, 128)),
         [VMEM, VMEM],
         (VMEM,) * 3,
         (),
@@ -701,7 +704,7 @@
         (f32(BASIS, 2, WINDOW, *plane), f32(1, 128), f32(2, 8, 128)),
         [VMEM] * 7,
         (VMEM, VMEM, VMEM),
-        [pltpu.VMEM((2, WINDOW) + plane, jnp.float32), pltpu.VMEM((128, 8, 128), jnp.float32)],
+        [pltpu.VMEM((2, WINDOW) + plane, jnp.float32), pltpu.VMEM((PAIRS, 8, 128), jnp.float32)],
         "outer",
         2 * 10**8,
     )(block, low, high, ends, *inner)

time: 88.9 us -> 88.4 us (level)
  no operation moved by 1% of the time
where the time goes in v10:
time: 88.4 us; the launch traced here: 88 us
  blocking collectives  51.1 us (58%)
  starting transfers between devices  18 us (20%)
  Pallas kernels  11.5 us (13%)
  waiting for transfers between devices  4.86 us (5%)
  between operations  1.58 us (2%)
    all_to_all x1, blocking collectives, on_device(): lax.all_to_all(packed, 'zslab', 0, 0, axis_index_groups=planes_of, tiled=...  18 us
    all_to_all x1, blocking collectives, on_device(): lax.all_to_all(solved, 'zslab', 0, 0, axis_index_groups=planes_of, tiled=...  16.8 us
    all_to_all x1, blocking collectives, on_device(): lax.all_to_all(jnp.broadcast_to(gram[None], (SYSTEMS, 1, 128)), 'zslab',...  16.3 us
    pallas_call x1, Pallas kernels, on_device(): call(outer_kernel, (f32(BASIS, 2, WINDOW, *plane), f32(1, 128), f32(2, 8,...  5.14 us
    ppermute x1, starting transfers between devices, on_device(): low = lax.ppermute(block[SYSTEMS // 2:], 'zslab', up)  4.2 us
    ppermute x1, starting transfers between devices, on_device(): beside = lax.ppermute(beside + across[1], 'group', swap)  3.99 us
    ppermute x1, starting transfers between devices, on_device(): ends = lax.ppermute(ends, 'group', swap)  3.33 us
    ppermute x1, starting transfers between devices, on_device(): other = lax.ppermute(block[:, 16:ROWS_AT], 'group', swap)  2.68 us
  transfers between devices with their start and end apart: 6, of which 5 were waited for; matrix products, arithmetic and copies ran while one was open for 0% of the time, Pallas kernels for 3%

profile of v10, /device:TPU:1, one launch (start us, length us, event | category | flops | bytes accessed | tf_op | source)
XLA Modules:
  0.0 88.0 jit_solution(13391347899567890400)
XLA Ops:
  1.3 1.2 %pack.1 = (f32[8,25,8,128]{3,2,1,0:T(8,128)S(1)}, f32[3,8,128]{2,1,0:T(8,128)S(1)}) custom-call(s32[4]{0:T(128)} %refs_0_.1, s32[1]{0:T(128)S(6)} %copy.32.refs_1_, f32[2,32,128]{2,1,0:T(8,128)} %refs_2_.1, f32[2,32,128]{2,1,0:T(8,128)} %refs_3_.1, f32[2,32,128]{2,1,0:T(8,128)} %refs_4_.1, f32[6,2,2,32,128]{4,3,2,1,0:T(8,128)} %refs_5_.1, ...), custom_call_target="tpu_custom_call" | custom-call | bytes 1048576 | tf_op jit(solution)/shard_map/pack/pallas_call | solution.py:668
  2.5 18.0 %all_to_all.15.block = f32[8,25,8,128]{3,2,1,0:T(8,128)S(1)} all-to-all(f32[8,25,8,128]{3,2,1,0:T(8,128)S(1)} %get-tuple-element.90), channel_id=1, replica_groups={{0,1,2,3,4,5,6,7},{8,9,10,11,12,13,14,15},{16,17,18,19,20,21,22,23},{24..., dimensions={0} | all-to-all | bytes 1638400 | tf_op jit(solution)/shard_map/all_to_all | solution.py:681
  20.5 0.1 fusion.55
  20.6 1.3 %collective-permute-start.19 = (f32[4,25,8,128]{3,2,1,0:T(8,128)S(1)}, f32[4,25,8,128]{3,2,1,0:T(8,128)S(1)}, u32[]{:S(2)}, u32[]{:S(2)}) collective-permute-start(f32[4,25,8,128]{3,2,1,0:T(8,128)S(1)} %get-tuple-element.325), channel_id=1, source_target_pairs={{8,0},{9,1},{10,2},{11,3},{12,4},{13,5},{14,6},{15,7},{16,8},{17,9... | collective-permute-start | bytes 1228808 | tf_op jit(solution)/shard_map/ppermute | solution.py:686
  21.9 4.2 %collective-permute-start.18 = (f32[4,25,8,128]{3,2,1,0:T(8,128)S(1)}, f32[4,25,8,128]{3,2,1,0:T(8,128)S(1)}, u32[]{:S(2)}, u32[]{:S(2)}) collective-permute-start(f32[4,25,8,128]{3,2,1,0:T(8,128)S(1)} %get-tuple-element.326), channel_id=1, source_target_pairs={{0,8},{1,9},{2,10},{3,11},{4,12},{5,13},{6,14},{7,15},{8,16},{9,17... | collective-permute-start | bytes 1228808 | tf_op jit(solution)/shard_map/ppermute | solution.py:685
  26.1 2.7 %collective-permute-start.20 = (f32[8,8,8,128]{3,2,1,0:T(8,128)S(1)}, f32[8,8,8,128]{3,2,1,0:T(8,128)S(1)}, u32[]{:S(2)}, u32[]{:S(2)}) collective-permute-start(f32[8,8,8,128]{3,2,1,0:T(8,128)S(1)} %slice.712), channel_id=1, source_target_pairs={{0,64},{64,0},{128,192},{192,128},{1,65},{65,1},{129,193},{193,129... | collective-permute-start | bytes 786440 | tf_op jit(solution)/shard_map/ppermute | solution.py:688
  28.8 1.2 %collective-permute-done.20.other = f32[8,8,8,128]{3,2,1,0:T(8,128)S(1)} collective-permute-done((f32[8,8,8,128]{3,2,1,0:T(8,128)S(1)}, f32[8,8,8,128]{3,2,1,0:T(8,128)S(1)}, u32[]{:S(2)}, u32[]{:S(2)}) %collective-permute-start.20) | collective-permute-done | bytes 262176 | tf_op jit(solution)/shard_map/ppermute | solution.py:688
  30.0 1.9 %inner.1 = (f32[8,2,16,4,8,128]{5,4,3,2,1,0:T(8,128)S(1)}, f32[2,16,4,8,128]{4,3,2,1,0:T(8,128)S(1)}, f32[88,8,128]{2,1,0:T(8,128)S(1)}) custom-call(f32[8,25,8,128]{3,2,1,0:T(8,128)S(1)} %all_to_all.15.block, f32[8,8,8,128]{3,2,1,0:T(8,128)S(1)} %collective-permute-done.20.other), custom_call_target="tpu_custom_call" | custom-call | flops 100000000 | bytes 1048576 | tf_op jit(solution)/shard_map/inner/pallas_call | solution.py:689
  31.9 0.6 collective-permute-done.18.low
  32.6 0.0 copy-start
  32.6 3.3 %collective-permute-start.21 = (f32[8,8,8,128]{3,2,1,0:T(8,128)S(1)}, f32[8,8,8,128]{3,2,1,0:T(8,128)S(1)}, u32[]{:S(2)}, u32[]{:S(2)}) collective-permute-start(f32[8,8,8,128]{3,2,1,0:T(8,128)S(1)} %pad_maximum_fusion.18), channel_id=1, source_target_pairs={{0,64},{64,0},{128,192},{192,128},{1,65},{65,1},{129,193},{193,129... | collective-permute-start | bytes 786440 | tf_op jit(solution)/shard_map/ppermute | solution.py:700
  35.9 1.2 %collective-permute-done.21.other = f32[8,8,8,128]{3,2,1,0:T(8,128)S(1)} collective-permute-done((f32[8,8,8,128]{3,2,1,0:T(8,128)S(1)}, f32[8,8,8,128]{3,2,1,0:T(8,128)S(1)}, u32[]{:S(2)}, u32[]{:S(2)}) %collective-permute-start.21) | collective-permute-done | bytes 262176 | tf_op jit(solution)/shard_map/ppermute | solution.py:700
  37.1 5.1 %outer.1 = (f32[9,2,32,4,8,128]{5,4,3,2,1,0:T(8,128)S(1)}, f32[1,128]{1,0:T(1,128)S(1)}, f32[2,8,128]{2,1,0:T(8,128)S(1)}) custom-call(f32[8,25,8,128]{3,2,1,0:T(8,128)S(1)} %all_to_all.15.block, f32[4,25,8,128]{3,2,1,0:T(8,128)S(1)} %collective-permute-done.18.low, f32[4,25,8,128]{3,2,1,0:T(8,128)S(1)} %collective-permute-done.19.high, ...), custom_call_target="tpu_custom_call" | custom-call | flops 200000000 | bytes 1048576 | tf_op jit(solution)/shard_map/outer/pallas_call | solution.py:702
  42.2 16.3 %all_to_all.16.grams = f32[8,1,128]{2,1,0:T(1,128)S(1)} all-to-all(f32[8,1,128]{2,1,0:T(1,128)S(1)} %broadcast_in_dim.18), channel_id=1, replica_groups={{0,8,16,24,32,40,48,56},{1,9,17,25,33,41,49,57},{2,10,18,26,34,42,50,58..., dimensions={0} | all-to-all | bytes 8192 | tf_op jit(solution)/shard_map/all_to_all | solution.py:711
  58.5 1.6 %combine.1 = f32[8,33,8,128]{3,2,1,0:T(8,128)S(1)} custom-call(f32[8,1,128]{2,1,0:T(1,128)S(1)} %all_to_all.16.grams, f32[304,128]{1,0:T(8,128)S(1)} %copy-done, f32[288,128]{1,0:T(8,128)S(1)} %copy-done.1, f32[9,2,32,4,8,128]{5,4,3,2,1,0:T(8,128)S(1)} %get-tuple-element.100.basis), custom_call_target="tpu_custom_call" | custom-call | bytes 1048576 | tf_op jit(solution)/shard_map/combine/pallas_call | solution.py:716
  60.2 16.8 %all_to_all.17.fields = f32[8,33,8,128]{3,2,1,0:T(8,128)S(1)} all-to-all(f32[8,33,8,128]{3,2,1,0:T(8,128)S(1)} %combine.1), channel_id=1, replica_groups={{0,1,2,3,4,5,6,7},{8,9,10,11,12,13,14,15},{16,17,18,19,20,21,22,23},{24..., dimensions={0} | all-to-all | bytes 2162688 | tf_op jit(solution)/shard_map/all_to_all | solution.py:719
  76.9 0.1 terms.1
  77.0 2.5 %collective-permute-start.22 = (f32[2,5,8,128]{3,2,1,0:T(8,128)S(1)}, f32[2,5,8,128]{3,2,1,0:T(8,128)S(1)}, u32[]{:S(2)}, u32[]{:S(2)}) collective-permute-start(f32[2,5,8,128]{3,2,1,0:T(8,128)S(1)} %get-tuple-element.102), channel_id=1, source_target_pairs={{0,128},{64,192},{128,0},{192,64},{1,129},{65,193},{129,1},{193,65... | collective-permute-start | bytes 122888 | tf_op jit(solution)/shard_map/ppermute | solution.py:730
  79.5 0.8 fields.1
  80.3 1.1 %collective-permute-done.22.across = f32[2,5,8,128]{3,2,1,0:T(8,128)S(1)} collective-permute-done((f32[2,5,8,128]{3,2,1,0:T(8,128)S(1)}, f32[2,5,8,128]{3,2,1,0:T(8,128)S(1)}, u32[]{:S(2)}, u32[]{:S(2)}) %collective-permute-start.22) | collective-permute-done | bytes 40992 | tf_op jit(solution)/shard_map/ppermute | solution.py:730
  81.4 4.0 %collective-permute-start.23 = (f32[5,8,128]{2,1,0:T(8,128)S(1)}, f32[5,8,128]{2,1,0:T(8,128)S(1)}, u32[]{:S(2)}, u32[]{:S(2)}) collective-permute-start(f32[5,8,128]{2,1,0:T(8,128)S(1)} %bitcast_add_fusion), channel_id=1, source_target_pairs={{0,64},{64,0},{128,192},{192,128},{1,65},{65,1},{129,193},{193,129... | collective-permute-start | bytes 61448 | tf_op jit(solution)/shard_map/ppermute | solution.py:732
  85.4 0.8 collective-permute-done.23.beside
  86.3 0.7 density.1
  87.0 0.9 while.13
  (12 shorter events, 0.1 us)
Async XLA Ops:
  20.6 11.3 %collective-permute-start.19 = (f32[4,25,8,128]{3,2,1,0:T(8,128)S(1)}, f32[4,25,8,128]{3,2,1,0:T(8,128)S(1)}, u32[]{:S(2)}, u32[]{:S(2)}) collective-permute-start(f32[4,25,8,128]{3,2,1,0:T(8,128)S(1)} %get-tuple-element.325), channel_id=1, source_target_pairs={{8,0},{9,1},{10,2},{11,3},{12,4},{13,5},{14,6},{15,7},{16,8},{17,9... | collective-permute-start | bytes 1228808 | tf_op jit(solution)/shard_map/ppermute | solution.py:686
  21.9 10.6 %collective-permute-start.18 = (f32[4,25,8,128]{3,2,1,0:T(8,128)S(1)}, f32[4,25,8,128]{3,2,1,0:T(8,128)S(1)}, u32[]{:S(2)}, u32[]{:S(2)}) collective-permute-start(f32[4,25,8,128]{3,2,1,0:T(8,128)S(1)} %get-tuple-element.326), channel_id=1, source_target_pairs={{0,8},{1,9},{2,10},{3,11},{4,12},{5,13},{6,14},{7,15},{8,16},{9,17... | collective-permute-start | bytes 1228808 | tf_op jit(solution)/shard_map/ppermute | solution.py:685
  26.1 3.8 %collective-permute-start.20 = (f32[8,8,8,128]{3,2,1,0:T(8,128)S(1)}, f32[8,8,8,128]{3,2,1,0:T(8,128)S(1)}, u32[]{:S(2)}, u32[]{:S(2)}) collective-permute-start(f32[8,8,8,128]{3,2,1,0:T(8,128)S(1)} %slice.712), channel_id=1, source_target_pairs={{0,64},{64,0},{128,192},{192,128},{1,65},{65,1},{129,193},{193,129... | collective-permute-start | bytes 786440 | tf_op jit(solution)/shard_map/ppermute | solution.py:688
  32.6 26.0 %copy-start = (f32[304,128]{1,0:T(8,128)S(1)}, f32[304,128]{1,0:T(8,128)}, u32[]{:S(2)}) copy-start(f32[304,128]{1,0:T(8,128)} %constant.57.clone.pick) | copy-start | bytes 466948
  32.6 26.0 %copy-start.1 = (f32[288,128]{1,0:T(8,128)S(1)}, f32[288,128]{1,0:T(8,128)}, u32[]{:S(2)}) copy-start(f32[288,128]{1,0:T(8,128)} %constant.58.clone.nudge) | copy-start | bytes 442372
  32.6 4.5 %collective-permute-start.21 = (f32[8,8,8,128]{3,2,1,0:T(8,128)S(1)}, f32[8,8,8,128]{3,2,1,0:T(8,128)S(1)}, u32[]{:S(2)}, u32[]{:S(2)}) collective-permute-start(f32[8,8,8,128]{3,2,1,0:T(8,128)S(1)} %pad_maximum_fusion.18), channel_id=1, source_target_pairs={{0,64},{64,0},{128,192},{192,128},{1,65},{65,1},{129,193},{193,129... | collective-permute-start | bytes 786440 | tf_op jit(solution)/shard_map/ppermute | solution.py:700
  60.1 26.8 %copy-start.20 = (f32[2,32,128]{2,1,0:T(8,128)S(1)}, f32[2,32,128]{2,1,0:T(8,128)}, u32[]{:S(2)}) copy-start(f32[2,32,128]{2,1,0:T(8,128)} %refs_2_.1) | copy-start | bytes 98308
  77.0 4.4 %collective-permute-start.22 = (f32[2,5,8,128]{3,2,1,0:T(8,128)S(1)}, f32[2,5,8,128]{3,2,1,0:T(8,128)S(1)}, u32[]{:S(2)}, u32[]{:S(2)}) collective-permute-start(f32[2,5,8,128]{3,2,1,0:T(8,128)S(1)} %get-tuple-element.102), channel_id=1, source_target_pairs={{0,128},{64,192},{128,0},{192,64},{1,129},{65,193},{129,1},{193,65... | collective-permute-start | bytes 122888 | tf_op jit(solution)/shard_map/ppermute | solution.py:730
  81.4 4.8 %collective-permute-start.23 = (f32[5,8,128]{2,1,0:T(8,128)S(1)}, f32[5,8,128]{2,1,0:T(8,128)S(1)}, u32[]{:S(2)}, u32[]{:S(2)}) collective-permute-start(f32[5,8,128]{2,1,0:T(8,128)S(1)} %bitcast_add_fusion), channel_id=1, source_target_pairs={{0,64},{64,0},{128,192},{192,128},{1,65},{65,1},{129,193},{193,129... | collective-permute-start | bytes 61448 | tf_op jit(solution)/shard_map/ppermute | solution.py:732

commit v11 on v10

--- a/solution.py
+++ b/solution.py
@@ -460,8 +460,43 @@
 )
 
 
+UPPER = 14
+UPPER_PLANES = WINDOW - UPPER
+
+
+def upper_kernel(high, other, inner, inner_diag, basis, diag):
+    place = slab_and_group()
+    core = place[1] % 2
+    for chunk in range(SYSTEMS // 2):
+        for plane in range(2):
+            window = CORE + OWN - UPPER + 2 * chunk + plane
+            for tile in range(TILES):
+                spot = plane * TILES + tile
+                basis[0, 0, window, tile] = high[chunk, spot]
+                basis[0, 1, window, tile] = high[chunk, 8 + spot]
+                diag[core, window, tile] = high[chunk, 16 + spot]
+                diag[1 - core, window, tile] = other[chunk, spot]
+    for at in range(OWN - SYSTEMS, OWN):
+        for part in range(2):
+            for tile in range(TILES):
+                diag[part, CORE + at - UPPER, tile] = inner_diag[part, at, tile]
+    for level in range(SYSTEMS):
+        for at in range(OWN - level - 2, OWN - level):
+            for part in range(2):
+                for tile in range(TILES):
+                    basis[level, part, CORE + at - UPPER, tile] = inner[level, part, at, tile]
+    third_high = jnp.where(place[0] < SYSTEMS * (SYSTEMS - 1), THIRD, 0.0)
+    stencil = Stencil()
+    for level in range(BASIS - 1):
+        upper = WINDOW - 1 - level - UPPER
+        stencil.run(
+            basis, diag, level, upper - CORE, upper,
+            lambda at: third_high if at >= CORE + OWN - UPPER else THIRD,
+        )
+
+
 def outer_kernel(
-    block, low, high, other, inner, inner_diag, inner_acc, basis, gram, dens, diag, acc
+    block, low, high, other, above, inner, inner_diag, inner_acc, basis, gram, dens, diag, acc
 ):
     place = slab_and_group()
     core = place[1] % 2
@@ -483,7 +518,11 @@
         lax.fori_loop(0, SYSTEMS // 2, one, 0, unroll=SYSTEMS // 2)
 
     load(low, 0, 0)
-    load(high, SYSTEMS // 2, CORE + OWN)
+    for level in range(BASIS):
+        for window in range(CORE + OWN - level, CORE + OWN + (level < BASIS - 1)):
+            for part in range(2):
+                for tile in range(TILES):
+                    basis[level, part, window, tile] = above[level, part, window - UPPER, tile]
     for level in range(SYSTEMS):
 
         def keep(at, _, level=level):
@@ -506,17 +545,12 @@
     )
 
     third_low = jnp.where(place[0] >= SYSTEMS, THIRD, 0.0)
-    third_high = jnp.where(place[0] < SYSTEMS * (SYSTEMS - 1), THIRD, 0.0)
     stencil = Stencil()
     for level in range(BASIS - 1):
-        lower, upper = level + 1, WINDOW - 1 - level
+        lower = level + 1
         stencil.run(
             basis, diag, level, lower, lower + CORE,
             lambda at: third_low if at < CORE else THIRD,
-        )
-        stencil.run(
-            basis, diag, level, upper - CORE, upper,
-            lambda at: third_high if at >= CORE + OWN else THIRD,
         )
     for columns, ranges in OUTER_PASSES:
         gram_pass(basis, acc, columns, ranges, CORE)
@@ -695,19 +729,29 @@
         "inner",
         10**8,
     )(block, other)
-    low, high, inner = lax.optimization_barrier((low, high, inner))
-    ends = jnp.concatenate([low[:, 16:ROWS_AT], high[:, 16:ROWS_AT]], axis=0)
-    ends = lax.ppermute(ends, "group", swap)
+    high, inner = lax.optimization_barrier((high, inner))
+    ends = lax.ppermute(high[:, 16:ROWS_AT], "group", swap)
+    above = call(
+        upper_kernel,
+        f32(BASIS, 2, UPPER_PLANES, TILES, 8, 128),
+        [VMEM] * 4,
+        VMEM,
+        [pltpu.VMEM((2, UPPER_PLANES, TILES, 8, 128), jnp.float32)],
+        "upper",
+        10**8,
+    )(high, ends, inner[0], inner[1])
+    low, above = lax.optimization_barrier((low, above))
+    ends = lax.ppermute(low[:, 16:ROWS_AT], "group", swap)
     plane = (TILES, 8, 128)
     basis, gram, dens = call(
         outer_kernel,
         (f32(BASIS, 2, WINDOW, *plane), f32(1, 128), f32(2, 8, 128)),
-        [VMEM] * 7,
+        [VMEM] * 8,
         (VMEM, VMEM, VMEM),
         [pltpu.VMEM((2, WINDOW) + plane, jnp.float32), pltpu.VMEM((PAIRS, 8, 128), jnp.float32)],
         "outer",
         2 * 10**8,
-    )(block, low, high, ends, *inner)
+    )(block, low, high, ends, above, *inner)
     grams = lax.all_to_all(
         jnp.broadcast_to(gram[None], (SYSTEMS, 1, 128)), "zslab", 0, 0,
         axis_index_groups=columns, tiled=True,

time: 88.4 us -> 89.4 us (1.011)
    pallas_call x0 -> x1, Pallas kernels: none -> 1.23 us  [on_device(): call(upper_kernel, f32(BASIS, 2, UPPER_PLANES, TILES, 8, 128), [VMEM] * 4...]
    ppermute x1, waiting for transfers between devices: 1.16 us -> 0.01 us  [on_device(): other = lax.ppermute(block[:, 16:ROWS_AT], 'group', swap)]
    ppermute x1, waiting for transfers between devices: 0.01 us -> 1.15 us  [on_device(): high = lax.ppermute(block[:SYSTEMS // 2], 'zslab', down)]
    pallas_call x1, Pallas kernels: 5.14 us -> 4.07 us  [on_device(): call(outer_kernel, (f32(BASIS, 2, WINDOW, *plane), f32(1, 128), f32(2, 8,...]
    ppermute x1 -> x2, waiting for transfers between devices: 1.16 us -> 1.97 us  [the longest x1 0.99 us: on_device(): ends = lax.ppermute(high[:, 16:ROWS_AT], 'group', swap)]
    ppermute x1 -> x2, starting transfers between devices: 3.33 us -> 3.94 us  [the longest x1 3.05 us: on_device(): ends = lax.ppermute(high[:, 16:ROWS_AT], 'group', swap)]
  transfers between devices with their start and end apart: 6 -> 7, of which waited for: 5 -> 6; matrix products, arithmetic and copies ran while one was open for 0% -> 0% of each run, Pallas kernels for 3% -> 4%
where the time goes in v11:
time: 89.4 us; the launch traced here: 89.1 us
  blocking collectives  51.1 us (57%)
  starting transfers between devices  18.3 us (20%)
  Pallas kernels  11.6 us (13%)
  waiting for transfers between devices  5.52 us (6%)
  between operations  1.57 us (2%)
    all_to_all x1, blocking collectives, on_device(): lax.all_to_all(packed, 'zslab', 0, 0, axis_index_groups=planes_of, tiled=...  18 us
    all_to_all x1, blocking collectives, on_device(): lax.all_to_all(solved, 'zslab', 0, 0, axis_index_groups=planes_of, tiled=...  16.8 us
    all_to_all x1, blocking collectives, on_device(): lax.all_to_all(jnp.broadcast_to(gram[None], (SYSTEMS, 1, 128)), 'zslab',...  16.3 us
    ppermute x1, starting transfers between devices, on_device(): low = lax.ppermute(block[SYSTEMS // 2:], 'zslab', up)  4.28 us
    pallas_call x1, Pallas kernels, on_device(): call(outer_kernel, (f32(BASIS, 2, WINDOW, *plane), f32(1, 128), f32(2, 8,...  4.07 us
    ppermute x1, starting transfers between devices, on_device(): beside = lax.ppermute(beside + across[1], 'group', swap)  3.95 us
    ppermute x1, starting transfers between devices, on_device(): ends = lax.ppermute(high[:, 16:ROWS_AT], 'group', swap)  3.05 us
    ppermute x1, starting transfers between devices, on_device(): across = lax.ppermute(across, 'group', [(i, i ^ 2) for i in range(4)])  2.54 us
  transfers between devices with their start and end apart: 7, of which 6 were waited for; matrix products, arithmetic and copies ran while one was open for 0% of the time, Pallas kernels for 4%

profile of v11, /device:TPU:1, one launch (start us, length us, event | category | flops | bytes accessed | tf_op | source)
XLA Modules:
  0.0 89.1 jit_solution(415443266361092339)
XLA Ops:
  1.3 1.2 %pack.1 = (f32[8,25,8,128]{3,2,1,0:T(8,128)S(1)}, f32[3,8,128]{2,1,0:T(8,128)S(1)}) custom-call(s32[4]{0:T(128)} %refs_0_.1, s32[1]{0:T(128)S(6)} %copy.32.refs_1_, f32[2,32,128]{2,1,0:T(8,128)} %refs_2_.1, f32[2,32,128]{2,1,0:T(8,128)} %refs_3_.1, f32[2,32,128]{2,1,0:T(8,128)} %refs_4_.1, f32[6,2,2,32,128]{4,3,2,1,0:T(8,128)} %refs_5_.1, ...), custom_call_target="tpu_custom_call" | custom-call | bytes 1048576 | tf_op jit(solution)/shard_map/pack/pallas_call | solution.py:702
  2.5 18.0 %all_to_all.15.block = f32[8,25,8,128]{3,2,1,0:T(8,128)S(1)} all-to-all(f32[8,25,8,128]{3,2,1,0:T(8,128)S(1)} %get-tuple-element.91), channel_id=1, replica_groups={{0,1,2,3,4,5,6,7},{8,9,10,11,12,13,14,15},{16,17,18,19,20,21,22,23},{24..., dimensions={0} | all-to-all | bytes 1638400 | tf_op jit(solution)/shard_map/all_to_all | solution.py:715
  20.6 1.3 %collective-permute-start.19 = (f32[4,25,8,128]{3,2,1,0:T(8,128)S(1)}, f32[4,25,8,128]{3,2,1,0:T(8,128)S(1)}, u32[]{:S(2)}, u32[]{:S(2)}) collective-permute-start(f32[4,25,8,128]{3,2,1,0:T(8,128)S(1)} %get-tuple-element.327), channel_id=1, source_target_pairs={{8,0},{9,1},{10,2},{11,3},{12,4},{13,5},{14,6},{15,7},{16,8},{17,9... | collective-permute-start | bytes 1228808 | tf_op jit(solution)/shard_map/ppermute | solution.py:720
  21.9 2.3 %collective-permute-start.20 = (f32[8,8,8,128]{3,2,1,0:T(8,128)S(1)}, f32[8,8,8,128]{3,2,1,0:T(8,128)S(1)}, u32[]{:S(2)}, u32[]{:S(2)}) collective-permute-start(f32[8,8,8,128]{3,2,1,0:T(8,128)S(1)} %slice.712), channel_id=1, source_target_pairs={{0,64},{64,0},{128,192},{192,128},{1,65},{65,1},{129,193},{193,129... | collective-permute-start | bytes 786440 | tf_op jit(solution)/shard_map/ppermute | solution.py:722
  24.2 4.3 %collective-permute-start.18 = (f32[4,25,8,128]{3,2,1,0:T(8,128)S(1)}, f32[4,25,8,128]{3,2,1,0:T(8,128)S(1)}, u32[]{:S(2)}, u32[]{:S(2)}) collective-permute-start(f32[4,25,8,128]{3,2,1,0:T(8,128)S(1)} %get-tuple-element.328), channel_id=1, source_target_pairs={{0,8},{1,9},{2,10},{3,11},{4,12},{5,13},{6,14},{7,15},{8,16},{9,17... | collective-permute-start | bytes 1228808 | tf_op jit(solution)/shard_map/ppermute | solution.py:719
  28.5 1.9 %inner.1 = (f32[8,2,16,4,8,128]{5,4,3,2,1,0:T(8,128)S(1)}, f32[2,16,4,8,128]{4,3,2,1,0:T(8,128)S(1)}, f32[88,8,128]{2,1,0:T(8,128)S(1)}) custom-call(f32[8,25,8,128]{3,2,1,0:T(8,128)S(1)} %all_to_all.15.block, f32[8,8,8,128]{3,2,1,0:T(8,128)S(1)} %collective-permute-done.20.other), custom_call_target="tpu_custom_call" | custom-call | flops 100000000 | bytes 1048576 | tf_op jit(solution)/shard_map/inner/pallas_call | solution.py:723
  30.4 1.1 %collective-permute-done.19.high = f32[4,25,8,128]{3,2,1,0:T(8,128)S(1)} collective-permute-done((f32[4,25,8,128]{3,2,1,0:T(8,128)S(1)}, f32[4,25,8,128]{3,2,1,0:T(8,128)S(1)}, u32[]{:S(2)}, u32[]{:S(2)}) %collective-permute-start.19) | collective-permute-done | bytes 409632 | tf_op jit(solution)/shard_map/ppermute | solution.py:720
  31.6 3.0 %collective-permute-start.21 = (f32[4,8,8,128]{3,2,1,0:T(8,128)S(1)}, f32[4,8,8,128]{3,2,1,0:T(8,128)S(1)}, u32[]{:S(2)}, u32[]{:S(2)}) collective-permute-start(f32[4,8,8,128]{3,2,1,0:T(8,128)S(1)} %slice.295), channel_id=1, source_target_pairs={{0,64},{64,0},{128,192},{192,128},{1,65},{65,1},{129,193},{193,129... | collective-permute-start | bytes 393224 | tf_op jit(solution)/shard_map/ppermute | solution.py:733
  34.7 1.0 %collective-permute-done.21.other = f32[4,8,8,128]{3,2,1,0:T(8,128)S(1)} collective-permute-done((f32[4,8,8,128]{3,2,1,0:T(8,128)S(1)}, f32[4,8,8,128]{3,2,1,0:T(8,128)S(1)}, u32[]{:S(2)}, u32[]{:S(2)}) %collective-permute-start.21) | collective-permute-done | bytes 131104 | tf_op jit(solution)/shard_map/ppermute | solution.py:733
  35.6 1.2 %upper.1.above = f32[9,2,18,4,8,128]{5,4,3,2,1,0:T(8,128)S(1)} custom-call(f32[4,25,8,128]{3,2,1,0:T(8,128)S(1)} %collective-permute-done.19.high, f32[4,8,8,128]{3,2,1,0:T(8,128)S(1)} %collective-permute-done.21.other, f32[8,2,16,4,8,128]{5,4,3,2,1,0:T(8,128)S(1)} %get-tuple-element.96.inner, f32[2,16,4,8,128]{4,3,2,1,0:T(8,128)S(1)} %get-tuple-element.97.inner_diag), custom_call_target="tpu_custom_call" | custom-call | flops 100000000 | bytes 1048576 | tf_op jit(solution)/shard_map/upper/pallas_call | solution.py:734
  36.9 0.5 collective-permute-done.18.low
  37.4 0.9 %collective-permute-start.22 = (f32[4,8,8,128]{3,2,1,0:T(8,128)S(1)}, f32[4,8,8,128]{3,2,1,0:T(8,128)S(1)}, u32[]{:S(2)}, u32[]{:S(2)}) collective-permute-start(f32[4,8,8,128]{3,2,1,0:T(8,128)S(1)} %slice.296), channel_id=1, source_target_pairs={{0,64},{64,0},{128,192},{192,128},{1,65},{65,1},{129,193},{193,129... | collective-permute-start | bytes 393224 | tf_op jit(solution)/shard_map/ppermute | solution.py:744
  38.3 1.0 %collective-permute-done.22.other = f32[4,8,8,128]{3,2,1,0:T(8,128)S(1)} collective-permute-done((f32[4,8,8,128]{3,2,1,0:T(8,128)S(1)}, f32[4,8,8,128]{3,2,1,0:T(8,128)S(1)}, u32[]{:S(2)}, u32[]{:S(2)}) %collective-permute-start.22) | collective-permute-done | bytes 131104 | tf_op jit(solution)/shard_map/ppermute | solution.py:744
  39.3 4.1 %outer.1 = (f32[9,2,32,4,8,128]{5,4,3,2,1,0:T(8,128)S(1)}, f32[1,128]{1,0:T(1,128)S(1)}, f32[2,8,128]{2,1,0:T(8,128)S(1)}) custom-call(f32[8,25,8,128]{3,2,1,0:T(8,128)S(1)} %all_to_all.15.block, f32[4,25,8,128]{3,2,1,0:T(8,128)S(1)} %collective-permute-done.18.low, f32[4,25,8,128]{3,2,1,0:T(8,128)S(1)} %collective-permute-done.19.high, ...), custom_call_target="tpu_custom_call" | custom-call | flops 200000000 | bytes 1048576 | tf_op jit(solution)/shard_map/outer/pallas_call | solution.py:746
  43.3 16.3 %all_to_all.16.grams = f32[8,1,128]{2,1,0:T(1,128)S(1)} all-to-all(f32[8,1,128]{2,1,0:T(1,128)S(1)} %broadcast_in_dim.18), channel_id=1, replica_groups={{0,8,16,24,32,40,48,56},{1,9,17,25,33,41,49,57},{2,10,18,26,34,42,50,58..., dimensions={0} | all-to-all | bytes 8192 | tf_op jit(solution)/shard_map/all_to_all | solution.py:755
  59.7 1.6 %combine.1 = f32[8,33,8,128]{3,2,1,0:T(8,128)S(1)} custom-call(f32[8,1,128]{2,1,0:T(1,128)S(1)} %all_to_all.16.grams, f32[304,128]{1,0:T(8,128)S(1)} %copy-done, f32[288,128]{1,0:T(8,128)S(1)} %copy-done.1, f32[9,2,32,4,8,128]{5,4,3,2,1,0:T(8,128)S(1)} %get-tuple-element.102.basis), custom_call_target="tpu_custom_call" | custom-call | bytes 1048576 | tf_op jit(solution)/shard_map/combine/pallas_call | solution.py:760
  61.3 16.8 %all_to_all.17.fields = f32[8,33,8,128]{3,2,1,0:T(8,128)S(1)} all-to-all(f32[8,33,8,128]{3,2,1,0:T(8,128)S(1)} %combine.1), channel_id=1, replica_groups={{0,1,2,3,4,5,6,7},{8,9,10,11,12,13,14,15},{16,17,18,19,20,21,22,23},{24..., dimensions={0} | all-to-all | bytes 2162688 | tf_op jit(solution)/shard_map/all_to_all | solution.py:763
  78.1 2.5 %collective-permute-start.23 = (f32[2,5,8,128]{3,2,1,0:T(8,128)S(1)}, f32[2,5,8,128]{3,2,1,0:T(8,128)S(1)}, u32[]{:S(2)}, u32[]{:S(2)}) collective-permute-start(f32[2,5,8,128]{3,2,1,0:T(8,128)S(1)} %get-tuple-element.104), channel_id=1, source_target_pairs={{0,128},{64,192},{128,0},{192,64},{1,129},{65,193},{129,1},{193,65... | collective-permute-start | bytes 122888 | tf_op jit(solution)/shard_map/ppermute | solution.py:774
  80.7 0.8 fields.1
  81.5 1.1 %collective-permute-done.23.across = f32[2,5,8,128]{3,2,1,0:T(8,128)S(1)} collective-permute-done((f32[2,5,8,128]{3,2,1,0:T(8,128)S(1)}, f32[2,5,8,128]{3,2,1,0:T(8,128)S(1)}, u32[]{:S(2)}, u32[]{:S(2)}) %collective-permute-start.23) | collective-permute-done | bytes 40992 | tf_op jit(solution)/shard_map/ppermute | solution.py:774
  82.6 4.0 %collective-permute-start.24 = (f32[5,8,128]{2,1,0:T(8,128)S(1)}, f32[5,8,128]{2,1,0:T(8,128)S(1)}, u32[]{:S(2)}, u32[]{:S(2)}) collective-permute-start(f32[5,8,128]{2,1,0:T(8,128)S(1)} %bitcast_add_fusion), channel_id=1, source_target_pairs={{0,64},{64,0},{128,192},{192,128},{1,65},{65,1},{129,193},{193,129... | collective-permute-start | bytes 61448 | tf_op jit(solution)/shard_map/ppermute | solution.py:776
  86.5 0.8 collective-permute-done.24.beside
  87.4 0.7 density.1
  88.1 0.8 while.13
  (14 shorter events, 0.2 us)
Async XLA Ops:
  20.6 11.0 %collective-permute-start.19 = (f32[4,25,8,128]{3,2,1,0:T(8,128)S(1)}, f32[4,25,8,128]{3,2,1,0:T(8,128)S(1)}, u32[]{:S(2)}, u32[]{:S(2)}) collective-permute-start(f32[4,25,8,128]{3,2,1,0:T(8,128)S(1)} %get-tuple-element.327), channel_id=1, source_target_pairs={{8,0},{9,1},{10,2},{11,3},{12,4},{13,5},{14,6},{15,7},{16,8},{17,9... | collective-permute-start | bytes 1228808 | tf_op jit(solution)/shard_map/ppermute | solution.py:720
  21.9 6.6 %collective-permute-start.20 = (f32[8,8,8,128]{3,2,1,0:T(8,128)S(1)}, f32[8,8,8,128]{3,2,1,0:T(8,128)S(1)}, u32[]{:S(2)}, u32[]{:S(2)}) collective-permute-start(f32[8,8,8,128]{3,2,1,0:T(8,128)S(1)} %slice.712), channel_id=1, source_target_pairs={{0,64},{64,0},{128,192},{192,128},{1,65},{65,1},{129,193},{193,129... | collective-permute-start | bytes 786440 | tf_op jit(solution)/shard_map/ppermute | solution.py:722
  24.2 13.1 %collective-permute-start.18 = (f32[4,25,8,128]{3,2,1,0:T(8,128)S(1)}, f32[4,25,8,128]{3,2,1,0:T(8,128)S(1)}, u32[]{:S(2)}, u32[]{:S(2)}) collective-permute-start(f32[4,25,8,128]{3,2,1,0:T(8,128)S(1)} %get-tuple-element.328), channel_id=1, source_target_pairs={{0,8},{1,9},{2,10},{3,11},{4,12},{5,13},{6,14},{7,15},{8,16},{9,17... | collective-permute-start | bytes 1228808 | tf_op jit(solution)/shard_map/ppermute | solution.py:719
  31.6 4.0 %collective-permute-start.21 = (f32[4,8,8,128]{3,2,1,0:T(8,128)S(1)}, f32[4,8,8,128]{3,2,1,0:T(8,128)S(1)}, u32[]{:S(2)}, u32[]{:S(2)}) collective-permute-start(f32[4,8,8,128]{3,2,1,0:T(8,128)S(1)} %slice.295), channel_id=1, source_target_pairs={{0,64},{64,0},{128,192},{192,128},{1,65},{65,1},{129,193},{193,129... | collective-permute-start | bytes 393224 | tf_op jit(solution)/shard_map/ppermute | solution.py:733
  37.4 22.3 %copy-start = (f32[304,128]{1,0:T(8,128)S(1)}, f32[304,128]{1,0:T(8,128)}, u32[]{:S(2)}) copy-start(f32[304,128]{1,0:T(8,128)} %constant.57.clone.pick) | copy-start | bytes 466948
  37.4 22.3 %copy-start.1 = (f32[288,128]{1,0:T(8,128)S(1)}, f32[288,128]{1,0:T(8,128)}, u32[]{:S(2)}) copy-start(f32[288,128]{1,0:T(8,128)} %constant.58.clone.nudge) | copy-start | bytes 442372
  37.4 1.9 %collective-permute-start.22 = (f32[4,8,8,128]{3,2,1,0:T(8,128)S(1)}, f32[4,8,8,128]{3,2,1,0:T(8,128)S(1)}, u32[]{:S(2)}, u32[]{:S(2)}) collective-permute-start(f32[4,8,8,128]{3,2,1,0:T(8,128)S(1)} %slice.296), channel_id=1, source_target_pairs={{0,64},{64,0},{128,192},{192,128},{1,65},{65,1},{129,193},{193,129... | collective-permute-start | bytes 393224 | tf_op jit(solution)/shard_map/ppermute | solution.py:744
  61.3 26.8 %copy-start.22 = (f32[2,32,128]{2,1,0:T(8,128)S(1)}, f32[2,32,128]{2,1,0:T(8,128)}, u32[]{:S(2)}) copy-start(f32[2,32,128]{2,1,0:T(8,128)} %refs_2_.1) | copy-start | bytes 98308
  78.1 4.4 %collective-permute-start.23 = (f32[2,5,8,128]{3,2,1,0:T(8,128)S(1)}, f32[2,5,8,128]{3,2,1,0:T(8,128)S(1)}, u32[]{:S(2)}, u32[]{:S(2)}) collective-permute-start(f32[2,5,8,128]{3,2,1,0:T(8,128)S(1)} %get-tuple-element.104), channel_id=1, source_target_pairs={{0,128},{64,192},{128,0},{192,64},{1,129},{65,193},{129,1},{193,65... | collective-permute-start | bytes 122888 | tf_op jit(solution)/shard_map/ppermute | solution.py:774
  82.6 4.8 %collective-permute-start.24 = (f32[5,8,128]{2,1,0:T(8,128)S(1)}, f32[5,8,128]{2,1,0:T(8,128)S(1)}, u32[]{:S(2)}, u32[]{:S(2)}) collective-permute-start(f32[5,8,128]{2,1,0:T(8,128)S(1)} %bitcast_add_fusion), channel_id=1, source_target_pairs={{0,64},{64,0},{128,192},{192,128},{1,65},{65,1},{129,193},{193,129... | collective-permute-start | bytes 61448 | tf_op jit(solution)/shard_map/ppermute | solution.py:776

commit v12 on v10

--- a/solution.py
+++ b/solution.py
@@ -415,7 +415,7 @@
     for first, last in ranges:
         sums = lax.fori_loop(
             0, (last - first) * TILES, functools.partial(position, first=first), sums,
-            unroll=8,
+            unroll=8 if (last - first) % 2 == 0 else 4,
         )
     for at, value in zip(places, sums):
         acc[at] = value
@@ -450,12 +450,13 @@
     ((0, 1, 2, 3, 4), ((4, 12),)),
     ((0, 1, 2), ((2, 4), (12, 14))),
     ((5, 6), ((6, 10),)),
+    ((7,), ((7, 9),)),
 )
 OUTER_PASSES = (
     ((0, 1, 2, 3, 4), ((0, 2), (14, 16))),
     ((3, 4), ((2, 4), (12, 14))),
     ((5, 6), ((0, 6), (10, 16))),
-    ((7,), ((0, 16),)),
+    ((7,), ((0, 6), (6, 7), (9, 10), (10, 16))),
     ((8,), ((0, 16),)),
 )
 

time: 88.4 us -> 88.3 us (level)
  no operation moved by 1% of the time
where the time goes in v12:
time: 88.3 us; the launch traced here: 87.9 us
  blocking collectives  51.1 us (58%)
  starting transfers between devices  18 us (20%)
  Pallas kernels  11.4 us (13%)
  waiting for transfers between devices  4.8 us (5%)
  between operations  1.58 us (2%)
    all_to_all x1, blocking collectives, on_device(): lax.all_to_all(packed, 'zslab', 0, 0, axis_index_groups=planes_of, tiled=...  18 us
    all_to_all x1, blocking collectives, on_device(): lax.all_to_all(solved, 'zslab', 0, 0, axis_index_groups=planes_of, tiled=...  16.8 us
    all_to_all x1, blocking collectives, on_device(): lax.all_to_all(jnp.broadcast_to(gram[None], (SYSTEMS, 1, 128)), 'zslab',...  16.3 us
    pallas_call x1, Pallas kernels, on_device(): call(outer_kernel, (f32(BASIS, 2, WINDOW, *plane), f32(1, 128), f32(2, 8,...  5.05 us
    ppermute x1, starting transfers between devices, on_device(): low = lax.ppermute(block[SYSTEMS // 2:], 'zslab', up)  4.2 us
    ppermute x1, starting transfers between devices, on_device(): beside = lax.ppermute(beside + across[1], 'group', swap)  3.99 us
    ppermute x1, starting transfers between devices, on_device(): ends = lax.ppermute(ends, 'group', swap)  3.33 us
    ppermute x1, starting transfers between devices, on_device(): other = lax.ppermute(block[:, 16:ROWS_AT], 'group', swap)  2.68 us
  transfers between devices with their start and end apart: 6, of which 5 were waited for; matrix products, arithmetic and copies ran while one was open for 0% of the time, Pallas kernels for 3%

profile of v12, /device:TPU:1, one launch (start us, length us, event | category | flops | bytes accessed | tf_op | source)
XLA Modules:
  0.0 87.9 jit_solution(13284718779411762588)
XLA Ops:
  1.3 1.2 %pack.1 = (f32[8,25,8,128]{3,2,1,0:T(8,128)S(1)}, f32[3,8,128]{2,1,0:T(8,128)S(1)}) custom-call(s32[4]{0:T(128)} %refs_0_.1, s32[1]{0:T(128)S(6)} %copy.32.refs_1_, f32[2,32,128]{2,1,0:T(8,128)} %refs_2_.1, f32[2,32,128]{2,1,0:T(8,128)} %refs_3_.1, f32[2,32,128]{2,1,0:T(8,128)} %refs_4_.1, f32[6,2,2,32,128]{4,3,2,1,0:T(8,128)} %refs_5_.1, ...), custom_call_target="tpu_custom_call" | custom-call | bytes 1048576 | tf_op jit(solution)/shard_map/pack/pallas_call | solution.py:669
  2.5 18.0 %all_to_all.15.block = f32[8,25,8,128]{3,2,1,0:T(8,128)S(1)} all-to-all(f32[8,25,8,128]{3,2,1,0:T(8,128)S(1)} %get-tuple-element.90), channel_id=1, replica_groups={{0,1,2,3,4,5,6,7},{8,9,10,11,12,13,14,15},{16,17,18,19,20,21,22,23},{24..., dimensions={0} | all-to-all | bytes 1638400 | tf_op jit(solution)/shard_map/all_to_all | solution.py:682
  20.5 0.1 fusion.55
  20.6 1.3 %collective-permute-start.19 = (f32[4,25,8,128]{3,2,1,0:T(8,128)S(1)}, f32[4,25,8,128]{3,2,1,0:T(8,128)S(1)}, u32[]{:S(2)}, u32[]{:S(2)}) collective-permute-start(f32[4,25,8,128]{3,2,1,0:T(8,128)S(1)} %get-tuple-element.325), channel_id=1, source_target_pairs={{8,0},{9,1},{10,2},{11,3},{12,4},{13,5},{14,6},{15,7},{16,8},{17,9... | collective-permute-start | bytes 1228808 | tf_op jit(solution)/shard_map/ppermute | solution.py:687
  21.9 4.2 %collective-permute-start.18 = (f32[4,25,8,128]{3,2,1,0:T(8,128)S(1)}, f32[4,25,8,128]{3,2,1,0:T(8,128)S(1)}, u32[]{:S(2)}, u32[]{:S(2)}) collective-permute-start(f32[4,25,8,128]{3,2,1,0:T(8,128)S(1)} %get-tuple-element.326), channel_id=1, source_target_pairs={{0,8},{1,9},{2,10},{3,11},{4,12},{5,13},{6,14},{7,15},{8,16},{9,17... | collective-permute-start | bytes 1228808 | tf_op jit(solution)/shard_map/ppermute | solution.py:686
  26.1 2.7 %collective-permute-start.20 = (f32[8,8,8,128]{3,2,1,0:T(8,128)S(1)}, f32[8,8,8,128]{3,2,1,0:T(8,128)S(1)}, u32[]{:S(2)}, u32[]{:S(2)}) collective-permute-start(f32[8,8,8,128]{3,2,1,0:T(8,128)S(1)} %slice.712), channel_id=1, source_target_pairs={{0,64},{64,0},{128,192},{192,128},{1,65},{65,1},{129,193},{193,129... | collective-permute-start | bytes 786440 | tf_op jit(solution)/shard_map/ppermute | solution.py:689
  28.8 1.2 %collective-permute-done.20.other = f32[8,8,8,128]{3,2,1,0:T(8,128)S(1)} collective-permute-done((f32[8,8,8,128]{3,2,1,0:T(8,128)S(1)}, f32[8,8,8,128]{3,2,1,0:T(8,128)S(1)}, u32[]{:S(2)}, u32[]{:S(2)}) %collective-permute-start.20) | collective-permute-done | bytes 262176 | tf_op jit(solution)/shard_map/ppermute | solution.py:689
  30.0 2.0 %inner.1 = (f32[8,2,16,4,8,128]{5,4,3,2,1,0:T(8,128)S(1)}, f32[2,16,4,8,128]{4,3,2,1,0:T(8,128)S(1)}, f32[88,8,128]{2,1,0:T(8,128)S(1)}) custom-call(f32[8,25,8,128]{3,2,1,0:T(8,128)S(1)} %all_to_all.15.block, f32[8,8,8,128]{3,2,1,0:T(8,128)S(1)} %collective-permute-done.20.other), custom_call_target="tpu_custom_call" | custom-call | flops 100000000 | bytes 1048576 | tf_op jit(solution)/shard_map/inner/pallas_call | solution.py:690
  31.9 0.5 collective-permute-done.18.low
  32.6 0.0 copy-start
  32.6 3.3 %collective-permute-start.21 = (f32[8,8,8,128]{3,2,1,0:T(8,128)S(1)}, f32[8,8,8,128]{3,2,1,0:T(8,128)S(1)}, u32[]{:S(2)}, u32[]{:S(2)}) collective-permute-start(f32[8,8,8,128]{3,2,1,0:T(8,128)S(1)} %pad_maximum_fusion.18), channel_id=1, source_target_pairs={{0,64},{64,0},{128,192},{192,128},{1,65},{65,1},{129,193},{193,129... | collective-permute-start | bytes 786440 | tf_op jit(solution)/shard_map/ppermute | solution.py:701
  35.9 1.2 %collective-permute-done.21.other = f32[8,8,8,128]{3,2,1,0:T(8,128)S(1)} collective-permute-done((f32[8,8,8,128]{3,2,1,0:T(8,128)S(1)}, f32[8,8,8,128]{3,2,1,0:T(8,128)S(1)}, u32[]{:S(2)}, u32[]{:S(2)}) %collective-permute-start.21) | collective-permute-done | bytes 262176 | tf_op jit(solution)/shard_map/ppermute | solution.py:701
  37.1 5.1 %outer.1 = (f32[9,2,32,4,8,128]{5,4,3,2,1,0:T(8,128)S(1)}, f32[1,128]{1,0:T(1,128)S(1)}, f32[2,8,128]{2,1,0:T(8,128)S(1)}) custom-call(f32[8,25,8,128]{3,2,1,0:T(8,128)S(1)} %all_to_all.15.block, f32[4,25,8,128]{3,2,1,0:T(8,128)S(1)} %collective-permute-done.18.low, f32[4,25,8,128]{3,2,1,0:T(8,128)S(1)} %collective-permute-done.19.high, ...), custom_call_target="tpu_custom_call" | custom-call | flops 200000000 | bytes 1048576 | tf_op jit(solution)/shard_map/outer/pallas_call | solution.py:703
  42.1 16.3 %all_to_all.16.grams = f32[8,1,128]{2,1,0:T(1,128)S(1)} all-to-all(f32[8,1,128]{2,1,0:T(1,128)S(1)} %broadcast_in_dim.18), channel_id=1, replica_groups={{0,8,16,24,32,40,48,56},{1,9,17,25,33,41,49,57},{2,10,18,26,34,42,50,58..., dimensions={0} | all-to-all | bytes 8192 | tf_op jit(solution)/shard_map/all_to_all | solution.py:712
  58.4 1.6 %combine.1 = f32[8,33,8,128]{3,2,1,0:T(8,128)S(1)} custom-call(f32[8,1,128]{2,1,0:T(1,128)S(1)} %all_to_all.16.grams, f32[304,128]{1,0:T(8,128)S(1)} %copy-done, f32[288,128]{1,0:T(8,128)S(1)} %copy-done.1, f32[9,2,32,4,8,128]{5,4,3,2,1,0:T(8,128)S(1)} %get-tuple-element.100.basis), custom_call_target="tpu_custom_call" | custom-call | bytes 1048576 | tf_op jit(solution)/shard_map/combine/pallas_call | solution.py:717
  60.1 16.8 %all_to_all.17.fields = f32[8,33,8,128]{3,2,1,0:T(8,128)S(1)} all-to-all(f32[8,33,8,128]{3,2,1,0:T(8,128)S(1)} %combine.1), channel_id=1, replica_groups={{0,1,2,3,4,5,6,7},{8,9,10,11,12,13,14,15},{16,17,18,19,20,21,22,23},{24..., dimensions={0} | all-to-all | bytes 2162688 | tf_op jit(solution)/shard_map/all_to_all | solution.py:720
  76.8 0.1 terms.1
  76.9 2.5 %collective-permute-start.22 = (f32[2,5,8,128]{3,2,1,0:T(8,128)S(1)}, f32[2,5,8,128]{3,2,1,0:T(8,128)S(1)}, u32[]{:S(2)}, u32[]{:S(2)}) collective-permute-start(f32[2,5,8,128]{3,2,1,0:T(8,128)S(1)} %get-tuple-element.102), channel_id=1, source_target_pairs={{0,128},{64,192},{128,0},{192,64},{1,129},{65,193},{129,1},{193,65... | collective-permute-start | bytes 122888 | tf_op jit(solution)/shard_map/ppermute | solution.py:731
  79.4 0.8 fields.1
  80.2 1.1 %collective-permute-done.22.across = f32[2,5,8,128]{3,2,1,0:T(8,128)S(1)} collective-permute-done((f32[2,5,8,128]{3,2,1,0:T(8,128)S(1)}, f32[2,5,8,128]{3,2,1,0:T(8,128)S(1)}, u32[]{:S(2)}, u32[]{:S(2)}) %collective-permute-start.22) | collective-permute-done | bytes 40992 | tf_op jit(solution)/shard_map/ppermute | solution.py:731
  81.3 4.0 %collective-permute-start.23 = (f32[5,8,128]{2,1,0:T(8,128)S(1)}, f32[5,8,128]{2,1,0:T(8,128)S(1)}, u32[]{:S(2)}, u32[]{:S(2)}) collective-permute-start(f32[5,8,128]{2,1,0:T(8,128)S(1)} %bitcast_add_fusion), channel_id=1, source_target_pairs={{0,64},{64,0},{128,192},{192,128},{1,65},{65,1},{129,193},{193,129... | collective-permute-start | bytes 61448 | tf_op jit(solution)/shard_map/ppermute | solution.py:733
  85.3 0.8 collective-permute-done.23.beside
  86.2 0.7 density.1
  86.9 0.9 while.13
  (12 shorter events, 0.1 us)
Async XLA Ops:
  20.6 11.3 %collective-permute-start.19 = (f32[4,25,8,128]{3,2,1,0:T(8,128)S(1)}, f32[4,25,8,128]{3,2,1,0:T(8,128)S(1)}, u32[]{:S(2)}, u32[]{:S(2)}) collective-permute-start(f32[4,25,8,128]{3,2,1,0:T(8,128)S(1)} %get-tuple-element.325), channel_id=1, source_target_pairs={{8,0},{9,1},{10,2},{11,3},{12,4},{13,5},{14,6},{15,7},{16,8},{17,9... | collective-permute-start | bytes 1228808 | tf_op jit(solution)/shard_map/ppermute | solution.py:687
  21.9 10.6 %collective-permute-start.18 = (f32[4,25,8,128]{3,2,1,0:T(8,128)S(1)}, f32[4,25,8,128]{3,2,1,0:T(8,128)S(1)}, u32[]{:S(2)}, u32[]{:S(2)}) collective-permute-start(f32[4,25,8,128]{3,2,1,0:T(8,128)S(1)} %get-tuple-element.326), channel_id=1, source_target_pairs={{0,8},{1,9},{2,10},{3,11},{4,12},{5,13},{6,14},{7,15},{8,16},{9,17... | collective-permute-start | bytes 1228808 | tf_op jit(solution)/shard_map/ppermute | solution.py:686
  26.1 3.8 %collective-permute-start.20 = (f32[8,8,8,128]{3,2,1,0:T(8,128)S(1)}, f32[8,8,8,128]{3,2,1,0:T(8,128)S(1)}, u32[]{:S(2)}, u32[]{:S(2)}) collective-permute-start(f32[8,8,8,128]{3,2,1,0:T(8,128)S(1)} %slice.712), channel_id=1, source_target_pairs={{0,64},{64,0},{128,192},{192,128},{1,65},{65,1},{129,193},{193,129... | collective-permute-start | bytes 786440 | tf_op jit(solution)/shard_map/ppermute | solution.py:689
  32.6 25.9 %copy-start = (f32[304,128]{1,0:T(8,128)S(1)}, f32[304,128]{1,0:T(8,128)}, u32[]{:S(2)}) copy-start(f32[304,128]{1,0:T(8,128)} %constant.57.clone.pick) | copy-start | bytes 466948
  32.6 25.9 %copy-start.1 = (f32[288,128]{1,0:T(8,128)S(1)}, f32[288,128]{1,0:T(8,128)}, u32[]{:S(2)}) copy-start(f32[288,128]{1,0:T(8,128)} %constant.58.clone.nudge) | copy-start | bytes 442372
  32.6 4.5 %collective-permute-start.21 = (f32[8,8,8,128]{3,2,1,0:T(8,128)S(1)}, f32[8,8,8,128]{3,2,1,0:T(8,128)S(1)}, u32[]{:S(2)}, u32[]{:S(2)}) collective-permute-start(f32[8,8,8,128]{3,2,1,0:T(8,128)S(1)} %pad_maximum_fusion.18), channel_id=1, source_target_pairs={{0,64},{64,0},{128,192},{192,128},{1,65},{65,1},{129,193},{193,129... | collective-permute-start | bytes 786440 | tf_op jit(solution)/shard_map/ppermute | solution.py:701
  60.0 26.8 %copy-start.20 = (f32[2,32,128]{2,1,0:T(8,128)S(1)}, f32[2,32,128]{2,1,0:T(8,128)}, u32[]{:S(2)}) copy-start(f32[2,32,128]{2,1,0:T(8,128)} %refs_2_.1) | copy-start | bytes 98308
  76.9 4.4 %collective-permute-start.22 = (f32[2,5,8,128]{3,2,1,0:T(8,128)S(1)}, f32[2,5,8,128]{3,2,1,0:T(8,128)S(1)}, u32[]{:S(2)}, u32[]{:S(2)}) collective-permute-start(f32[2,5,8,128]{3,2,1,0:T(8,128)S(1)} %get-tuple-element.102), channel_id=1, source_target_pairs={{0,128},{64,192},{128,0},{192,64},{1,129},{65,193},{129,1},{193,65... | collective-permute-start | bytes 122888 | tf_op jit(solution)/shard_map/ppermute | solution.py:731
  81.3 4.8 %collective-permute-start.23 = (f32[5,8,128]{2,1,0:T(8,128)S(1)}, f32[5,8,128]{2,1,0:T(8,128)S(1)}, u32[]{:S(2)}, u32[]{:S(2)}) collective-permute-start(f32[5,8,128]{2,1,0:T(8,128)S(1)} %bitcast_add_fusion), channel_id=1, source_target_pairs={{0,64},{64,0},{128,192},{192,128},{1,65},{65,1},{129,193},{193,129... | collective-permute-start | bytes 61448 | tf_op jit(solution)/shard_map/ppermute | solution.py:733
